TPU v7x, 32 devices: a whole 2x2x4 slice. The times are simulated.
32 devices in a mesh: ctx: 16 (over z, y, x), tp: 2 (over core).
Axes of the slice: x: 2, y: 2, z: 4, core: 2. Of those that a mesh axis runs over, the one named last changes fastest.
Arguments:
- tokens: bfloat16 [2048, 4096], P('ctx'), may hold values from -6 to 6
- weights: bfloat16 [2, 2048, 3, 4096], P('tp', 'ctx'), may hold values from -0.09375 to 0.09375
- residues: float32 [2, 2048, 16], P('tp', 'ctx'), may hold values from -1.5 to 1.5
- decay_rates: float32 [2, 2048, 16], P('tp', 'ctx'), may hold values from 0.00024414062 to 0.03
- cotangent: bfloat16 [4096, 2048], P('tp', 'ctx'), may hold values from -6 to 6
Outputs:
- hyena_out: bfloat16 [4096, 2048], P('tp', 'ctx')
- grad_input: bfloat16 [2048, 4096], P('ctx', 'tp')
- grad_residue: float32 [2, 2048, 16], P('tp', 'ctx')
All inputs are finite; a program needn't handle non-finite values.
Results may differ from a plain program's by a relative error of at most 0.018.
Values may be sent and summed in bfloat16 or wider, within the bound.
No kernel may reach another device: no remote copies, remote signals or barrier semaphores. Data moves between devices by JAX's collectives and lax.ppermute only.
A program may use at most 128 MiB of HBM per device.

v0:
```python
import functools
import math

import jax
import jax.numpy as jnp
from jax import lax
from jax.experimental import pallas as pl
from jax.experimental.pallas import tpu as pltpu
from jax.sharding import PartitionSpec as P


def precise(form, left, right):
    return jnp.einsum(
        form, left, right, precision=lax.Precision.HIGHEST, preferred_element_type=jnp.float32
    )


def tripled(form, left, right):
    return jnp.einsum(
        form, left, right, precision=lax.Precision.HIGH, preferred_element_type=jnp.float32
    )


def angle_table(row_count, col_count, period):
    product = (
        jnp.arange(row_count, dtype=jnp.int32)[:, None]
        * jnp.arange(col_count, dtype=jnp.int32)[None, :]
        % period
    )
    angles = product.astype(jnp.float32) * (2.0 * math.pi / period)
    return (jnp.cos(angles), jnp.sin(angles))


def make_tables(length):
    padded = 2 * length
    outer = math.gcd(padded, 1 << (padded.bit_length() - 1) // 2)
    inner = padded // outer
    cos_outer, sin_outer = angle_table(outer, outer, outer)
    cos_inner, sin_inner = angle_table(inner, inner, inner)
    twist_cos, twist_sin = angle_table(outer, inner, padded)
    return (outer, inner, cos_outer, sin_outer, cos_inner, sin_inner, twist_cos, twist_sin)


def spectrum(signal, tables, product):
    outer, inner, cos_outer, sin_outer, cos_inner, sin_inner, twist_cos, twist_sin = tables
    half_rows = outer // 2
    blocks = signal.reshape(signal.shape[0], half_rows, inner)
    first_re = product("kp,bpq->bkq", cos_outer[:, :half_rows], blocks)
    first_im = -product("kp,bpq->bkq", sin_outer[:, :half_rows], blocks)
    turned_re = first_re * twist_cos + first_im * twist_sin
    turned_im = first_im * twist_cos - first_re * twist_sin
    spec_re = product("bkq,qj->bkj", turned_re, cos_inner) + product(
        "bkq,qj->bkj", turned_im, sin_inner
    )
    spec_im = product("bkq,qj->bkj", turned_im, cos_inner) - product(
        "bkq,qj->bkj", turned_re, sin_inner
    )
    return (spec_re, spec_im)


def signal_of(spec_re, spec_im, tables):
    outer, inner, cos_outer, sin_outer, cos_inner, sin_inner, twist_cos, twist_sin = tables
    half_rows = outer // 2
    back_re = tripled("bkj,jq->bkq", spec_re, cos_inner) - tripled(
        "bkj,jq->bkq", spec_im, sin_inner
    )
    back_im = tripled("bkj,jq->bkq", spec_im, cos_inner) + tripled(
        "bkj,jq->bkq", spec_re, sin_inner
    )
    turned_re = back_re * twist_cos - back_im * twist_sin
    turned_im = back_im * twist_cos + back_re * twist_sin
    values = tripled("pk,bkq->bpq", cos_outer[:half_rows, :], turned_re) - tripled(
        "pk,bkq->bpq", sin_outer[:half_rows, :], turned_im
    )
    return values.reshape(values.shape[0], half_rows * inner) * (1.0 / (outer * inner))


def spec_product(left_re, left_im, right_re, right_im):
    return (left_re * right_re - left_im * right_im, left_re * right_im + left_im * right_re)


def conj_product(left_re, left_im, right_re, right_im):
    return (left_re * right_re + left_im * right_im, left_re * right_im - left_im * right_re)


def filter_basis(residue_loc, rate_loc, length):
    position = jnp.arange(length, dtype=jnp.float32)
    basis_all = jnp.sqrt(2.0 * rate_loc)[:, :, None] * jnp.exp(
        -rate_loc[:, :, None] * position[None, None, :]
    )
    return (basis_all, precise("cm,cmt->ct", residue_loc, basis_all))


def forward_cols(gated_cols, taps_re, taps_im, tables):
    gated_re, gated_im = spectrum(gated_cols.astype(jnp.float32), tables, tripled)
    conv_re, conv_im = spec_product(gated_re, gated_im, taps_re, taps_im)
    conv_cols = signal_of(conv_re, conv_im, tables).astype(jnp.bfloat16)
    return (conv_cols, gated_re, gated_im)


def backward_cols(slope_cols, gated_re, gated_im, taps_re, taps_im, basis_all, tables, length):
    slope_re, slope_im = spectrum(slope_cols.astype(jnp.float32), tables, tripled)
    grad_re, grad_im = conj_product(taps_re, taps_im, slope_re, slope_im)
    back_cols = signal_of(grad_re, grad_im, tables).astype(jnp.bfloat16)
    lag_re, lag_im = conj_product(gated_re, gated_im, slope_re, slope_im)
    taps_grad = signal_of(lag_re, lag_im, tables)
    grad_residue = precise("ct,cmt->cm", taps_grad, basis_all) * (1.0 / math.sqrt(length))
    return (back_cols, grad_residue)


def gather_weights(tokens, weights, residues, decay_rates, cotangent):
    gathered = lax.all_gather(weights, "ctx", axis=1, tiled=True)
    projected = jnp.einsum("xcpd,td->xcpt", gathered, tokens, preferred_element_type=jnp.float32)
    features = projected[0].astype(jnp.bfloat16)
    query_f = features[:, 0].astype(jnp.float32)
    key_part = features[:, 1].astype(jnp.float32)
    value_part = features[:, 2].astype(jnp.float32)
    gated_in = (key_part * value_part).astype(jnp.bfloat16)
    slope_in = (cotangent.astype(jnp.float32) * query_f).astype(jnp.bfloat16)
    length = tokens.shape[0] * lax.axis_size("ctx")
    tables = make_tables(length)
    basis_all, taps_full = filter_basis(residues[0], decay_rates[0], length)
    taps_re, taps_im = spectrum(taps_full, tables, precise)
    gated_cols = lax.all_to_all(gated_in, "ctx", split_axis=0, concat_axis=1, tiled=True)
    conv_cols, gated_re, gated_im = forward_cols(gated_cols, taps_re, taps_im, tables)
    conv_rows = lax.all_to_all(conv_cols, "ctx", split_axis=1, concat_axis=0, tiled=True)
    slope_cols = lax.all_to_all(slope_in, "ctx", split_axis=0, concat_axis=1, tiled=True)
    back_cols, grad_residue = backward_cols(
        slope_cols, gated_re, gated_im, taps_re, taps_im, basis_all, tables, length
    )
    back_rows = lax.all_to_all(back_cols, "ctx", split_axis=1, concat_axis=0, tiled=True)
    conv_f = conv_rows.astype(jnp.float32)
    back_f = back_rows.astype(jnp.float32)
    hyena_out = (query_f * conv_f).astype(jnp.bfloat16)
    grad_query = (cotangent.astype(jnp.float32) * conv_f).astype(jnp.bfloat16)
    grad_key = (back_f * value_part).astype(jnp.bfloat16)
    grad_value = (back_f * key_part).astype(jnp.bfloat16)
    grad_proj = jnp.stack([grad_query, grad_key, grad_value], axis=1)
    partial_value = jnp.einsum(
        "cpt,cpd->td", grad_proj, gathered[0], preferred_element_type=jnp.float32
    )
    grad_input = lax.psum_scatter(
        partial_value.astype(jnp.bfloat16), "tp", scatter_dimension=1, tiled=True
    )
    return (hyena_out, grad_input, grad_residue[None])


GROUP = 4
PLANE = 4


def rounded(value):
    return value.astype(jnp.bfloat16).astype(jnp.float32)


def earlier_sum(finals, rate, span, back):
    count = finals.shape[0]
    row = lax.broadcasted_iota(jnp.int32, finals.shape, 0)

    def shifted(value, by):
        if back:
            moved = pltpu.roll(value, count - by, 0)
            return jnp.where(row < count - by, moved, 0.0)
        moved = pltpu.roll(value, by, 0)
        return jnp.where(row >= by, moved, 0.0)

    total = shifted(finals, 1)
    by = 1
    while by < count:
        total = total + jnp.exp(rate * (-1.0 * span * by)) * shifted(total, by)
        by *= 2
    return total


def scan_kernel(
    groups,
    runs,
    order,
    me_ref,
    cot_ref,
    residue_ref,
    rate_ref,
    *refs,
):
    inputs = 1 + max(run[0] for run in runs)
    own, other = refs[:inputs], refs[inputs : 2 * inputs]
    hyena_ref, grad_ref = refs[2 * inputs : 2 * inputs + 2]
    proj_refs = refs[2 * inputs + 2 : 2 * inputs + 2 + len(order)]
    gated_s, slope_s, conv_s, back_s, feats_s = refs[2 * inputs + 2 + len(order) :]
    length, width = cot_ref.shape
    chunks = PLANE * groups
    span = length // chunks
    modes = rate_ref.shape[0]
    me = me_ref[0]

    def place(group, member):
        return lax.rem(me // PLANE + group, groups) * PLANE + (member ^ lax.rem(me, PLANE))

    def aligned(start, size):
        return pl.ds(pl.multiple_of(start, size), size)

    for source, offset, group, base, members, count, first in runs:

        def before(step, _, source=source, offset=offset, group=group, base=base, count=count, first=first):
            member = base + step
            index = place(group, member)
            rows = pl.ds(pl.multiple_of(offset + step * count, 16), count)
            feats = own[source][rows, 3 * width :] + other[source][rows, :].astype(jnp.float32)
            feats = rounded(feats)
            slot = (group * PLANE + member) * span + first
            feats_s[pl.ds(pl.multiple_of(slot, 16), count), :] = feats
            cot = cot_ref[pl.ds(pl.multiple_of(index * span + first, 16), count), :]
            query, key = feats[:, :width], feats[:, width : 2 * width]
            into = pl.ds(first * chunks + index, count, stride=chunks)
            gated_s[into, :] = rounded(key * feats[:, 2 * width :])
            slope_s[into, :] = rounded(cot.astype(jnp.float32) * query)
            return 0

        lax.fori_loop(0, members, before, 0)

    def at(step):
        return aligned(step * chunks, chunks)

    zero = jnp.zeros((chunks, width), jnp.float32)
    scale = 1.0 / math.sqrt(length)
    for first in range(0, modes, GROUP):
        count = min(GROUP, modes - first)
        rates = [
            jnp.broadcast_to(rate_ref[m : m + 1, :], (chunks, width))
            for m in range(first, first + count)
        ]
        decays = [jnp.exp(-rate) for rate in rates]
        norms = [jnp.sqrt(2.0 * rate) for rate in rates]
        gains = [
            residue_ref[first + n : first + n + 1, :] * norms[n] for n in range(count)
        ]

        def sums(step, state):
            ahead, behind = state
            gated = gated_s[at(step), :]
            slope = slope_s[at(span - 1 - step), :]
            return (
                tuple(decays[n] * ahead[n] + gated for n in range(count)),
                tuple(decays[n] * behind[n] + slope for n in range(count)),
            )

        ahead, behind = lax.fori_loop(0, span, sums, ((zero,) * count, (zero,) * count), unroll=4)
        ahead = tuple(earlier_sum(ahead[n], rates[n], span, False) for n in range(count))
        behind = tuple(earlier_sum(behind[n], rates[n], span, True) for n in range(count))

        def outs(step, state):
            ahead, behind, grads = state
            other = span - 1 - step
            gated = gated_s[at(step), :]
            slope = slope_s[at(step), :]
            slope_back = slope_s[at(other), :]
            ahead = tuple(decays[n] * ahead[n] + gated for n in range(count))
            behind = tuple(decays[n] * behind[n] + slope_back for n in range(count))
            grads = tuple(grads[n] + slope * ahead[n] for n in range(count))
            conv = sum(gains[n] * ahead[n] for n in range(count))
            back = sum(gains[n] * behind[n] for n in range(count))
            if first:
                conv = conv + conv_s[at(step), :]
                back = back + back_s[at(other), :]
            conv_s[at(step), :] = conv
            back_s[at(other), :] = back
            return ahead, behind, grads

        _, _, grads = lax.fori_loop(0, span, outs, (ahead, behind, (zero,) * count), unroll=2)
        for n in range(count):
            total = jnp.sum(grads[n] * norms[n], axis=0, keepdims=True) * scale
            grad_ref[first + n : first + n + 1, :] = total

    for proj_ref, pieces in zip(proj_refs, order):
        start = 0
        for group, base, members in pieces:

            def after(step, _, proj_ref=proj_ref, start=start, group=group, base=base):
                member = base + step
                index = place(group, member)
                feats = feats_s[aligned((group * PLANE + member) * span, span), :]
                query, key = feats[:, :width], feats[:, width : 2 * width]
                cot = cot_ref[aligned(index * span, span), :].astype(jnp.float32)
                conv = rounded(conv_s[pl.ds(index, span, stride=chunks), :])
                back = rounded(back_s[pl.ds(index, span, stride=chunks), :])
                hyena_ref[aligned(index * span, span), :] = narrowed(query * conv)
                rows = aligned(start + step * span, span)
                proj_ref[rows, :width] = narrowed(cot * conv)
                proj_ref[rows, width : 2 * width] = narrowed(back * feats[:, 2 * width :])
                proj_ref[rows, 2 * width :] = narrowed(back * key)
                return 0

            lax.fori_loop(0, members, after, 0)
            start += members * span


def scan_all(me, cot_cols, residue_rows, rate_rows, runs, order, own, other):
    length, width = cot_cols.shape
    span = length // (PLANE * PLANE)
    vmem = pl.BlockSpec(memory_space=pltpu.VMEM)
    outs = pl.pallas_call(
        functools.partial(scan_kernel, PLANE, runs, order),
        out_shape=(
            jax.ShapeDtypeStruct((length, width), jnp.bfloat16),
            jax.ShapeDtypeStruct(rate_rows.shape, jnp.float32),
        )
        + tuple(
            jax.ShapeDtypeStruct((span * sum(piece[2] for piece in pieces), 3 * width), jnp.bfloat16)
            for pieces in order
        ),
        in_specs=[pl.BlockSpec(memory_space=pltpu.SMEM)] + [vmem] * (3 + 2 * len(own)),
        out_specs=(vmem,) * (2 + len(order)),
        scratch_shapes=[pltpu.VMEM((length, width), jnp.float32)] * 4
        + [pltpu.VMEM((length, 3 * width), jnp.float32)],
        compiler_params=pltpu.CompilerParams(vmem_limit_bytes=40 * 2**20),
        name="modal_scan",
    )(me, cot_cols, residue_rows, rate_rows, *own, *other)
    return outs[0], outs[1], outs[2:]


def swapped(value):
    return lax.ppermute(value, "tp", [(0, 1), (1, 0)])


def over_x(value):
    return lax.ppermute(value, "ctx", [(i, i ^ 1) for i in range(lax.axis_size("ctx"))])


def over_y(value):
    return lax.ppermute(value, "ctx", [(i, i ^ 2) for i in range(lax.axis_size("ctx"))])


def up(value):
    count = lax.axis_size("ctx")
    return lax.ppermute(value, "ctx", [(i, (i + PLANE) % count) for i in range(count)])


def down(value):
    count = lax.axis_size("ctx")
    return lax.ppermute(value, "ctx", [((i + PLANE) % count, i) for i in range(count)])


def stack(*parts):
    return jnp.concatenate(parts, axis=0)


def beside(*parts):
    return jnp.concatenate(parts, axis=1)


def narrowed(value):
    return value.astype(jnp.bfloat16)


def widened(value):
    return value.astype(jnp.float32)


def over_plane(for_x, for_y):
    return lax.optimization_barrier((over_x(for_x), over_y(for_y)))


def over_depth(for_above, for_below):
    return lax.optimization_barrier((up(for_above), down(for_below)))


def gather_groups(tokens, matrix, others):
    span = tokens.shape[0]
    n, m = span * 3 // 4, span // 4
    nh, mh = n // 2, m // 2
    wide = tokens[:n]
    own_x, own_y = over_plane(tokens, tokens)
    wide_3, wide_1 = over_depth(wide, wide)
    across_x, across_y = over_plane(
        stack(own_y[:nh], own_y[n : n + mh]), stack(own_x[nh:n], own_x[n + mh :])
    )
    wide_2 = stack(*over_depth(wide_3[:nh], wide_1[nh:]))
    near = stack(wide_3, wide_1)
    near, matrix, others = lax.optimization_barrier((near, matrix, others))
    near_x, near_y = over_plane(near, near)
    plane = stack(tokens[n:], own_x[n:], own_y[n:], across_x[nh:], across_y[nh:])
    plane, wide_2 = lax.optimization_barrier((plane, wide_2))
    plane_3, plane_1 = over_depth(plane, plane)
    far_x, far_y = over_plane(
        stack(near_y[:nh], near_y[n : n + nh], wide_2), stack(near_x[nh:n], near_x[n + nh :], wide_2)
    )
    half = plane.shape[0] // 2
    far = over_depth(plane_3[:half], plane_1[half:])
    last_x, last_y = over_plane(far_y[n : n + nh], far_x[n + nh :])
    parts = (
        stack(tokens, own_x, own_y, across_x, across_y),
        stack(near, near_x, near_y),
        stack(plane_1, plane_3),
        stack(wide_2, far_x, far_y),
        stack(last_x, last_y, *far),
    )
    runs = [
        (0, 0, 0, 0, 3, span, 0),
        (2, 0, 1, 0, 4, m, n),
        (2, 4 * m, 3, 0, 4, m, n),
        (3, 0, 2, 0, 1, n, 0),
        (4, 2 * nh, 2, 0, 4, m, n),
    ]
    for side in range(2):
        runs += [
            (0, 3 * span + side * (nh + mh), 0, 3, 1, nh, side * nh),
            (0, 3 * span + side * (nh + mh) + nh, 0, 3, 1, mh, n + side * mh),
            (3, n + side * 2 * n, 3, 3, 1, nh, side * nh),
            (3, n + side * 2 * n + nh, 1, 3, 1, nh, side * nh),
            (3, n + side * 2 * n + n, 2, 1 + side, 1, n, 0),
            (4, side * nh, 2, 3, 1, nh, side * nh),
        ]
    for member in range(3):
        runs += [(1, member * 2 * n, 3, member, 1, n, 0), (1, member * 2 * n + n, 1, member, 1, n, 0)]
    return parts, tuple(runs), matrix, others


ORDER = (((2, 0, 4), (1, 3, 1)), ((1, 0, 3), (3, 0, 4), (0, 0, 4)))


def scatter_sum(early, later, matrix, hyena):
    span = later.shape[0] // 11
    columns = matrix.shape[1]
    wide, narrow = columns * 3 // 8, columns // 8

    def product(part):
        both = beside(part, swapped(part))
        return narrowed(jnp.dot(both, matrix, preferred_element_type=jnp.float32))

    blocks = {}

    def keep(value, pieces):
        start = 0
        for group, base, members in pieces:
            for member in range(base, base + members):
                blocks[group, member] = value[start : start + span]
                start += span

    early = product(early)
    keep(early, ORDER[0])

    def term(group, member, side):
        return blocks[group, member][:, side * wide : (side + 1) * wide]

    def low(group, side):
        first = 2 * wide + side * narrow
        return stack(*[blocks[group, m][:, first : first + narrow] for m in range(PLANE)])

    def total(*parts):
        return sum(widened(part) for part in parts)

    def to_x(group, across):
        return term(group, 1, 0), narrowed(total(term(group, 1, 1), across))

    def to_y(group, across):
        return narrowed(total(term(group, 2, 0), across)), term(group, 2, 1)

    def kept(group, got_x, got_y):
        return [
            total(
                term(group, 0, side),
                got_x[:, side * wide : (side + 1) * wide],
                got_y[:, side * wide : (side + 1) * wide],
            )
            for side in (0, 1)
        ]

    got_x, got_y = over_plane(
        beside(term(2, 3, 0), term(1, 3, 0)), beside(term(2, 3, 1), term(1, 3, 1))
    )
    low_up, low_down = over_depth(low(2, 0), low(2, 1))
    later, early = lax.optimization_barrier((later, early))
    later, hyena, got_x, got_y = lax.optimization_barrier((product(later), hyena, got_x, got_y))
    keep(later, ORDER[1])
    hyena_out = lax.all_to_all(hyena, "ctx", split_axis=0, concat_axis=1, tiled=True).T
    got_x, got_y = over_plane(
        beside(*to_x(2, got_y[:, :wide]), *to_x(1, got_y[:, wide:]), term(3, 3, 0)),
        beside(*to_y(2, got_x[:, :wide]), *to_y(1, got_x[:, wide:]), term(3, 3, 1)),
    )
    low_up, low_down = over_depth(
        beside(narrowed(total(low(1, 0), low_up)), low(1, 1)),
        beside(low(3, 0), narrowed(total(low(3, 1), low_down))),
    )
    sum_2 = kept(2, got_x[:, : 2 * wide], got_y[:, : 2 * wide])
    sum_1 = kept(1, got_x[:, 2 * wide : 4 * wide], got_y[:, 2 * wide : 4 * wide])
    sum_2, low_up, low_down = lax.optimization_barrier((sum_2, low_up, low_down))
    wide_up, wide_down = over_depth(narrowed(sum_2[0]), narrowed(sum_2[1]))
    got_x, got_y = over_plane(
        beside(*to_x(3, got_y[:, 4 * wide :]), term(0, 3, 0)),
        beside(*to_y(3, got_x[:, 4 * wide :]), term(0, 3, 1)),
    )
    got_x, got_y, wide_up, wide_down = lax.optimization_barrier((got_x, got_y, wide_up, wide_down))
    sum_3 = kept(3, got_x[:, : 2 * wide], got_y[:, : 2 * wide])
    wide_up, wide_down = over_depth(
        beside(narrowed(total(sum_1[0], wide_up)), narrowed(sum_1[1])),
        beside(narrowed(sum_3[0]), narrowed(total(sum_3[1], wide_down))),
    )
    low_sum = [
        total(
            low(0, side),
            low_up[:, side * narrow : (side + 1) * narrow],
            low_down[:, side * narrow : (side + 1) * narrow],
        )
        for side in (0, 1)
    ]

    def low_term(member, side):
        return low_sum[side][member * span : (member + 1) * span]

    got_x, got_y = over_plane(
        beside(*to_x(0, got_y[:, 2 * wide :]), narrowed(low_term(3, 0))),
        beside(*to_y(0, got_x[:, 2 * wide :]), narrowed(low_term(3, 1))),
    )
    sum_0 = kept(0, got_x[:, : 2 * wide], got_y[:, : 2 * wide])
    across_y, across_x = got_x[:, 2 * wide :], got_y[:, 2 * wide :]
    low_x, low_y = over_plane(
        beside(narrowed(low_term(1, 0)), narrowed(total(low_term(1, 1), across_x))),
        beside(narrowed(total(low_term(2, 0), across_y)), narrowed(low_term(2, 1))),
    )
    outs = [
        total(
            sum_0[side],
            wide_up[:, side * wide : (side + 1) * wide],
            wide_down[:, side * wide : (side + 1) * wide],
        )
        for side in (0, 1)
    ]
    outs += [
        total(
            low_term(0, side),
            low_x[:, side * narrow : (side + 1) * narrow],
            low_y[:, side * narrow : (side + 1) * narrow],
        )
        for side in (0, 1)
    ]
    return beside(*[narrowed(part) for part in outs]), hyena_out


def gather_tokens(tokens, weights, residues, decay_rates, cotangent):
    core = lax.axis_index("tp")
    me = lax.axis_index("ctx").astype(jnp.int32).reshape(1)
    half = tokens.shape[1] // 2
    channels = weights.shape[1]
    rows = weights[0].swapaxes(0, 1).reshape(3 * channels, 2 * half)
    kept = lax.dynamic_slice_in_dim(rows, core * half, half, 1)
    taken = swapped(lax.dynamic_slice_in_dim(rows, (1 - core) * half, half, 1))
    cot_cols = lax.all_to_all(cotangent.T, "ctx", split_axis=1, concat_axis=0, tiled=True)
    parts, runs, matrix, cot_cols = gather_groups(
        lax.dynamic_slice_in_dim(tokens, core * half, half, 1), stack(taken, kept), cot_cols
    )
    both = [
        jnp.einsum("td,rd->tr", part, matrix, preferred_element_type=jnp.float32) for part in parts
    ]
    other = [swapped(narrowed(part[:, : 3 * channels])) for part in both]
    hyena, grads, (early, later) = scan_all(
        me, cot_cols, residues[0].T, decay_rates[0].T, runs, ORDER, both, other
    )
    grad_input, hyena_out = scatter_sum(early, later, stack(kept, taken), hyena)
    return (hyena_out, grad_input, grads.T[None])


def shards(tokens, weights, residues, decay_rates, cotangent):
    ctx, tp = lax.axis_size("ctx"), lax.axis_size("tp")
    if ctx == 4 * PLANE and tp == 2 and weights.size * tp > 2 * tokens.size:
        return gather_tokens(tokens, weights, residues, decay_rates, cotangent)
    return gather_weights(tokens, weights, residues, decay_rates, cotangent)


def solution(mesh):
    return jax.shard_map(
        shards,
        mesh=mesh,
        in_specs=(
            P("ctx", None),
            P("tp", "ctx", None, None),
            P("tp", "ctx", None),
            P("tp", "ctx", None),
            P("tp", "ctx"),
        ),
        out_specs=(P("tp", "ctx"), P("ctx", "tp"), P("tp", "ctx", None)),
        check_vma=False,
    )
```

profile of v0, /device:TPU:0, one launch (start us, length us, event | category | flops | bytes accessed | tf_op | source)
XLA Modules:
  0.0 264.8 jit_solution(8999921344790767182)
XLA Ops:
  0.6 1.8 constant_dynamic-slice_fusion
  2.4 3.0 %collective-permute-start = (bf16[96,2048]{1,0:T(8,128)(2,1)}, bf16[96,2048]{1,0:T(8,128)(2,1)S(1)}, u32[]{:S(2)}, u32[]{:S(2)}) collective-permute-start(bf16[96,2048]{1,0:T(8,128)(2,1)} %constant_dynamic-slice_fusion), channel_id=1, source_target_pairs={{0,8},{2,10},{4,12},{6,14},{8,16},{10,18},{12,20},{14,22},{16,24},... | collective-permute-start | bytes 1179656 | tf_op jit(solution)/shard_map/ppermute | solution.py:335
  5.4 2.0 collective-permute-start.1
  7.5 2.1 constant_dynamic-update-slice_fusion.4
  9.6 1.7 collective-permute-start.3
  12.8 3.4 %constant_dynamic-slice_fusion.2 = (bf16[384,2048]{1,0:T(8,128)(2,1)}, bf16[384,2048]{1,0:T(8,128)(2,1)S(1)}) fusion(bf16[384,4096]{1,0:T(8,128)(2,1)} %bitcast.35, s32[]{:T(128)S(6)} %select_n.8, s32[]{:T(128)S(6)} %select_n.7), kind=kLoop, calls=%fused_computation.110 | loop fusion | bytes 6291464 | tf_op jit(solution)/shard_map/dynamic_slice | solution.py:546
  17.5 3.6 %all-to-all-start = ((bf16[128,16,128]{2,0,1:T(8,128)(2,1)}), bf16[128,16,128]{2,0,1:T(8,128)(2,1)S(1)}, u32[]{:S(2)}, u32[]{:S(2)}) async-start(bf16[128,16,128]{2,0,1:T(8,128)(2,1)} %copy.8), calls=%async_computation | async-start | bytes 1048576 | tf_op jit(solution)/shard_map/all_to_all | solution.py:547
  22.0 3.5 %collective-permute-done.1 = bf16[96,2048]{1,0:T(8,128)(2,1)} collective-permute-done((bf16[96,2048]{1,0:T(8,128)(2,1)}, bf16[96,2048]{1,0:T(8,128)(2,1)}, u32[]{:S(2)}, u32[]{:S(2)}) %collective-permute-start.1) | collective-permute-done | bytes 393248 | tf_op jit(solution)/shard_map/ppermute | solution.py:340
  27.0 3.4 %collective-permute-start.10 = (bf16[48,2048]{1,0:T(8,128)(2,1)S(1)}, bf16[48,2048]{1,0:T(8,128)(2,1)S(1)}, u32[]{:S(2)}, u32[]{:S(2)}) collective-permute-start(bf16[48,2048]{1,0:T(8,128)(2,1)S(1)} %slice.493), channel_id=1, source_target_pairs={{8,0},{10,2},{12,4},{14,6},{16,8},{18,10},{20,12},{22,14},{24,16},... | collective-permute-start | bytes 589832 | tf_op jit(solution)/shard_map/ppermute | solution.py:340
  32.1 2.5 collective-permute-start.6
  34.6 4.6 %collective-permute-done.9 = bf16[48,2048]{1,0:T(8,128)(2,1)S(1)} collective-permute-done((bf16[48,2048]{1,0:T(8,128)(2,1)S(1)}, bf16[48,2048]{1,0:T(8,128)(2,1)S(1)}, u32[]{:S(2)}, u32[]{:S(2)}) %collective-permute-start.9) | collective-permute-done | bytes 196640 | tf_op jit(solution)/shard_map/ppermute | solution.py:335
  39.2 2.3 collective-permute-done.10
  43.7 4.0 %collective-permute-start.11 = (bf16[128,2048]{1,0:T(8,128)(2,1)S(1)}, bf16[128,2048]{1,0:T(8,128)(2,1)S(1)}, u32[]{:S(2)}, u32[]{:S(2)}) collective-permute-start(bf16[128,2048]{1,0:T(8,128)(2,1)S(1)} %slice_dynamic-update-slice_fusion.8), channel_id=1, source_target_pairs={{0,8},{2,10},{4,12},{6,14},{8,16},{10,18},{12,20},{14,22},{16,24},... | collective-permute-start | bytes 1572872 | tf_op jit(solution)/shard_map/ppermute | solution.py:335
  47.7 2.0 pad_maximum_fusion.6
  51.3 9.1 %collective-permute-done.11 = bf16[128,2048]{1,0:T(8,128)(2,1)S(1)} collective-permute-done((bf16[128,2048]{1,0:T(8,128)(2,1)S(1)}, bf16[128,2048]{1,0:T(8,128)(2,1)S(1)}, u32[]{:S(2)}, u32[]{:S(2)}) %collective-permute-start.11) | collective-permute-done | bytes 524320 | tf_op jit(solution)/shard_map/ppermute | solution.py:335
  60.4 9.6 %collective-permute-done.12 = bf16[128,2048]{1,0:T(8,128)(2,1)S(1)} collective-permute-done((bf16[128,2048]{1,0:T(8,128)(2,1)S(1)}, bf16[128,2048]{1,0:T(8,128)(2,1)S(1)}, u32[]{:S(2)}, u32[]{:S(2)}) %collective-permute-start.12) | collective-permute-done | bytes 524320 | tf_op jit(solution)/shard_map/ppermute | solution.py:340
  70.7 3.9 %collective-permute-start.18 = (bf16[64,2048]{1,0:T(8,128)(2,1)S(1)}, bf16[64,2048]{1,0:T(8,128)(2,1)}, u32[]{:S(2)}, u32[]{:S(2)}) collective-permute-start(bf16[64,2048]{1,0:T(8,128)(2,1)S(1)} %slice.501), channel_id=1, source_target_pairs={{8,0},{10,2},{12,4},{14,6},{16,8},{18,10},{20,12},{22,14},{24,16},... | collective-permute-start | bytes 786440 | tf_op jit(solution)/shard_map/ppermute | solution.py:340
  74.6 3.5 %pad_maximum_fusion = bf16[768,2048]{1,0:T(8,128)(2,1)} fusion(bf16[384,2048]{1,0:T(8,128)(2,1)S(1)} %get-tuple-element.156, bf16[384,2048]{1,0:T(8,128)(2,1)} %collective-permute-done.2), kind=kLoop, calls=%fused_computation.2 | loop fusion | flops 6291456 | bytes 6291456 | tf_op jit(solution)/shard_map/concatenate | solution.py:344
  84.6 4.4 %fusion.57.refs_0_ = f32[512,768]{1,0:T(8,128)S(1)} fusion(bf16[512,2048]{1,0:T(8,128)(2,1)} %constant_dynamic-update-slice_fusion, bf16[768,2048]{1,0:T(8,128)(2,1)} %pad_maximum_fusion), kind=kOutput, calls=%fused_computation.129 | convolution fusion | flops 1610612736 | bytes 6815744 | tf_op jit(solution)/shard_map/td,rd->tr/dot_general | solution.py:552
  89.8 7.0 %collective-permute-done.7 = bf16[192,2048]{1,0:T(8,128)(2,1)S(1)} collective-permute-done((bf16[192,2048]{1,0:T(8,128)(2,1)}, bf16[192,2048]{1,0:T(8,128)(2,1)S(1)}, u32[]{:S(2)}, u32[]{:S(2)}) %collective-permute-start.7) | collective-permute-done | bytes 786464 | tf_op jit(solution)/shard_map/ppermute | solution.py:326
  98.9 1.7 collective-permute-start.14
  103.3 3.2 %fusion.refs_1_ = f32[576,768]{1,0:T(8,128)S(1)} fusion(bf16[768,2048]{1,0:T(8,128)(2,1)S(1)} %copy-done.13, bf16[192,2048]{1,0:T(8,128)(2,1)S(1)} %collective-permute-done.8, bf16[192,2048]{1,0:T(8,128)(2,1)S(1)} %collective-permute-done.7, bf16[192,2048]{1,0:T(8,128)(2,1)} %pad_maximum_fusion.6), kind=kOutput, calls=%fused_computation.4 | convolution fusion | flops 1819017216 | bytes 7274496 | tf_op jit(solution)/shard_map/td,rd->tr/dot_general | solution.py:552
  107.7 7.9 %collective-permute-done.13 = bf16[192,2048]{1,0:T(8,128)(2,1)S(1)} collective-permute-done((bf16[192,2048]{1,0:T(8,128)(2,1)S(1)}, bf16[192,2048]{1,0:T(8,128)(2,1)S(1)}, u32[]{:S(2)}, u32[]{:S(2)}) %collective-permute-start.13) | collective-permute-done | bytes 786464 | tf_op jit(solution)/shard_map/ppermute | solution.py:326
  117.5 1.8 collective-permute-start.16
  119.4 1.7 fusion.9.refs_3_
  123.3 2.1 fusion.22.refs_4_
  126.9 1.7 collective-permute-done.23.refs_9_
  133.3 14.6 %modal_scan.1 = (bf16[2048,128]{1,0:T(8,128)(2,1)}, f32[16,128]{1,0:T(8,128)}, bf16[640,384]{1,0:T(8,128)(2,1)S(1)}, bf16[1408,384]{1,0:T(8,128)(2,1)S(1)}) custom-call(s32[1]{0:T(128)} %bitcast.me_ref, bf16[2048,128]{1,0:T(8,128)(2,1)S(1)} %bitcast.32, f32[16,128]{1,0:T(8,128)S(1)} %bitcast.33, f32[16,128]{1,0:T(8,128)S(1)} %bitcast.34, ...), custom_call_target="tpu_custom_call" | custom-call | tf_op jit(solution)/shard_map/modal_scan/pallas_call | solution.py:301
  148.1 1.7 collective-permute-done.24
  149.8 3.7 %convolution_convert_fusion.1 = bf16[640,2048]{1,0:T(8,128)(2,1)S(1)} fusion(bf16[384,2048]{1,0:T(8,128)(2,1)} %collective-permute-done.2, bf16[384,2048]{1,0:T(8,128)(2,1)S(1)} %copy-done.11, bf16[640,384]{1,0:T(8,128)(2,1)S(1)} %collective-permute-done.24, bf16[640,384]{1,0:T(8,128)(2,1)S(1)} %get-tuple-element.85), kind=kOutput, calls=%fused_computation.1 | convolution fusion | flops 2022834176 | bytes 6750208 | tf_op jit(solution)/shard_map/dot_general | solution.py:428
  154.4 1.8 collective-permute-start.27
  156.5 3.8 %collective-permute-start.33 = (bf16[512,256]{1,0:T(8,128)(2,1)S(1)}, bf16[512,256]{1,0:T(8,128)(2,1)S(1)}, u32[]{:S(2)}, u32[]{:S(2)}) collective-permute-start(bf16[512,256]{1,0:T(8,128)(2,1)S(1)} %get-tuple-element.159), channel_id=1, source_target_pairs={{8,0},{10,2},{12,4},{14,6},{16,8},{18,10},{20,12},{22,14},{24,16},... | collective-permute-start | bytes 786440 | tf_op jit(solution)/shard_map/ppermute | solution.py:340
  160.4 7.2 %collective-permute-done.32 = bf16[512,256]{1,0:T(8,128)(2,1)S(1)} collective-permute-done((bf16[512,256]{1,0:T(8,128)(2,1)S(1)}, bf16[512,256]{1,0:T(8,128)(2,1)S(1)}, u32[]{:S(2)}, u32[]{:S(2)}) %collective-permute-start.32) | collective-permute-done | bytes 262176 | tf_op jit(solution)/shard_map/ppermute | solution.py:335
  167.5 2.7 %collective-permute-done.33 = bf16[512,256]{1,0:T(8,128)(2,1)S(1)} collective-permute-done((bf16[512,256]{1,0:T(8,128)(2,1)S(1)}, bf16[512,256]{1,0:T(8,128)(2,1)S(1)}, u32[]{:S(2)}, u32[]{:S(2)}) %collective-permute-start.33) | collective-permute-done | bytes 262176 | tf_op jit(solution)/shard_map/ppermute | solution.py:340
  170.2 6.3 %convolution_convert_fusion = bf16[1408,2048]{1,0:T(8,128)(2,1)S(1)} fusion(bf16[1408,384]{1,0:T(8,128)(2,1)S(1)} %collective-permute-done.25, bf16[1408,384]{1,0:T(8,128)(2,1)S(1)} %get-tuple-element.86, bf16[384,2048]{1,0:T(8,128)(2,1)} %collective-permute-done.2, bf16[384,2048]{1,0:T(8,128)(2,1)S(1)} %copy-done.11), kind=kOutput, calls=%fused_computation | convolution fusion | flops 4442685440 | bytes 11075584 | tf_op jit(solution)/shard_map/dot_general | solution.py:428
  185.9 3.4 %collective-permute-start.35 = (bf16[512,512]{1,0:T(8,128)(2,1)}, bf16[512,512]{1,0:T(8,128)(2,1)}, u32[]{:S(2)}, u32[]{:S(2)}) collective-permute-start(bf16[512,512]{1,0:T(8,128)(2,1)} %pad_maximum_fusion.9), channel_id=1, source_target_pairs={{8,0},{10,2},{12,4},{14,6},{16,8},{18,10},{20,12},{22,14},{24,16},... | collective-permute-start | bytes 1572872 | tf_op jit(solution)/shard_map/ppermute | solution.py:340
  189.3 3.6 %all-to-all-start.1 = ((bf16[16,128,128]{2,1,0:T(8,128)(2,1)}), bf16[16,128,128]{2,1,0:T(8,128)(2,1)S(1)}, u32[]{:S(2)}, u32[]{:S(2)}) async-start(bf16[16,128,128]{2,1,0:T(8,128)(2,1)} %bitcast.14), calls=%async_computation.1 | async-start | bytes 1048576 | tf_op jit(solution)/shard_map/all_to_all | solution.py:475
  192.9 8.6 %collective-permute-done.34 = bf16[512,512]{1,0:T(8,128)(2,1)} collective-permute-done((bf16[512,512]{1,0:T(8,128)(2,1)}, bf16[512,512]{1,0:T(8,128)(2,1)}, u32[]{:S(2)}, u32[]{:S(2)}) %collective-permute-start.34) | collective-permute-done | bytes 524320 | tf_op jit(solution)/shard_map/ppermute | solution.py:335
  201.6 9.4 %collective-permute-done.35 = bf16[512,512]{1,0:T(8,128)(2,1)} collective-permute-done((bf16[512,512]{1,0:T(8,128)(2,1)}, bf16[512,512]{1,0:T(8,128)(2,1)}, u32[]{:S(2)}, u32[]{:S(2)}) %collective-permute-start.35) | collective-permute-done | bytes 524320 | tf_op jit(solution)/shard_map/ppermute | solution.py:340
  215.8 6.4 %collective-permute-start.36 = (bf16[128,768]{1,0:T(8,128)(2,1)S(1)}, bf16[128,768]{1,0:T(8,128)(2,1)S(1)}, u32[]{:S(2)}, u32[]{:S(2)}) collective-permute-start(bf16[128,768]{1,0:T(8,128)(2,1)S(1)} %get-tuple-element.102), channel_id=1, source_target_pairs={{0,8},{2,10},{4,12},{6,14},{8,16},{10,18},{12,20},{14,22},{16,24},... | collective-permute-start | bytes 589832 | tf_op jit(solution)/shard_map/ppermute | solution.py:335
  225.5 2.9 %collective-permute-done.37 = bf16[128,768]{1,0:T(8,128)(2,1)S(1)} collective-permute-done((bf16[128,768]{1,0:T(8,128)(2,1)S(1)}, bf16[128,768]{1,0:T(8,128)(2,1)S(1)}, u32[]{:S(2)}, u32[]{:S(2)}) %collective-permute-start.37) | collective-permute-done | bytes 196640 | tf_op jit(solution)/shard_map/ppermute | solution.py:340
  228.4 2.7 %collective-permute-done.30 = bf16[128,2304]{1,0:T(8,128)(2,1)S(1)} collective-permute-done((bf16[128,2304]{1,0:T(8,128)(2,1)S(1)}, bf16[128,2304]{1,0:T(8,128)(2,1)S(1)}, u32[]{:S(2)}, u32[]{:S(2)}) %collective-permute-start.30) | collective-permute-done | bytes 589856 | tf_op jit(solution)/shard_map/ppermute | solution.py:326
  231.0 2.1 add_convert_fusion.5
  238.6 2.6 collective-permute-start.41
  242.3 8.9 %collective-permute-done.40 = bf16[128,1536]{1,0:T(8,128)(2,1)S(1)} collective-permute-done((bf16[128,1536]{1,0:T(8,128)(2,1)S(1)}, bf16[128,1536]{1,0:T(8,128)(2,1)S(1)}, u32[]{:S(2)}, u32[]{:S(2)}) %collective-permute-start.40) | collective-permute-done | bytes 393248 | tf_op jit(solution)/shard_map/ppermute | solution.py:335
  251.2 4.8 %collective-permute-done.41 = bf16[128,1536]{1,0:T(8,128)(2,1)S(1)} collective-permute-done((bf16[128,1536]{1,0:T(8,128)(2,1)S(1)}, bf16[128,1536]{1,0:T(8,128)(2,1)S(1)}, u32[]{:S(2)}, u32[]{:S(2)}) %collective-permute-start.41) | collective-permute-done | bytes 393248 | tf_op jit(solution)/shard_map/ppermute | solution.py:340
  259.6 1.6 add_convert_fusion.3
  261.9 2.0 collective-permute-done.43
  (187 shorter events, 65.5 us)
Async XLA Ops:
  2.4 19.6 %collective-permute-start = (bf16[96,2048]{1,0:T(8,128)(2,1)}, bf16[96,2048]{1,0:T(8,128)(2,1)S(1)}, u32[]{:S(2)}, u32[]{:S(2)}) collective-permute-start(bf16[96,2048]{1,0:T(8,128)(2,1)} %constant_dynamic-slice_fusion), channel_id=1, source_target_pairs={{0,8},{2,10},{4,12},{6,14},{8,16},{10,18},{12,20},{14,22},{16,24},... | collective-permute-start | bytes 1179656 | tf_op jit(solution)/shard_map/ppermute | solution.py:335
  5.4 20.0 %collective-permute-start.1 = (bf16[96,2048]{1,0:T(8,128)(2,1)}, bf16[96,2048]{1,0:T(8,128)(2,1)}, u32[]{:S(2)}, u32[]{:S(2)}) collective-permute-start(bf16[96,2048]{1,0:T(8,128)(2,1)} %constant_dynamic-slice_fusion), channel_id=1, source_target_pairs={{8,0},{10,2},{12,4},{14,6},{16,8},{18,10},{20,12},{22,14},{24,16},... | collective-permute-start | bytes 1179656 | tf_op jit(solution)/shard_map/ppermute | solution.py:340
  9.6 20.8 %collective-permute-start.3 = (bf16[128,2048]{1,0:T(8,128)(2,1)}, bf16[128,2048]{1,0:T(8,128)(2,1)S(1)}, u32[]{:S(2)}, u32[]{:S(2)}) collective-permute-start(bf16[128,2048]{1,0:T(8,128)(2,1)} %get-tuple-element.124), channel_id=1, source_target_pairs={{0,2},{2,0},{4,6},{6,4},{8,10},{10,8},{12,14},{14,12},{16,18},{18,... | collective-permute-start | bytes 1572872 | tf_op jit(solution)/shard_map/ppermute | solution.py:326
  11.3 19.1 %collective-permute-start.4 = (bf16[128,2048]{1,0:T(8,128)(2,1)}, bf16[128,2048]{1,0:T(8,128)(2,1)S(1)}, u32[]{:S(2)}, u32[]{:S(2)}) collective-permute-start(bf16[128,2048]{1,0:T(8,128)(2,1)} %get-tuple-element.124), channel_id=1, source_target_pairs={{0,4},{2,6},{4,0},{6,2},{8,12},{10,14},{12,8},{14,10},{16,20},{18,... | collective-permute-start | bytes 1572872 | tf_op jit(solution)/shard_map/ppermute | solution.py:330
  16.2 58.4 %copy-start.10 = (bf16[384,2048]{1,0:T(8,128)(2,1)}, bf16[384,2048]{1,0:T(8,128)(2,1)S(1)}, u32[]{:S(2)}) copy-start(bf16[384,2048]{1,0:T(8,128)(2,1)S(1)} %get-tuple-element.156) | copy-start | bytes 4718596
  16.2 58.3 %collective-permute-start.2 = (bf16[384,2048]{1,0:T(8,128)(2,1)}, bf16[384,2048]{1,0:T(8,128)(2,1)}, u32[]{:S(2)}, u32[]{:S(2)}) collective-permute-start(bf16[384,2048]{1,0:T(8,128)(2,1)} %get-tuple-element.155), channel_id=1, source_target_pairs={{0,1},{1,0},{2,3},{3,2},{4,5},{5,4},{6,7},{7,6},{8,9},{9,8},{10,11... | collective-permute-start | bytes 4718600 | tf_op jit(solution)/shard_map/ppermute | solution.py:322
  17.5 60.6 %all-to-all-start = ((bf16[128,16,128]{2,0,1:T(8,128)(2,1)}), bf16[128,16,128]{2,0,1:T(8,128)(2,1)S(1)}, u32[]{:S(2)}, u32[]{:S(2)}) async-start(bf16[128,16,128]{2,0,1:T(8,128)(2,1)} %copy.8), calls=%async_computation | async-start | bytes 1048576 | tf_op jit(solution)/shard_map/all_to_all | solution.py:547
  25.5 13.7 %collective-permute-start.9 = (bf16[48,2048]{1,0:T(8,128)(2,1)S(1)}, bf16[48,2048]{1,0:T(8,128)(2,1)S(1)}, u32[]{:S(2)}, u32[]{:S(2)}) collective-permute-start(bf16[48,2048]{1,0:T(8,128)(2,1)S(1)} %slice.492), channel_id=1, source_target_pairs={{0,8},{2,10},{4,12},{6,14},{8,16},{10,18},{12,20},{14,22},{16,24},... | collective-permute-start | bytes 589832 | tf_op jit(solution)/shard_map/ppermute | solution.py:335
  27.0 14.5 %collective-permute-start.10 = (bf16[48,2048]{1,0:T(8,128)(2,1)S(1)}, bf16[48,2048]{1,0:T(8,128)(2,1)S(1)}, u32[]{:S(2)}, u32[]{:S(2)}) collective-permute-start(bf16[48,2048]{1,0:T(8,128)(2,1)S(1)} %slice.493), channel_id=1, source_target_pairs={{8,0},{10,2},{12,4},{14,6},{16,8},{18,10},{20,12},{22,14},{24,16},... | collective-permute-start | bytes 589832 | tf_op jit(solution)/shard_map/ppermute | solution.py:340
  30.5 11.8 %collective-permute-start.5 = (bf16[64,2048]{1,0:T(8,128)(2,1)S(1)}, bf16[64,2048]{1,0:T(8,128)(2,1)S(1)}, u32[]{:S(2)}, u32[]{:S(2)}) collective-permute-start(bf16[64,2048]{1,0:T(8,128)(2,1)S(1)} %pad_maximum_fusion.18), channel_id=1, source_target_pairs={{0,2},{2,0},{4,6},{6,4},{8,10},{10,8},{12,14},{14,12},{16,18},{18,... | collective-permute-start | bytes 786440 | tf_op jit(solution)/shard_map/ppermute | solution.py:326
  32.1 10.2 %collective-permute-start.6 = (bf16[64,2048]{1,0:T(8,128)(2,1)S(1)}, bf16[64,2048]{1,0:T(8,128)(2,1)S(1)}, u32[]{:S(2)}, u32[]{:S(2)}) collective-permute-start(bf16[64,2048]{1,0:T(8,128)(2,1)S(1)} %pad_maximum_fusion.19), channel_id=1, source_target_pairs={{0,4},{2,6},{4,0},{6,2},{8,12},{10,14},{12,8},{14,10},{16,20},{18,... | collective-permute-start | bytes 786440 | tf_op jit(solution)/shard_map/ppermute | solution.py:330
  43.7 16.7 %collective-permute-start.11 = (bf16[128,2048]{1,0:T(8,128)(2,1)S(1)}, bf16[128,2048]{1,0:T(8,128)(2,1)S(1)}, u32[]{:S(2)}, u32[]{:S(2)}) collective-permute-start(bf16[128,2048]{1,0:T(8,128)(2,1)S(1)} %slice_dynamic-update-slice_fusion.8), channel_id=1, source_target_pairs={{0,8},{2,10},{4,12},{6,14},{8,16},{10,18},{12,20},{14,22},{16,24},... | collective-permute-start | bytes 1572872 | tf_op jit(solution)/shard_map/ppermute | solution.py:335
  47.7 22.4 %collective-permute-start.12 = (bf16[128,2048]{1,0:T(8,128)(2,1)S(1)}, bf16[128,2048]{1,0:T(8,128)(2,1)S(1)}, u32[]{:S(2)}, u32[]{:S(2)}) collective-permute-start(bf16[128,2048]{1,0:T(8,128)(2,1)S(1)} %slice_dynamic-update-slice_fusion.8), channel_id=1, source_target_pairs={{8,0},{10,2},{12,4},{14,6},{16,8},{18,10},{20,12},{22,14},{24,16},... | collective-permute-start | bytes 1572872 | tf_op jit(solution)/shard_map/ppermute | solution.py:340
  70.1 12.5 %collective-permute-start.17 = (bf16[64,2048]{1,0:T(8,128)(2,1)S(1)}, bf16[64,2048]{1,0:T(8,128)(2,1)S(1)}, u32[]{:S(2)}, u32[]{:S(2)}) collective-permute-start(bf16[64,2048]{1,0:T(8,128)(2,1)S(1)} %slice.500), channel_id=1, source_target_pairs={{0,8},{2,10},{4,12},{6,14},{8,16},{10,18},{12,20},{14,22},{16,24},... | collective-permute-start | bytes 786440 | tf_op jit(solution)/shard_map/ppermute | solution.py:335
  70.7 13.9 %collective-permute-start.18 = (bf16[64,2048]{1,0:T(8,128)(2,1)S(1)}, bf16[64,2048]{1,0:T(8,128)(2,1)}, u32[]{:S(2)}, u32[]{:S(2)}) collective-permute-start(bf16[64,2048]{1,0:T(8,128)(2,1)S(1)} %slice.501), channel_id=1, source_target_pairs={{8,0},{10,2},{12,4},{14,6},{16,8},{18,10},{20,12},{22,14},{24,16},... | collective-permute-start | bytes 786440 | tf_op jit(solution)/shard_map/ppermute | solution.py:340
  78.1 18.7 %collective-permute-start.7 = (bf16[192,2048]{1,0:T(8,128)(2,1)}, bf16[192,2048]{1,0:T(8,128)(2,1)S(1)}, u32[]{:S(2)}, u32[]{:S(2)}) collective-permute-start(bf16[192,2048]{1,0:T(8,128)(2,1)} %pad_maximum_fusion.6), channel_id=1, source_target_pairs={{0,2},{2,0},{4,6},{6,4},{8,10},{10,8},{12,14},{14,12},{16,18},{18,... | collective-permute-start | bytes 2359304 | tf_op jit(solution)/shard_map/ppermute | solution.py:326
  79.6 18.4 %collective-permute-start.8 = (bf16[192,2048]{1,0:T(8,128)(2,1)}, bf16[192,2048]{1,0:T(8,128)(2,1)S(1)}, u32[]{:S(2)}, u32[]{:S(2)}) collective-permute-start(bf16[192,2048]{1,0:T(8,128)(2,1)} %pad_maximum_fusion.6), channel_id=1, source_target_pairs={{0,4},{2,6},{4,0},{6,2},{8,12},{10,14},{12,8},{14,10},{16,20},{18,... | collective-permute-start | bytes 2359304 | tf_op jit(solution)/shard_map/ppermute | solution.py:330
  89.8 37.1 %collective-permute-start.19 = (bf16[512,384]{1,0:T(8,128)(2,1)}, bf16[512,384]{1,0:T(8,128)(2,1)}, u32[]{:S(2)}, u32[]{:S(2)}) collective-permute-start(bf16[512,384]{1,0:T(8,128)(2,1)} %slice.711), channel_id=1, source_target_pairs={{0,1},{1,0},{2,3},{3,2},{4,5},{5,4},{6,7},{7,6},{8,9},{9,8},{10,11... | collective-permute-start | bytes 1179656 | tf_op jit(solution)/shard_map/ppermute | solution.py:322
  98.2 17.4 %collective-permute-start.13 = (bf16[192,2048]{1,0:T(8,128)(2,1)S(1)}, bf16[192,2048]{1,0:T(8,128)(2,1)S(1)}, u32[]{:S(2)}, u32[]{:S(2)}) collective-permute-start(bf16[192,2048]{1,0:T(8,128)(2,1)S(1)} %get-tuple-element.174), channel_id=1, source_target_pairs={{0,2},{2,0},{4,6},{6,4},{8,10},{10,8},{12,14},{14,12},{16,18},{18,... | collective-permute-start | bytes 2359304 | tf_op jit(solution)/shard_map/ppermute | solution.py:326
  98.9 17.1 %collective-permute-start.14 = (bf16[192,2048]{1,0:T(8,128)(2,1)S(1)}, bf16[192,2048]{1,0:T(8,128)(2,1)S(1)}, u32[]{:S(2)}, u32[]{:S(2)}) collective-permute-start(bf16[192,2048]{1,0:T(8,128)(2,1)S(1)} %get-tuple-element.173), channel_id=1, source_target_pairs={{0,4},{2,6},{4,0},{6,2},{8,12},{10,14},{12,8},{14,10},{16,20},{18,... | collective-permute-start | bytes 2359304 | tf_op jit(solution)/shard_map/ppermute | solution.py:330
  103.3 23.6 %collective-permute-start.21 = (bf16[256,384]{1,0:T(8,128)(2,1)}, bf16[256,384]{1,0:T(8,128)(2,1)S(1)}, u32[]{:S(2)}, u32[]{:S(2)}) collective-permute-start(bf16[256,384]{1,0:T(8,128)(2,1)} %slice.713), channel_id=1, source_target_pairs={{0,1},{1,0},{2,3},{3,2},{4,5},{5,4},{6,7},{7,6},{8,9},{9,8},{10,11... | collective-permute-start | bytes 589832 | tf_op jit(solution)/shard_map/ppermute | solution.py:322
  107.2 19.7 %collective-permute-start.20 = (bf16[576,384]{1,0:T(8,128)(2,1)}, bf16[576,384]{1,0:T(8,128)(2,1)}, u32[]{:S(2)}, u32[]{:S(2)}) collective-permute-start(bf16[576,384]{1,0:T(8,128)(2,1)} %slice.710), channel_id=1, source_target_pairs={{0,1},{1,0},{2,3},{3,2},{4,5},{5,4},{6,7},{7,6},{8,9},{9,8},{10,11... | collective-permute-start | bytes 1327112 | tf_op jit(solution)/shard_map/ppermute | solution.py:322
  116.0 6.0 %collective-permute-start.15 = (bf16[48,2048]{1,0:T(8,128)(2,1)S(1)}, bf16[48,2048]{1,0:T(8,128)(2,1)S(1)}, u32[]{:S(2)}, u32[]{:S(2)}) collective-permute-start(bf16[48,2048]{1,0:T(8,128)(2,1)S(1)} %slice.498), channel_id=1, source_target_pairs={{0,2},{2,0},{4,6},{6,4},{8,10},{10,8},{12,14},{14,12},{16,18},{18,... | collective-permute-start | bytes 589832 | tf_op jit(solution)/shard_map/ppermute | solution.py:326
  117.5 5.7 %collective-permute-start.16 = (bf16[48,2048]{1,0:T(8,128)(2,1)S(1)}, bf16[48,2048]{1,0:T(8,128)(2,1)S(1)}, u32[]{:S(2)}, u32[]{:S(2)}) collective-permute-start(bf16[48,2048]{1,0:T(8,128)(2,1)S(1)} %slice.499), channel_id=1, source_target_pairs={{0,4},{2,6},{4,0},{6,2},{8,12},{10,14},{12,8},{14,10},{16,20},{18,... | collective-permute-start | bytes 589832 | tf_op jit(solution)/shard_map/ppermute | solution.py:330
  122.0 5.0 %collective-permute-start.22 = (bf16[480,384]{1,0:T(8,128)(2,1)}, bf16[480,384]{1,0:T(8,128)(2,1)}, u32[]{:S(2)}, u32[]{:S(2)}) collective-permute-start(bf16[480,384]{1,0:T(8,128)(2,1)} %slice.712), channel_id=1, source_target_pairs={{0,1},{1,0},{2,3},{3,2},{4,5},{5,4},{6,7},{7,6},{8,9},{9,8},{10,11... | collective-permute-start | bytes 1105928 | tf_op jit(solution)/shard_map/ppermute | solution.py:322
  126.9 1.7 collective-permute-start.23
  147.9 1.9 collective-permute-start.24
  153.4 16.8 %collective-permute-start.25 = (bf16[1408,384]{1,0:T(8,128)(2,1)S(1)}, bf16[1408,384]{1,0:T(8,128)(2,1)S(1)}, u32[]{:S(2)}, u32[]{:S(2)}) collective-permute-start(bf16[1408,384]{1,0:T(8,128)(2,1)S(1)} %get-tuple-element.86), channel_id=1, source_target_pairs={{0,1},{1,0},{2,3},{3,2},{4,5},{5,4},{6,7},{7,6},{8,9},{9,8},{10,11... | collective-permute-start | bytes 3244040 | tf_op jit(solution)/shard_map/ppermute | solution.py:322
  153.7 16.5 %collective-permute-start.26 = (bf16[128,1536]{1,0:T(8,128)(2,1)S(1)}, bf16[128,1536]{1,0:T(8,128)(2,1)S(1)}, u32[]{:S(2)}, u32[]{:S(2)}) collective-permute-start(bf16[128,1536]{1,0:T(8,128)(2,1)S(1)} %pad_maximum_fusion.14), channel_id=1, source_target_pairs={{0,2},{2,0},{4,6},{6,4},{8,10},{10,8},{12,14},{14,12},{16,18},{18,... | collective-permute-start | bytes 1179656 | tf_op jit(solution)/shard_map/ppermute | solution.py:326
  154.4 15.8 %collective-permute-start.27 = (bf16[128,1536]{1,0:T(8,128)(2,1)S(1)}, bf16[128,1536]{1,0:T(8,128)(2,1)S(1)}, u32[]{:S(2)}, u32[]{:S(2)}) collective-permute-start(bf16[128,1536]{1,0:T(8,128)(2,1)S(1)} %pad_maximum_fusion.15), channel_id=1, source_target_pairs={{0,4},{2,6},{4,0},{6,2},{8,12},{10,14},{12,8},{14,10},{16,20},{18,... | collective-permute-start | bytes 1179656 | tf_op jit(solution)/shard_map/ppermute | solution.py:330
  156.3 11.3 %collective-permute-start.32 = (bf16[512,256]{1,0:T(8,128)(2,1)S(1)}, bf16[512,256]{1,0:T(8,128)(2,1)S(1)}, u32[]{:S(2)}, u32[]{:S(2)}) collective-permute-start(bf16[512,256]{1,0:T(8,128)(2,1)S(1)} %get-tuple-element.160), channel_id=1, source_target_pairs={{0,8},{2,10},{4,12},{6,14},{8,16},{10,18},{12,20},{14,22},{16,24},... | collective-permute-start | bytes 786440 | tf_op jit(solution)/shard_map/ppermute | solution.py:335
  156.5 13.7 %collective-permute-start.33 = (bf16[512,256]{1,0:T(8,128)(2,1)S(1)}, bf16[512,256]{1,0:T(8,128)(2,1)S(1)}, u32[]{:S(2)}, u32[]{:S(2)}) collective-permute-start(bf16[512,256]{1,0:T(8,128)(2,1)S(1)} %get-tuple-element.159), channel_id=1, source_target_pairs={{8,0},{10,2},{12,4},{14,6},{16,8},{18,10},{20,12},{22,14},{24,16},... | collective-permute-start | bytes 786440 | tf_op jit(solution)/shard_map/ppermute | solution.py:340
  181.9 29.1 %collective-permute-start.28 = (bf16[128,3840]{1,0:T(8,128)(2,1)}, bf16[128,3840]{1,0:T(8,128)(2,1)}, u32[]{:S(2)}, u32[]{:S(2)}) collective-permute-start(bf16[128,3840]{1,0:T(8,128)(2,1)} %get-tuple-element.142), channel_id=1, source_target_pairs={{0,2},{2,0},{4,6},{6,4},{8,10},{10,8},{12,14},{14,12},{16,18},{18,... | collective-permute-start | bytes 2949128 | tf_op jit(solution)/shard_map/ppermute | solution.py:326
  183.3 27.6 %collective-permute-start.29 = (bf16[128,3840]{1,0:T(8,128)(2,1)}, bf16[128,3840]{1,0:T(8,128)(2,1)}, u32[]{:S(2)}, u32[]{:S(2)}) collective-permute-start(bf16[128,3840]{1,0:T(8,128)(2,1)} %get-tuple-element.141), channel_id=1, source_target_pairs={{0,4},{2,6},{4,0},{6,2},{8,12},{10,14},{12,8},{14,10},{16,20},{18,... | collective-permute-start | bytes 2949128 | tf_op jit(solution)/shard_map/ppermute | solution.py:330
  184.6 17.0 %collective-permute-start.34 = (bf16[512,512]{1,0:T(8,128)(2,1)}, bf16[512,512]{1,0:T(8,128)(2,1)}, u32[]{:S(2)}, u32[]{:S(2)}) collective-permute-start(bf16[512,512]{1,0:T(8,128)(2,1)} %maximum_maximum_fusion), channel_id=1, source_target_pairs={{0,8},{2,10},{4,12},{6,14},{8,16},{10,18},{12,20},{14,22},{16,24},... | collective-permute-start | bytes 1572872 | tf_op jit(solution)/shard_map/ppermute | solution.py:335
  185.9 25.1 %collective-permute-start.35 = (bf16[512,512]{1,0:T(8,128)(2,1)}, bf16[512,512]{1,0:T(8,128)(2,1)}, u32[]{:S(2)}, u32[]{:S(2)}) collective-permute-start(bf16[512,512]{1,0:T(8,128)(2,1)} %pad_maximum_fusion.9), channel_id=1, source_target_pairs={{8,0},{10,2},{12,4},{14,6},{16,8},{18,10},{20,12},{22,14},{24,16},... | collective-permute-start | bytes 1572872 | tf_op jit(solution)/shard_map/ppermute | solution.py:340
  189.3 52.0 %all-to-all-start.1 = ((bf16[16,128,128]{2,1,0:T(8,128)(2,1)}), bf16[16,128,128]{2,1,0:T(8,128)(2,1)S(1)}, u32[]{:S(2)}, u32[]{:S(2)}) async-start(bf16[16,128,128]{2,1,0:T(8,128)(2,1)} %bitcast.14), calls=%async_computation.1 | async-start | bytes 1048576 | tf_op jit(solution)/shard_map/all_to_all | solution.py:475
  213.7 17.3 %collective-permute-start.30 = (bf16[128,2304]{1,0:T(8,128)(2,1)S(1)}, bf16[128,2304]{1,0:T(8,128)(2,1)S(1)}, u32[]{:S(2)}, u32[]{:S(2)}) collective-permute-start(bf16[128,2304]{1,0:T(8,128)(2,1)S(1)} %pad_maximum_fusion.7), channel_id=1, source_target_pairs={{0,2},{2,0},{4,6},{6,4},{8,10},{10,8},{12,14},{14,12},{16,18},{18,... | collective-permute-start | bytes 1769480 | tf_op jit(solution)/shard_map/ppermute | solution.py:326
  214.4 16.7 %collective-permute-start.31 = (bf16[128,2304]{1,0:T(8,128)(2,1)S(1)}, bf16[128,2304]{1,0:T(8,128)(2,1)S(1)}, u32[]{:S(2)}, u32[]{:S(2)}) collective-permute-start(bf16[128,2304]{1,0:T(8,128)(2,1)S(1)} %pad_maximum_fusion.8), channel_id=1, source_target_pairs={{0,4},{2,6},{4,0},{6,2},{8,12},{10,14},{12,8},{14,10},{16,20},{18,... | collective-permute-start | bytes 1769480 | tf_op jit(solution)/shard_map/ppermute | solution.py:330
  215.8 9.7 %collective-permute-start.36 = (bf16[128,768]{1,0:T(8,128)(2,1)S(1)}, bf16[128,768]{1,0:T(8,128)(2,1)S(1)}, u32[]{:S(2)}, u32[]{:S(2)}) collective-permute-start(bf16[128,768]{1,0:T(8,128)(2,1)S(1)} %get-tuple-element.102), channel_id=1, source_target_pairs={{0,8},{2,10},{4,12},{6,14},{8,16},{10,18},{12,20},{14,22},{16,24},... | collective-permute-start | bytes 589832 | tf_op jit(solution)/shard_map/ppermute | solution.py:335
  222.2 6.1 %collective-permute-start.37 = (bf16[128,768]{1,0:T(8,128)(2,1)S(1)}, bf16[128,768]{1,0:T(8,128)(2,1)S(1)}, u32[]{:S(2)}, u32[]{:S(2)}) collective-permute-start(bf16[128,768]{1,0:T(8,128)(2,1)S(1)} %get-tuple-element.103), channel_id=1, source_target_pairs={{8,0},{10,2},{12,4},{14,6},{16,8},{18,10},{20,12},{22,14},{24,16},... | collective-permute-start | bytes 589832 | tf_op jit(solution)/shard_map/ppermute | solution.py:340
  234.0 22.0 %collective-permute-start.38 = (bf16[128,1792]{1,0:T(8,128)(2,1)}, bf16[128,1792]{1,0:T(8,128)(2,1)}, u32[]{:S(2)}, u32[]{:S(2)}) collective-permute-start(bf16[128,1792]{1,0:T(8,128)(2,1)} %pad_maximum_fusion.11), channel_id=1, source_target_pairs={{0,2},{2,0},{4,6},{6,4},{8,10},{10,8},{12,14},{14,12},{16,18},{18,... | collective-permute-start | bytes 1376264 | tf_op jit(solution)/shard_map/ppermute | solution.py:326
  235.2 23.7 %copy-start.24 = (bf16[128,256]{1,0:T(8,128)(2,1)S(1)}, bf16[128,256]{1,0:T(8,128)(2,1)}, u32[]{:S(2)}) copy-start(bf16[128,256]{1,0:T(8,128)(2,1)} %get-tuple-element.177) | copy-start | bytes 196612
  236.1 19.9 %collective-permute-start.39 = (bf16[128,1792]{1,0:T(8,128)(2,1)}, bf16[128,1792]{1,0:T(8,128)(2,1)}, u32[]{:S(2)}, u32[]{:S(2)}) collective-permute-start(bf16[128,1792]{1,0:T(8,128)(2,1)} %pad_maximum_fusion.12), channel_id=1, source_target_pairs={{0,4},{2,6},{4,0},{6,2},{8,12},{10,14},{12,8},{14,10},{16,20},{18,... | collective-permute-start | bytes 1376264 | tf_op jit(solution)/shard_map/ppermute | solution.py:330
  237.3 13.9 %collective-permute-start.40 = (bf16[128,1536]{1,0:T(8,128)(2,1)S(1)}, bf16[128,1536]{1,0:T(8,128)(2,1)S(1)}, u32[]{:S(2)}, u32[]{:S(2)}) collective-permute-start(bf16[128,1536]{1,0:T(8,128)(2,1)S(1)} %pad_maximum_fusion.16), channel_id=1, source_target_pairs={{0,8},{2,10},{4,12},{6,14},{8,16},{10,18},{12,20},{14,22},{16,24},... | collective-permute-start | bytes 1179656 | tf_op jit(solution)/shard_map/ppermute | solution.py:335
  238.6 17.3 %collective-permute-start.41 = (bf16[128,1536]{1,0:T(8,128)(2,1)S(1)}, bf16[128,1536]{1,0:T(8,128)(2,1)S(1)}, u32[]{:S(2)}, u32[]{:S(2)}) collective-permute-start(bf16[128,1536]{1,0:T(8,128)(2,1)S(1)} %pad_maximum_fusion.17), channel_id=1, source_target_pairs={{8,0},{10,2},{12,4},{14,6},{16,8},{18,10},{20,12},{22,14},{24,16},... | collective-permute-start | bytes 1179656 | tf_op jit(solution)/shard_map/ppermute | solution.py:340
  256.9 5.0 %collective-permute-start.42 = (bf16[128,512]{1,0:T(8,128)(2,1)S(1)}, bf16[128,512]{1,0:T(8,128)(2,1)S(1)}, u32[]{:S(2)}, u32[]{:S(2)}) collective-permute-start(bf16[128,512]{1,0:T(8,128)(2,1)S(1)} %pad_maximum_fusion.20), channel_id=1, source_target_pairs={{0,2},{2,0},{4,6},{6,4},{8,10},{10,8},{12,14},{14,12},{16,18},{18,... | collective-permute-start | bytes 393224 | tf_op jit(solution)/shard_map/ppermute | solution.py:326
  258.9 5.0 %collective-permute-start.43 = (bf16[128,512]{1,0:T(8,128)(2,1)S(1)}, bf16[128,512]{1,0:T(8,128)(2,1)S(1)}, u32[]{:S(2)}, u32[]{:S(2)}) collective-permute-start(bf16[128,512]{1,0:T(8,128)(2,1)S(1)} %pad_maximum_fusion.21), channel_id=1, source_target_pairs={{0,4},{2,6},{4,0},{6,2},{8,12},{10,14},{12,8},{14,10},{16,20},{18,... | collective-permute-start | bytes 393224 | tf_op jit(solution)/shard_map/ppermute | solution.py:330
  (30 other events, 252.0 us)
where the time goes:
time: 266 us; the launch traced here: 265 us
  waiting for transfers between devices  102 us (38%)
  starting transfers between devices  70.3 us (26%)
  local copies, waits for them, and re-layouts  29.7 us (11%)
  other arithmetic  24.7 us (9%)
  matrix products  22.4 us (8%)
  Pallas kernels  14.6 us (5%)
    ppermute x8, waiting for transfers between devices, up(): lax.ppermute(value, 'ctx', [(i, (i + PLANE) % count) for i in range(count)])  38.9 us
    ppermute x8, waiting for transfers between devices, down(): lax.ppermute(value, 'ctx', [((i + PLANE) % count, i) for i in range(count)])  36.4 us
    ppermute x8, starting transfers between devices, down(): lax.ppermute(value, 'ctx', [((i + PLANE) % count, i) for i in range(count)])  19.2 us
    ppermute x10, waiting for transfers between devices, over_x(): lax.ppermute(value, 'ctx', [(i, i ^ 1) for i in range(lax.axis_size('ctx'...  18.2 us
    ppermute x8, starting transfers between devices, up(): lax.ppermute(value, 'ctx', [(i, (i + PLANE) % count) for i in range(count)])  16.5 us
    pallas_call x1, Pallas kernels, scan_all(): pl.pallas_call(functools.partial(scan_kernel, PLANE, runs, order), out_sh...  14.6 us
    ppermute x10, starting transfers between devices, over_y(): lax.ppermute(value, 'ctx', [(i, i ^ 2) for i in range(lax.axis_size('ctx'...  14.6 us
    unnamed x72, local copies, waits for them, and re-layouts  14 us
  transfers between devices with their start and end apart: 46, of which 24 were waited for; matrix products, arithmetic and copies ran while one was open for 19% of the time, Pallas kernels for 0%

commit v1 on v0

--- a/solution.py
+++ b/solution.py
@@ -177,16 +177,23 @@
     runs,
     order,
     me_ref,
-    cot_ref,
     residue_ref,
     rate_ref,
     *refs,
 ):
     inputs = 1 + max(run[0] for run in runs)
-    own, other = refs[:inputs], refs[inputs : 2 * inputs]
-    hyena_ref, grad_ref = refs[2 * inputs : 2 * inputs + 2]
-    proj_refs = refs[2 * inputs + 2 : 2 * inputs + 2 + len(order)]
-    gated_s, slope_s, conv_s, back_s, feats_s = refs[2 * inputs + 2 + len(order) :]
+    arrays, refs = refs[: 2 * inputs + 1], refs[2 * inputs + 1 :]
+    hyena_ref, grad_ref = refs[:2]
+    proj_refs, refs = refs[2 : 2 + len(order)], refs[2 + len(order) :]
+    gated_s, slope_s, conv_s, back_s, feats_s, arrived = refs[:6]
+    held = refs[6:]
+    cot_ref, own, other = held[0], held[1 : 1 + inputs], held[1 + inputs :]
+    copies = [
+        pltpu.make_async_copy(array, here, arrived.at[k])
+        for k, (array, here) in enumerate(zip(arrays, held))
+    ]
+    for copy in copies:
+        copy.start()
     length, width = cot_ref.shape
     chunks = PLANE * groups
     span = length // chunks
@@ -199,13 +206,19 @@
     def aligned(start, size):
         return pl.ds(pl.multiple_of(start, size), size)
 
-    for source, offset, group, base, members, count, first in runs:
+    copies[0].wait()
+    waited = set()
+    for source, offset, group, base, members, count, first in sorted(runs):
+        if source not in waited:
+            waited.add(source)
+            copies[1 + source].wait()
+            copies[1 + inputs + source].wait()
 
         def before(step, _, source=source, offset=offset, group=group, base=base, count=count, first=first):
             member = base + step
             index = place(group, member)
             rows = pl.ds(pl.multiple_of(offset + step * count, 16), count)
-            feats = own[source][rows, 3 * width :] + other[source][rows, :].astype(jnp.float32)
+            feats = own[source][rows, :] + other[source][rows, :].astype(jnp.float32)
             feats = rounded(feats)
             slot = (group * PLANE + member) * span + first
             feats_s[pl.ds(pl.multiple_of(slot, 16), count), :] = feats
@@ -298,6 +311,7 @@
     length, width = cot_cols.shape
     span = length // (PLANE * PLANE)
     vmem = pl.BlockSpec(memory_space=pltpu.VMEM)
+    arrays = (cot_cols, *own, *other)
     outs = pl.pallas_call(
         functools.partial(scan_kernel, PLANE, runs, order),
         out_shape=(
@@ -308,13 +322,15 @@
             jax.ShapeDtypeStruct((span * sum(piece[2] for piece in pieces), 3 * width), jnp.bfloat16)
             for pieces in order
         ),
-        in_specs=[pl.BlockSpec(memory_space=pltpu.SMEM)] + [vmem] * (3 + 2 * len(own)),
+        in_specs=[pl.BlockSpec(memory_space=pltpu.SMEM), vmem, vmem]
+        + [pl.BlockSpec(memory_space=pl.ANY)] * len(arrays),
         out_specs=(vmem,) * (2 + len(order)),
         scratch_shapes=[pltpu.VMEM((length, width), jnp.float32)] * 4
-        + [pltpu.VMEM((length, 3 * width), jnp.float32)],
+        + [pltpu.VMEM((length, 3 * width), jnp.float32), pltpu.SemaphoreType.DMA((len(arrays),))]
+        + [pltpu.VMEM(array.shape, array.dtype) for array in arrays],
         compiler_params=pltpu.CompilerParams(vmem_limit_bytes=40 * 2**20),
         name="modal_scan",
-    )(me, cot_cols, residue_rows, rate_rows, *own, *other)
+    )(me, residue_rows, rate_rows, *arrays)
     return outs[0], outs[1], outs[2:]
 
 
@@ -356,78 +372,92 @@
     return value.astype(jnp.float32)
 
 
-def over_plane(for_x, for_y):
-    return lax.optimization_barrier((over_x(for_x), over_y(for_y)))
-
-
-def over_depth(for_above, for_below):
-    return lax.optimization_barrier((up(for_above), down(for_below)))
-
-
-def gather_groups(tokens, matrix, others):
+def all_ways(for_x, for_y, for_above, for_below):
+    return lax.optimization_barrier((over_x(for_x), over_y(for_y), up(for_above), down(for_below)))
+
+
+def gather_groups(tokens, prepared):
     span = tokens.shape[0]
     n, m = span * 3 // 4, span // 4
     nh, mh = n // 2, m // 2
-    wide = tokens[:n]
-    own_x, own_y = over_plane(tokens, tokens)
-    wide_3, wide_1 = over_depth(wide, wide)
-    across_x, across_y = over_plane(
-        stack(own_y[:nh], own_y[n : n + mh]), stack(own_x[nh:n], own_x[n + mh :])
-    )
-    wide_2 = stack(*over_depth(wide_3[:nh], wide_1[nh:]))
-    near = stack(wide_3, wide_1)
-    near, matrix, others = lax.optimization_barrier((near, matrix, others))
-    near_x, near_y = over_plane(near, near)
-    plane = stack(tokens[n:], own_x[n:], own_y[n:], across_x[nh:], across_y[nh:])
-    plane, wide_2 = lax.optimization_barrier((plane, wide_2))
-    plane_3, plane_1 = over_depth(plane, plane)
-    far_x, far_y = over_plane(
-        stack(near_y[:nh], near_y[n : n + nh], wide_2), stack(near_x[nh:n], near_x[n + nh :], wide_2)
-    )
-    half = plane.shape[0] // 2
-    far = over_depth(plane_3[:half], plane_1[half:])
-    last_x, last_y = over_plane(far_y[n : n + nh], far_x[n + nh :])
-    parts = (
-        stack(tokens, own_x, own_y, across_x, across_y),
-        stack(near, near_x, near_y),
-        stack(plane_1, plane_3),
-        stack(wide_2, far_x, far_y),
-        stack(last_x, last_y, *far),
-    )
+    wide, narrow = tokens[:n], tokens[n:]
+    own_x, own_y, wide_3, wide_1 = all_ways(tokens, tokens, wide, wide)
+    own_x, prepared = lax.optimization_barrier((own_x, prepared))
+    members = (narrow, own_x[n:], own_y[n:])
+    first = (tokens, own_x, own_y, wide_3, wide_1)
+    second = all_ways(
+        stack(own_y[:nh], own_y[n : n + mh], wide_3, wide_1),
+        stack(own_x[nh:n], own_x[n + mh :], wide_3, wide_1),
+        stack(wide_3[:nh], *members),
+        stack(wide_1[nh:], *members),
+    )
+    got_x, got_y, below, above = second
+    start = nh + mh
+    across = (got_x[nh:start], got_y[nh:start])
+    wide_2 = (below[:nh], above[:nh])
+    third = all_ways(
+        stack(got_y[start : start + nh], got_y[start + n : start + n + nh], *wide_2),
+        stack(got_x[start + nh : start + n], got_x[start + n + nh :], *wide_2),
+        stack(*across, below[nh : 2 * nh]),
+        stack(*across, above[2 * nh :]),
+    )
+    got_x, got_y, below, above = third
+    fourth = all_ways(got_y[n : n + nh], got_x[n + nh :], below[:mh], above[mh:m])
     runs = [
         (0, 0, 0, 0, 3, span, 0),
-        (2, 0, 1, 0, 4, m, n),
-        (2, 4 * m, 3, 0, 4, m, n),
-        (3, 0, 2, 0, 1, n, 0),
-        (4, 2 * nh, 2, 0, 4, m, n),
+        (0, 3 * span, 3, 0, 1, n, 0),
+        (0, 3 * span + n, 1, 0, 1, n, 0),
     ]
+    offset = 0
     for side in range(2):
         runs += [
-            (0, 3 * span + side * (nh + mh), 0, 3, 1, nh, side * nh),
-            (0, 3 * span + side * (nh + mh) + nh, 0, 3, 1, mh, n + side * mh),
-            (3, n + side * 2 * n, 3, 3, 1, nh, side * nh),
-            (3, n + side * 2 * n + nh, 1, 3, 1, nh, side * nh),
-            (3, n + side * 2 * n + n, 2, 1 + side, 1, n, 0),
-            (4, side * nh, 2, 3, 1, nh, side * nh),
+            (1, offset, 0, 3, 1, nh, side * nh),
+            (1, offset + nh, 0, 3, 1, mh, n + side * mh),
+            (1, offset + start, 3, 1 + side, 1, n, 0),
+            (1, offset + start + n, 1, 1 + side, 1, n, 0),
         ]
-    for member in range(3):
-        runs += [(1, member * 2 * n, 3, member, 1, n, 0), (1, member * 2 * n + n, 1, member, 1, n, 0)]
-    return parts, tuple(runs), matrix, others
-
-
-ORDER = (((2, 0, 4), (1, 3, 1)), ((1, 0, 3), (3, 0, 4), (0, 0, 4)))
+        offset += start + 2 * n
+    for side in range(2):
+        runs += [
+            (1, offset, 2, 0, 1, nh, side * nh),
+            (1, offset + nh, 3 - 2 * side, 0, 3, m, n),
+        ]
+        offset += nh + 3 * m
+    offset = 0
+    for side in range(2):
+        runs += [
+            (2, offset, 3, 3, 1, nh, side * nh),
+            (2, offset + nh, 1, 3, 1, nh, side * nh),
+            (2, offset + n, 2, 1 + side, 1, n, 0),
+        ]
+        offset += 2 * n
+    runs += [
+        (2, offset, 3, 3, 1, m, n),
+        (2, offset + m, 2, 0, 1, m, n),
+        (2, offset + 2 * m, 2, 1, 1, mh, n),
+        (2, offset + 2 * m + mh, 1, 3, 1, m, n),
+        (2, offset + 3 * m + mh, 2, 1, 1, mh, n + mh),
+        (2, offset + 3 * m + 2 * mh, 2, 2, 1, m, n),
+        (3, 0, 2, 3, 1, nh, 0),
+        (3, nh, 2, 3, 1, nh, nh),
+        (3, n, 2, 3, 1, mh, n),
+        (3, n + mh, 2, 3, 1, mh, n + mh),
+    ]
+    return [stack(*part) for part in (first, second, third, fourth)], tuple(runs), prepared
+
+
+ORDER = (((2, 0, 4), (1, 3, 1), (3, 3, 1)), ((1, 0, 3), (3, 0, 3), (0, 0, 4)))
 
 
 def scatter_sum(early, later, matrix, hyena):
-    span = later.shape[0] // 11
+    span = early.shape[0] // 6
     columns = matrix.shape[1]
     wide, narrow = columns * 3 // 8, columns // 8
-
-    def product(part):
-        both = beside(part, swapped(part))
+    blocks = {}
+
+    def product(part, other):
+        both = beside(part, other)
         return narrowed(jnp.dot(both, matrix, preferred_element_type=jnp.float32))
-
-    blocks = {}
 
     def keep(value, pieces):
         start = 0
@@ -436,104 +466,118 @@
                 blocks[group, member] = value[start : start + span]
                 start += span
 
-    early = product(early)
-    keep(early, ORDER[0])
-
     def term(group, member, side):
         return blocks[group, member][:, side * wide : (side + 1) * wide]
 
-    def low(group, side):
+    def low(group, member, side):
         first = 2 * wide + side * narrow
-        return stack(*[blocks[group, m][:, first : first + narrow] for m in range(PLANE)])
+        return blocks[group, member][:, first : first + narrow]
 
     def total(*parts):
         return sum(widened(part) for part in parts)
 
-    def to_x(group, across):
-        return term(group, 1, 0), narrowed(total(term(group, 1, 1), across))
-
-    def to_y(group, across):
-        return narrowed(total(term(group, 2, 0), across)), term(group, 2, 1)
-
-    def kept(group, got_x, got_y):
-        return [
-            total(
-                term(group, 0, side),
-                got_x[:, side * wide : (side + 1) * wide],
-                got_y[:, side * wide : (side + 1) * wide],
-            )
-            for side in (0, 1)
-        ]
-
-    got_x, got_y = over_plane(
-        beside(term(2, 3, 0), term(1, 3, 0)), beside(term(2, 3, 1), term(1, 3, 1))
-    )
-    low_up, low_down = over_depth(low(2, 0), low(2, 1))
-    later, early = lax.optimization_barrier((later, early))
-    later, hyena, got_x, got_y = lax.optimization_barrier((product(later), hyena, got_x, got_y))
+    def added(*parts):
+        return narrowed(total(*parts))
+
+    def cut(value, *widths):
+        parts, start = [], 0
+        for width in widths:
+            parts.append(value[:, start : start + width])
+            start += width
+        return parts
+
+    early = product(early, swapped(early))
+    keep(early, ORDER[0])
+    other = swapped(later)
+    across_y, across_x, from_below, from_above = all_ways(
+        term(2, 3, 0), term(2, 3, 1), low(2, 3, 0), low(2, 3, 1)
+    )
+    later, across_x = lax.optimization_barrier((later, across_x))
+    got_x, got_y, below, above = all_ways(
+        beside(term(2, 1, 0), added(term(2, 1, 1), across_x), term(1, 3, 0), term(3, 3, 0)),
+        beside(added(term(2, 2, 0), across_y), term(2, 2, 1), term(1, 3, 1), term(3, 3, 1)),
+        beside(
+            added(low(1, 3, 0), from_below), low(1, 3, 1), *[low(2, k, 0) for k in range(3)]
+        ),
+        beside(
+            low(3, 3, 0), added(low(3, 3, 1), from_above), *[low(2, k, 1) for k in range(3)]
+        ),
+    )
+    later = product(later, other)
+    later, hyena, got_x = lax.optimization_barrier((later, hyena, got_x))
     keep(later, ORDER[1])
     hyena_out = lax.all_to_all(hyena, "ctx", split_axis=0, concat_axis=1, tiled=True).T
-    got_x, got_y = over_plane(
-        beside(*to_x(2, got_y[:, :wide]), *to_x(1, got_y[:, wide:]), term(3, 3, 0)),
-        beside(*to_y(2, got_x[:, :wide]), *to_y(1, got_x[:, wide:]), term(3, 3, 1)),
-    )
-    low_up, low_down = over_depth(
-        beside(narrowed(total(low(1, 0), low_up)), low(1, 1)),
-        beside(low(3, 0), narrowed(total(low(3, 1), low_down))),
-    )
-    sum_2 = kept(2, got_x[:, : 2 * wide], got_y[:, : 2 * wide])
-    sum_1 = kept(1, got_x[:, 2 * wide : 4 * wide], got_y[:, 2 * wide : 4 * wide])
-    sum_2, low_up, low_down = lax.optimization_barrier((sum_2, low_up, low_down))
-    wide_up, wide_down = over_depth(narrowed(sum_2[0]), narrowed(sum_2[1]))
-    got_x, got_y = over_plane(
-        beside(*to_x(3, got_y[:, 4 * wide :]), term(0, 3, 0)),
-        beside(*to_y(3, got_x[:, 4 * wide :]), term(0, 3, 1)),
-    )
-    got_x, got_y, wide_up, wide_down = lax.optimization_barrier((got_x, got_y, wide_up, wide_down))
-    sum_3 = kept(3, got_x[:, : 2 * wide], got_y[:, : 2 * wide])
-    wide_up, wide_down = over_depth(
-        beside(narrowed(total(sum_1[0], wide_up)), narrowed(sum_1[1])),
-        beside(narrowed(sum_3[0]), narrowed(total(sum_3[1], wide_down))),
-    )
-    low_sum = [
-        total(
-            low(0, side),
-            low_up[:, side * narrow : (side + 1) * narrow],
-            low_down[:, side * narrow : (side + 1) * narrow],
-        )
-        for side in (0, 1)
+    *own_x, across_1y, across_3y = cut(got_x, *[wide] * 4)
+    *own_y, across_1x, across_3x = cut(got_y, *[wide] * 4)
+    below_0, below_1, *from_below = cut(below, *[narrow] * 5)
+    above_0, above_1, *from_above = cut(above, *[narrow] * 5)
+    sum_2 = [added(term(2, 0, side), own_x[side], own_y[side]) for side in (0, 1)]
+    low_3 = [added(low(0, 3, 0), below_0, above_0), added(low(0, 3, 1), below_1, above_1)]
+    for_above, for_below = [], []
+    for k in range(3):
+        for_above += [added(low(1, k, 0), from_below[k]), low(1, k, 1)]
+        for_below += [low(3, k, 0), added(low(3, k, 1), from_above[k])]
+    got_x, got_y, below, above = all_ways(
+        beside(
+            term(1, 1, 0),
+            added(term(1, 1, 1), across_1x),
+            term(3, 1, 0),
+            added(term(3, 1, 1), across_3x),
+            term(0, 3, 0),
+            low_3[0],
+        ),
+        beside(
+            added(term(1, 2, 0), across_1y),
+            term(1, 2, 1),
+            added(term(3, 2, 0), across_3y),
+            term(3, 2, 1),
+            term(0, 3, 1),
+            low_3[1],
+        ),
+        beside(sum_2[0], *for_above),
+        beside(sum_2[1], *for_below),
+    )
+    *own_x, across_y, low_across_y = cut(got_x, *[wide] * 5, narrow)
+    *own_y, across_x, low_across_x = cut(got_y, *[wide] * 5, narrow)
+    from_below, *low_below = cut(below, wide, *[narrow] * 6)
+    from_above, *low_above = cut(above, wide, *[narrow] * 6)
+    low_own = [
+        [total(low(0, k, side), low_below[2 * k + side], low_above[2 * k + side]) for side in (0, 1)]
+        for k in range(3)
     ]
-
-    def low_term(member, side):
-        return low_sum[side][member * span : (member + 1) * span]
-
-    got_x, got_y = over_plane(
-        beside(*to_x(0, got_y[:, 2 * wide :]), narrowed(low_term(3, 0))),
-        beside(*to_y(0, got_x[:, 2 * wide :]), narrowed(low_term(3, 1))),
-    )
-    sum_0 = kept(0, got_x[:, : 2 * wide], got_y[:, : 2 * wide])
-    across_y, across_x = got_x[:, 2 * wide :], got_y[:, 2 * wide :]
-    low_x, low_y = over_plane(
-        beside(narrowed(low_term(1, 0)), narrowed(total(low_term(1, 1), across_x))),
-        beside(narrowed(total(low_term(2, 0), across_y)), narrowed(low_term(2, 1))),
-    )
-    outs = [
-        total(
-            sum_0[side],
-            wide_up[:, side * wide : (side + 1) * wide],
-            wide_down[:, side * wide : (side + 1) * wide],
-        )
-        for side in (0, 1)
-    ]
-    outs += [
-        total(
-            low_term(0, side),
-            low_x[:, side * narrow : (side + 1) * narrow],
-            low_y[:, side * narrow : (side + 1) * narrow],
-        )
-        for side in (0, 1)
-    ]
-    return beside(*[narrowed(part) for part in outs]), hyena_out
+    got_x, got_y, below, above = all_ways(
+        beside(
+            term(0, 1, 0),
+            added(term(0, 1, 1), across_x),
+            narrowed(low_own[1][0]),
+            added(low_own[1][1], low_across_x),
+        ),
+        beside(
+            added(term(0, 2, 0), across_y),
+            term(0, 2, 1),
+            added(low_own[2][0], low_across_y),
+            narrowed(low_own[2][1]),
+        ),
+        beside(
+            added(term(1, 0, 0), own_x[0], own_y[0], from_below),
+            added(term(1, 0, 1), own_x[1], own_y[1]),
+        ),
+        beside(
+            added(term(3, 0, 0), own_x[2], own_y[2]),
+            added(term(3, 0, 1), own_x[3], own_y[3], from_above),
+        ),
+    )
+    return (
+        beside(
+            added(
+                blocks[0, 0][:, : 2 * wide], got_x[:, : 2 * wide], got_y[:, : 2 * wide], below, above
+            ),
+            added(
+                beside(*low_own[0]), got_x[:, 2 * wide :], got_y[:, 2 * wide :]
+            ),
+        ),
+        hyena_out,
+    )
 
 
 def gather_tokens(tokens, weights, residues, decay_rates, cotangent):
@@ -545,15 +589,17 @@
     kept = lax.dynamic_slice_in_dim(rows, core * half, half, 1)
     taken = swapped(lax.dynamic_slice_in_dim(rows, (1 - core) * half, half, 1))
     cot_cols = lax.all_to_all(cotangent.T, "ctx", split_axis=1, concat_axis=0, tiled=True)
-    parts, runs, matrix, cot_cols = gather_groups(
-        lax.dynamic_slice_in_dim(tokens, core * half, half, 1), stack(taken, kept), cot_cols
-    )
-    both = [
-        jnp.einsum("td,rd->tr", part, matrix, preferred_element_type=jnp.float32) for part in parts
-    ]
-    other = [swapped(narrowed(part[:, : 3 * channels])) for part in both]
+    parts, runs, (kept, taken, cot_cols) = gather_groups(
+        lax.dynamic_slice_in_dim(tokens, core * half, half, 1), (kept, taken, cot_cols)
+    )
+
+    def project(part, matrix):
+        return jnp.einsum("td,rd->tr", part, matrix, preferred_element_type=jnp.float32)
+
+    other = [swapped(narrowed(project(part, taken))) for part in parts]
+    own = [project(part, kept) for part in parts]
     hyena, grads, (early, later) = scan_all(
-        me, cot_cols, residues[0].T, decay_rates[0].T, runs, ORDER, both, other
+        me, cot_cols, residues[0].T, decay_rates[0].T, runs, ORDER, own, other
     )
     grad_input, hyena_out = scatter_sum(early, later, stack(kept, taken), hyena)
     return (hyena_out, grad_input, grads.T[None])

time: 266 us -> 238 us (0.89)
  starting transfers between devices: 70.3 us -> 56.8 us
  other arithmetic: 24.7 us -> 14.8 us
  local copies, waits for them, and re-layouts: 29.7 us -> 22.7 us
    ppermute x10 -> x8, waiting for transfers between devices: 18.2 us -> 4.79 us  [over_x(): lax.ppermute(value, 'ctx', [(i, i ^ 1) for i in range(lax.axis_size('ctx'...]
    ppermute x8, waiting for transfers between devices: 38.9 us -> 49.1 us  [up(): lax.ppermute(value, 'ctx', [(i, (i + PLANE) % count) for i in range(count)])]
    ppermute x8, starting transfers between devices: 16.5 us -> 7.85 us  [up(): lax.ppermute(value, 'ctx', [(i, (i + PLANE) % count) for i in range(count)])]
    unnamed x72 -> x39, local copies, waits for them, and re-layouts: 14 us -> 6.55 us
    ppermute x10 -> x8, starting transfers between devices: 14.6 us -> 8.47 us  [over_y(): lax.ppermute(value, 'ctx', [(i, i ^ 2) for i in range(lax.axis_size('ctx'...]
    concatenate x6 -> x4, other arithmetic: 6.42 us -> 0.64 us  [stack(): return jnp.concatenate(parts, axis=0)]
    all_to_all x1, starting transfers between devices: 3.57 us -> 7.87 us  [gather_tokens(): lax.all_to_all(cotangent.T, 'ctx', split_axis=1, concat_axis=0, tiled=True)]
    slice x19 -> x16, local copies, waits for them, and re-layouts: 8.06 us -> 4.24 us  [the longest x3 1.75 us: gather_groups(): wide, narrow = (tokens[:n], tokens[n:])]
  transfers between devices with their start and end apart: 46 -> 41, of which waited for: 24 -> 20; matrix products, arithmetic and copies ran while one was open for 19% -> 16% of each run, Pallas kernels for 0% -> 0%
where the time goes in v1:
time: 238 us; the launch traced here: 237 us
  waiting for transfers between devices  103 us (43%)
  starting transfers between devices  56.8 us (24%)
  matrix products  23.5 us (10%)
  local copies, waits for them, and re-layouts  22.7 us (10%)
  Pallas kernels  14.9 us (6%)
  other arithmetic  14.8 us (6%)
    ppermute x8, waiting for transfers between devices, up(): lax.ppermute(value, 'ctx', [(i, (i + PLANE) % count) for i in range(count)])  49.1 us
    ppermute x8, waiting for transfers between devices, down(): lax.ppermute(value, 'ctx', [((i + PLANE) % count, i) for i in range(count)])  39.6 us
    ppermute x8, starting transfers between devices, down(): lax.ppermute(value, 'ctx', [((i + PLANE) % count, i) for i in range(count)])  17 us
    dot_general x8, matrix products, project(): jnp.einsum('td,rd->tr', part, matrix, preferred_element_type=jnp.float32)  16.1 us
    pallas_call x1, Pallas kernels, scan_all(): pl.pallas_call(functools.partial(scan_kernel, PLANE, runs, order), out_sh...  14.9 us
    ppermute x8, starting transfers between devices, over_x(): lax.ppermute(value, 'ctx', [(i, i ^ 1) for i in range(lax.axis_size('ctx'...  10.6 us
    ppermute x8, starting transfers between devices, over_y(): lax.ppermute(value, 'ctx', [(i, i ^ 2) for i in range(lax.axis_size('ctx'...  8.47 us
    all_to_all x1, starting transfers between devices, gather_tokens(): lax.all_to_all(cotangent.T, 'ctx', split_axis=1, concat_axis=0, tiled=True)  7.87 us
  transfers between devices with their start and end apart: 41, of which 20 were waited for; matrix products, arithmetic and copies ran while one was open for 16% of the time, Pallas kernels for 0%

profile of v1, /device:TPU:0, one launch (start us, length us, event | category | flops | bytes accessed | tf_op | source)
XLA Modules:
  0.0 237.1 jit_solution(9682136721600393896)
XLA Ops:
  0.6 3.5 %constant_dynamic-slice_fusion.1 = (bf16[384,2048]{1,0:T(8,128)(2,1)}, bf16[384,2048]{1,0:T(8,128)(2,1)S(1)}) fusion(bf16[384,4096]{1,0:T(8,128)(2,1)} %bitcast.47, s32[]{:T(128)S(6)} %select_n.8, s32[]{:T(128)} %select_n.7), kind=kLoop, calls=%fused_computation.126 | loop fusion | bytes 6291464 | tf_op jit(solution)/shard_map/dynamic_slice | solution.py:590
  5.6 7.9 %all-to-all-start = ((bf16[128,16,128]{2,0,1:T(8,128)(2,1)}), bf16[128,16,128]{2,0,1:T(8,128)(2,1)S(1)}, u32[]{:S(2)}, u32[]{:S(2)}) async-start(bf16[128,16,128]{2,0,1:T(8,128)(2,1)} %copy.8), calls=%async_computation | async-start | bytes 1048576 | tf_op jit(solution)/shard_map/all_to_all | solution.py:591
  14.6 1.9 collective-permute-start.1
  16.5 1.5 collective-permute-start
  18.0 1.8 constant_dynamic-slice_fusion
  19.7 3.3 %collective-permute-start.3 = (bf16[96,2048]{1,0:T(8,128)(2,1)}, bf16[96,2048]{1,0:T(8,128)(2,1)S(1)}, u32[]{:S(2)}, u32[]{:S(2)}) collective-permute-start(bf16[96,2048]{1,0:T(8,128)(2,1)} %constant_dynamic-slice_fusion), channel_id=1, source_target_pairs={{8,0},{10,2},{12,4},{14,6},{16,8},{18,10},{20,12},{22,14},{24,16},... | collective-permute-start | bytes 1179656 | tf_op jit(solution)/shard_map/ppermute | solution.py:356
  23.0 10.2 %collective-permute-done.3 = bf16[96,2048]{1,0:T(8,128)(2,1)S(1)} collective-permute-done((bf16[96,2048]{1,0:T(8,128)(2,1)}, bf16[96,2048]{1,0:T(8,128)(2,1)S(1)}, u32[]{:S(2)}, u32[]{:S(2)}) %collective-permute-start.3) | collective-permute-done | bytes 393248 | tf_op jit(solution)/shard_map/ppermute | solution.py:356
  33.2 10.4 %collective-permute-done.2 = bf16[96,2048]{1,0:T(8,128)(2,1)S(1)} collective-permute-done((bf16[96,2048]{1,0:T(8,128)(2,1)}, bf16[96,2048]{1,0:T(8,128)(2,1)S(1)}, u32[]{:S(2)}, u32[]{:S(2)}) %collective-permute-start.2) | collective-permute-done | bytes 393248 | tf_op jit(solution)/shard_map/ppermute | solution.py:351
  49.1 1.9 constant_dynamic-update-slice_fusion.3
  52.1 1.5 collective-permute-start.6
  53.6 1.5 collective-permute-start.5
  55.7 2.0 collective-permute-start.7
  57.8 2.8 %convolution_convert_fusion.3 = bf16[576,384]{1,0:T(8,128)(2,1)S(1)} fusion(bf16[576,2048]{1,0:T(8,128)(2,1)S(1)} %constant_dynamic-update-slice_fusion, bf16[384,2048]{1,0:T(8,128)(2,1)} %collective-permute-done.4), kind=kOutput, calls=%fused_computation.6 | convolution fusion | flops 906190848 | bytes 4374528 | tf_op jit(solution)/shard_map/td,rd->tr/dot_general | solution.py:597
  60.6 1.4 fusion.23.refs_1_
  62.1 8.4 %collective-permute-done.8 = bf16[144,2048]{1,0:T(8,128)(2,1)S(1)} collective-permute-done((bf16[144,2048]{1,0:T(8,128)(2,1)S(1)}, bf16[144,2048]{1,0:T(8,128)(2,1)S(1)}, u32[]{:S(2)}, u32[]{:S(2)}) %collective-permute-start.8) | collective-permute-done | bytes 589856 | tf_op jit(solution)/shard_map/ppermute | solution.py:356
  70.4 13.7 %collective-permute-done.7 = bf16[144,2048]{1,0:T(8,128)(2,1)S(1)} collective-permute-done((bf16[144,2048]{1,0:T(8,128)(2,1)S(1)}, bf16[144,2048]{1,0:T(8,128)(2,1)S(1)}, u32[]{:S(2)}, u32[]{:S(2)}) %collective-permute-start.7) | collective-permute-done | bytes 589856 | tf_op jit(solution)/shard_map/ppermute | solution.py:351
  87.2 1.4 collective-permute-start.9
  88.8 3.3 %convolution_convert_fusion.2 = bf16[800,384]{1,0:T(8,128)(2,1)S(1)} fusion(bf16[800,2048]{1,0:T(8,128)(2,1)S(1)} %constant_dynamic-update-slice_fusion.5, bf16[384,2048]{1,0:T(8,128)(2,1)} %collective-permute-done.4), kind=kOutput, calls=%fused_computation.5 | convolution fusion | flops 1258598400 | bytes 5464064 | tf_op jit(solution)/shard_map/td,rd->tr/dot_general | solution.py:597
  92.1 1.9 fusion.24.refs_2_
  94.0 6.4 %collective-permute-done.11 = bf16[80,2048]{1,0:T(8,128)(2,1)S(1)} collective-permute-done((bf16[80,2048]{1,0:T(8,128)(2,1)S(1)}, bf16[80,2048]{1,0:T(8,128)(2,1)S(1)}, u32[]{:S(2)}, u32[]{:S(2)}) %collective-permute-start.11) | collective-permute-done | bytes 327712 | tf_op jit(solution)/shard_map/ppermute | solution.py:351
  100.4 4.2 %collective-permute-done.10 = bf16[192,2048]{1,0:T(8,128)(2,1)S(1)} collective-permute-done((bf16[192,2048]{1,0:T(8,128)(2,1)S(1)}, bf16[192,2048]{1,0:T(8,128)(2,1)S(1)}, u32[]{:S(2)}, u32[]{:S(2)}) %collective-permute-start.10) | collective-permute-done | bytes 786464 | tf_op jit(solution)/shard_map/ppermute | solution.py:346
  105.0 3.6 %collective-permute-start.16 = (bf16[16,2048]{1,0:T(8,128)(2,1)S(1)}, bf16[16,2048]{1,0:T(8,128)(2,1)S(1)}, u32[]{:S(2)}, u32[]{:S(2)}) collective-permute-start(bf16[16,2048]{1,0:T(8,128)(2,1)S(1)} %slice.507), channel_id=1, source_target_pairs={{8,0},{10,2},{12,4},{14,6},{16,8},{18,10},{20,12},{22,14},{24,16},... | collective-permute-start | bytes 196616 | tf_op jit(solution)/shard_map/ppermute | solution.py:356
  108.6 1.8 collective-permute-start.13
  110.9 2.7 %convolution_convert_fusion.4 = bf16[544,384]{1,0:T(8,128)(2,1)S(1)} fusion(bf16[544,2048]{1,0:T(8,128)(2,1)S(1)} %constant_dynamic-update-slice_fusion.9, bf16[384,2048]{1,0:T(8,128)(2,1)} %collective-permute-done.4), kind=kOutput, calls=%fused_computation.7 | convolution fusion | flops 855846912 | bytes 4218880 | tf_op jit(solution)/shard_map/td,rd->tr/dot_general | solution.py:597
  116.2 2.0 convolution_convert_fusion.5
  119.6 14.9 %modal_scan.1 = (bf16[2048,128]{1,0:T(8,128)(2,1)}, f32[16,128]{1,0:T(8,128)}, bf16[768,384]{1,0:T(8,128)(2,1)S(1)}, bf16[1280,384]{1,0:T(8,128)(2,1)S(1)}) custom-call(s32[1]{0:T(128)} %bitcast.me_ref, f32[16,128]{1,0:T(8,128)S(1)} %bitcast.45, f32[16,128]{1,0:T(8,128)S(1)} %bitcast.46, bf16[2048,128]{1,0:T(8,128)(2,1)S(1)} %bitcast.44, ...), custom_call_target="tpu_custom_call" | custom-call | tf_op jit(solution)/shard_map/modal_scan/pallas_call | solution.py:315
  134.8 1.5 constant_dynamic-update-slice_fusion.17
  136.6 2.9 %convolution_convert_fusion.1 = bf16[768,2048]{1,0:T(8,128)(2,1)S(1)} fusion(bf16[768,2048]{1,0:T(8,128)(2,1)S(1)} %constant_dynamic-update-slice_fusion.17, bf16[768,384]{1,0:T(8,128)(2,1)S(1)} %collective-permute-done.21, bf16[768,384]{1,0:T(8,128)(2,1)S(1)} %get-tuple-element.69), kind=kOutput, calls=%fused_computation.1 | convolution fusion | flops 2419851264 | bytes 7471104 | tf_op jit(solution)/shard_map/dot_general | solution.py:460
  141.5 3.9 %collective-permute-start.25 = (bf16[128,256]{1,0:T(8,128)(2,1)S(1)}, bf16[128,256]{1,0:T(8,128)(2,1)S(1)}, u32[]{:S(2)}, u32[]{:S(2)}) collective-permute-start(bf16[128,256]{1,0:T(8,128)(2,1)S(1)} %get-tuple-element.152), channel_id=1, source_target_pairs={{8,0},{10,2},{12,4},{14,6},{16,8},{18,10},{20,12},{22,14},{24,16},... | collective-permute-start | bytes 196616 | tf_op jit(solution)/shard_map/ppermute | solution.py:356
  145.4 1.9 collective-permute-done.25
  147.3 4.2 %collective-permute-done.24 = bf16[128,256]{1,0:T(8,128)(2,1)S(1)} collective-permute-done((bf16[128,256]{1,0:T(8,128)(2,1)S(1)}, bf16[128,256]{1,0:T(8,128)(2,1)S(1)}, u32[]{:S(2)}, u32[]{:S(2)}) %collective-permute-start.24) | collective-permute-done | bytes 65568 | tf_op jit(solution)/shard_map/ppermute | solution.py:351
  151.7 2.0 collective-permute-start.29
  153.9 1.8 collective-permute-start.27
  156.7 4.5 %convolution_convert_fusion = bf16[1280,2048]{1,0:T(8,128)(2,1)S(1)} fusion(bf16[768,2048]{1,0:T(8,128)(2,1)S(1)} %constant_dynamic-update-slice_fusion.17, bf16[1280,384]{1,0:T(8,128)(2,1)S(1)} %collective-permute-done.26, bf16[1280,384]{1,0:T(8,128)(2,1)S(1)} %get-tuple-element.71), kind=kOutput, calls=%fused_computation | convolution fusion | flops 4033085440 | bytes 10354688 | tf_op jit(solution)/shard_map/dot_general | solution.py:460
  161.2 5.2 %collective-permute-done.30 = bf16[128,1280]{1,0:T(8,128)(2,1)S(1)} collective-permute-done((bf16[128,1280]{1,0:T(8,128)(2,1)S(1)}, bf16[128,1280]{1,0:T(8,128)(2,1)S(1)}, u32[]{:S(2)}, u32[]{:S(2)}) %collective-permute-start.30) | collective-permute-done | bytes 327712 | tf_op jit(solution)/shard_map/ppermute | solution.py:356
  166.4 4.5 %collective-permute-done.27 = bf16[128,3072]{1,0:T(8,128)(2,1)S(1)} collective-permute-done((bf16[128,3072]{1,0:T(8,128)(2,1)S(1)}, bf16[128,3072]{1,0:T(8,128)(2,1)S(1)}, u32[]{:S(2)}, u32[]{:S(2)}) %collective-permute-start.27) | collective-permute-done | bytes 786464 | tf_op jit(solution)/shard_map/ppermute | solution.py:342
  183.6 3.5 %collective-permute-start.34 = (bf16[128,2304]{1,0:T(8,128)(2,1)}, bf16[128,2304]{1,0:T(8,128)(2,1)}, u32[]{:S(2)}, u32[]{:S(2)}) collective-permute-start(bf16[128,2304]{1,0:T(8,128)(2,1)} %get-tuple-element.108), channel_id=1, source_target_pairs={{8,0},{10,2},{12,4},{14,6},{16,8},{18,10},{20,12},{22,14},{24,16},... | collective-permute-start | bytes 1769480 | tf_op jit(solution)/shard_map/ppermute | solution.py:356
  187.1 3.6 %all-to-all-start.1 = ((bf16[16,128,128]{2,1,0:T(8,128)(2,1)}), bf16[16,128,128]{2,1,0:T(8,128)(2,1)S(1)}, u32[]{:S(2)}, u32[]{:S(2)}) async-start(bf16[16,128,128]{2,1,0:T(8,128)(2,1)} %bitcast.14), calls=%async_computation.1 | async-start | bytes 1048576 | tf_op jit(solution)/shard_map/all_to_all | solution.py:509
  190.7 11.0 %collective-permute-done.33 = bf16[128,2304]{1,0:T(8,128)(2,1)} collective-permute-done((bf16[128,2304]{1,0:T(8,128)(2,1)}, bf16[128,2304]{1,0:T(8,128)(2,1)}, u32[]{:S(2)}, u32[]{:S(2)}) %collective-permute-start.33) | collective-permute-done | bytes 589856 | tf_op jit(solution)/shard_map/ppermute | solution.py:351
  201.7 8.4 %collective-permute-done.34 = bf16[128,2304]{1,0:T(8,128)(2,1)} collective-permute-done((bf16[128,2304]{1,0:T(8,128)(2,1)}, bf16[128,2304]{1,0:T(8,128)(2,1)}, u32[]{:S(2)}, u32[]{:S(2)}) %collective-permute-start.34) | collective-permute-done | bytes 589856 | tf_op jit(solution)/shard_map/ppermute | solution.py:356
  211.0 1.4 add_convert_fusion.16
  212.4 1.9 add_convert_fusion.2
  215.1 2.2 collective-permute-start.37
  220.5 1.5 collective-permute-start.38
  222.0 2.8 %all-to-all-done.1 = bf16[16,128,128]{2,1,0:T(8,128)(2,1)S(1)} async-done(((bf16[16,128,128]{2,1,0:T(8,128)(2,1)}), bf16[16,128,128]{2,1,0:T(8,128)(2,1)S(1)}, u32[]{:S(2)}, u32[]{:S(2)}) %all-to-all-start.1) | async-done | bytes 524320 | tf_op jit(solution)/shard_map/all_to_all | solution.py:509
  225.8 3.4 %collective-permute-done.37 = bf16[128,1536]{1,0:T(8,128)(2,1)} collective-permute-done((bf16[128,1536]{1,0:T(8,128)(2,1)}, bf16[128,1536]{1,0:T(8,128)(2,1)}, u32[]{:S(2)}, u32[]{:S(2)}) %collective-permute-start.37) | collective-permute-done | bytes 393248 | tf_op jit(solution)/shard_map/ppermute | solution.py:351
  229.2 5.5 %collective-permute-done.38 = bf16[128,1536]{1,0:T(8,128)(2,1)S(1)} collective-permute-done((bf16[128,1536]{1,0:T(8,128)(2,1)}, bf16[128,1536]{1,0:T(8,128)(2,1)S(1)}, u32[]{:S(2)}, u32[]{:S(2)}) %collective-permute-start.38) | collective-permute-done | bytes 393248 | tf_op jit(solution)/shard_map/ppermute | solution.py:356
  234.8 1.4 add_convert_fusion
  (142 shorter events, 41.0 us)
Async XLA Ops:
  4.1 9.3 %copy-start.3 = (bf16[128,4096]{1,0:T(8,128)(2,1)S(1)}, bf16[128,4096]{1,0:T(8,128)(2,1)}, u32[]{:S(2)}) copy-start(bf16[128,4096]{1,0:T(8,128)(2,1)} %param.5) | copy-start | bytes 3145732
  4.1 42.2 %collective-permute-start.4 = (bf16[384,2048]{1,0:T(8,128)(2,1)}, bf16[384,2048]{1,0:T(8,128)(2,1)}, u32[]{:S(2)}, u32[]{:S(2)}) collective-permute-start(bf16[384,2048]{1,0:T(8,128)(2,1)} %get-tuple-element.154), channel_id=1, source_target_pairs={{0,1},{1,0},{2,3},{3,2},{4,5},{5,4},{6,7},{7,6},{8,9},{9,8},{10,11... | collective-permute-start | bytes 4718600 | tf_op jit(solution)/shard_map/ppermute | solution.py:338
  5.6 40.7 %all-to-all-start = ((bf16[128,16,128]{2,0,1:T(8,128)(2,1)}), bf16[128,16,128]{2,0,1:T(8,128)(2,1)S(1)}, u32[]{:S(2)}, u32[]{:S(2)}) async-start(bf16[128,16,128]{2,0,1:T(8,128)(2,1)} %copy.8), calls=%async_computation | async-start | bytes 1048576 | tf_op jit(solution)/shard_map/all_to_all | solution.py:591
  14.6 29.0 %collective-permute-start.1 = (bf16[128,2048]{1,0:T(8,128)(2,1)}, bf16[128,2048]{1,0:T(8,128)(2,1)S(1)}, u32[]{:S(2)}, u32[]{:S(2)}) collective-permute-start(bf16[128,2048]{1,0:T(8,128)(2,1)} %get-tuple-element.94), channel_id=1, source_target_pairs={{0,4},{2,6},{4,0},{6,2},{8,12},{10,14},{12,8},{14,10},{16,20},{18,... | collective-permute-start | bytes 1572872 | tf_op jit(solution)/shard_map/ppermute | solution.py:346
  16.5 27.1 %collective-permute-start = (bf16[128,2048]{1,0:T(8,128)(2,1)}, bf16[128,2048]{1,0:T(8,128)(2,1)}, u32[]{:S(2)}, u32[]{:S(2)}) collective-permute-start(bf16[128,2048]{1,0:T(8,128)(2,1)} %get-tuple-element.94), channel_id=1, source_target_pairs={{0,2},{2,0},{4,6},{6,4},{8,10},{10,8},{12,14},{14,12},{16,18},{18,... | collective-permute-start | bytes 1572872 | tf_op jit(solution)/shard_map/ppermute | solution.py:342
  19.7 13.5 %collective-permute-start.3 = (bf16[96,2048]{1,0:T(8,128)(2,1)}, bf16[96,2048]{1,0:T(8,128)(2,1)S(1)}, u32[]{:S(2)}, u32[]{:S(2)}) collective-permute-start(bf16[96,2048]{1,0:T(8,128)(2,1)} %constant_dynamic-slice_fusion), channel_id=1, source_target_pairs={{8,0},{10,2},{12,4},{14,6},{16,8},{18,10},{20,12},{22,14},{24,16},... | collective-permute-start | bytes 1179656 | tf_op jit(solution)/shard_map/ppermute | solution.py:356
  23.0 20.6 %collective-permute-start.2 = (bf16[96,2048]{1,0:T(8,128)(2,1)}, bf16[96,2048]{1,0:T(8,128)(2,1)S(1)}, u32[]{:S(2)}, u32[]{:S(2)}) collective-permute-start(bf16[96,2048]{1,0:T(8,128)(2,1)} %constant_dynamic-slice_fusion), channel_id=1, source_target_pairs={{0,8},{2,10},{4,12},{6,14},{8,16},{10,18},{12,20},{14,22},{16,24},... | collective-permute-start | bytes 1179656 | tf_op jit(solution)/shard_map/ppermute | solution.py:351
  46.3 5.5 %copy-start.6 = (bf16[48,2048]{1,0:T(8,128)(2,1)S(1)}, bf16[48,2048]{1,0:T(8,128)(2,1)}, u32[]{:S(2)}) copy-start(bf16[48,2048]{1,0:T(8,128)(2,1)} %slice.485) | copy-start | bytes 589828
  46.3 5.5 %copy-start.8 = (bf16[16,2048]{1,0:T(8,128)(2,1)S(1)}, bf16[16,2048]{1,0:T(8,128)(2,1)}, u32[]{:S(2)}) copy-start(bf16[16,2048]{1,0:T(8,128)(2,1)} %slice.486) | copy-start | bytes 196612
  51.0 4.1 %dynamic-slice-start = ((bf16[128,4096]{1,0:T(8,128)(2,1)}, s32[]{:T(128)}, s32[]{:T(128)}), bf16[32,2048]{1,0:T(8,128)(2,1)S(1)}, s32[]{:S(2)}) async-start(bf16[128,4096]{1,0:T(8,128)(2,1)} %param.5, s32[]{:T(128)} %add.225, s32[]{:T(128)} %select_n.7), calls=%async_computation.2 | async-start | bytes 262656 | tf_op jit(solution)/shard_map/slice | solution.py:383
  51.0 4.1 %copy-start.4 = (bf16[48,2048]{1,0:T(8,128)(2,1)S(1)}, bf16[48,2048]{1,0:T(8,128)(2,1)}, u32[]{:S(2)}) copy-start(bf16[48,2048]{1,0:T(8,128)(2,1)} %slice.489) | copy-start | bytes 589828
  51.0 4.1 %copy-start.5 = (bf16[48,2048]{1,0:T(8,128)(2,1)S(1)}, bf16[48,2048]{1,0:T(8,128)(2,1)}, u32[]{:S(2)}) copy-start(bf16[48,2048]{1,0:T(8,128)(2,1)} %slice.493) | copy-start | bytes 589828
  52.1 32.0 %collective-permute-start.6 = (bf16[256,2048]{1,0:T(8,128)(2,1)S(1)}, bf16[256,2048]{1,0:T(8,128)(2,1)S(1)}, u32[]{:S(2)}, u32[]{:S(2)}) collective-permute-start(bf16[256,2048]{1,0:T(8,128)(2,1)S(1)} %get-tuple-element.162), channel_id=1, source_target_pairs={{0,4},{2,6},{4,0},{6,2},{8,12},{10,14},{12,8},{14,10},{16,20},{18,... | collective-permute-start | bytes 3145736 | tf_op jit(solution)/shard_map/ppermute | solution.py:346
  53.6 30.5 %collective-permute-start.5 = (bf16[256,2048]{1,0:T(8,128)(2,1)S(1)}, bf16[256,2048]{1,0:T(8,128)(2,1)S(1)}, u32[]{:S(2)}, u32[]{:S(2)}) collective-permute-start(bf16[256,2048]{1,0:T(8,128)(2,1)S(1)} %get-tuple-element.163), channel_id=1, source_target_pairs={{0,2},{2,0},{4,6},{6,4},{8,10},{10,8},{12,14},{14,12},{16,18},{18,... | collective-permute-start | bytes 3145736 | tf_op jit(solution)/shard_map/ppermute | solution.py:342
  55.3 15.1 %collective-permute-start.8 = (bf16[144,2048]{1,0:T(8,128)(2,1)S(1)}, bf16[144,2048]{1,0:T(8,128)(2,1)S(1)}, u32[]{:S(2)}, u32[]{:S(2)}) collective-permute-start(bf16[144,2048]{1,0:T(8,128)(2,1)S(1)} %get-tuple-element.170), channel_id=1, source_target_pairs={{8,0},{10,2},{12,4},{14,6},{16,8},{18,10},{20,12},{22,14},{24,16},... | collective-permute-start | bytes 1769480 | tf_op jit(solution)/shard_map/ppermute | solution.py:356
  55.7 28.4 %collective-permute-start.7 = (bf16[144,2048]{1,0:T(8,128)(2,1)S(1)}, bf16[144,2048]{1,0:T(8,128)(2,1)S(1)}, u32[]{:S(2)}, u32[]{:S(2)}) collective-permute-start(bf16[144,2048]{1,0:T(8,128)(2,1)S(1)} %get-tuple-element.171), channel_id=1, source_target_pairs={{0,8},{2,10},{4,12},{6,14},{8,16},{10,18},{12,20},{14,22},{16,24},... | collective-permute-start | bytes 1769480 | tf_op jit(solution)/shard_map/ppermute | solution.py:351
  60.6 58.3 %collective-permute-start.17 = (bf16[576,384]{1,0:T(8,128)(2,1)S(1)}, bf16[576,384]{1,0:T(8,128)(2,1)S(1)}, u32[]{:S(2)}, u32[]{:S(2)}) collective-permute-start(bf16[576,384]{1,0:T(8,128)(2,1)S(1)} %convolution_convert_fusion.3), channel_id=1, source_target_pairs={{0,1},{1,0},{2,3},{3,2},{4,5},{5,4},{6,7},{7,6},{8,9},{9,8},{10,11... | collective-permute-start | bytes 1327112 | tf_op jit(solution)/shard_map/ppermute | solution.py:338
  84.5 9.5 %collective-permute-start.12 = (bf16[80,2048]{1,0:T(8,128)(2,1)S(1)}, bf16[80,2048]{1,0:T(8,128)(2,1)S(1)}, u32[]{:S(2)}, u32[]{:S(2)}) collective-permute-start(bf16[80,2048]{1,0:T(8,128)(2,1)S(1)} %get-tuple-element.172), channel_id=1, source_target_pairs={{8,0},{10,2},{12,4},{14,6},{16,8},{18,10},{20,12},{22,14},{24,16},... | collective-permute-start | bytes 983048 | tf_op jit(solution)/shard_map/ppermute | solution.py:356
  85.2 15.2 %collective-permute-start.11 = (bf16[80,2048]{1,0:T(8,128)(2,1)S(1)}, bf16[80,2048]{1,0:T(8,128)(2,1)S(1)}, u32[]{:S(2)}, u32[]{:S(2)}) collective-permute-start(bf16[80,2048]{1,0:T(8,128)(2,1)S(1)} %get-tuple-element.173), channel_id=1, source_target_pairs={{0,8},{2,10},{4,12},{6,14},{8,16},{10,18},{12,20},{14,22},{16,24},... | collective-permute-start | bytes 983048 | tf_op jit(solution)/shard_map/ppermute | solution.py:351
  86.7 17.9 %collective-permute-start.10 = (bf16[192,2048]{1,0:T(8,128)(2,1)S(1)}, bf16[192,2048]{1,0:T(8,128)(2,1)S(1)}, u32[]{:S(2)}, u32[]{:S(2)}) collective-permute-start(bf16[192,2048]{1,0:T(8,128)(2,1)S(1)} %get-tuple-element.168), channel_id=1, source_target_pairs={{0,4},{2,6},{4,0},{6,2},{8,12},{10,14},{12,8},{14,10},{16,20},{18,... | collective-permute-start | bytes 2359304 | tf_op jit(solution)/shard_map/ppermute | solution.py:346
  87.2 17.7 %collective-permute-start.9 = (bf16[192,2048]{1,0:T(8,128)(2,1)S(1)}, bf16[192,2048]{1,0:T(8,128)(2,1)S(1)}, u32[]{:S(2)}, u32[]{:S(2)}) collective-permute-start(bf16[192,2048]{1,0:T(8,128)(2,1)S(1)} %get-tuple-element.169), channel_id=1, source_target_pairs={{0,2},{2,0},{4,6},{6,4},{8,10},{10,8},{12,14},{14,12},{16,18},{18,... | collective-permute-start | bytes 2359304 | tf_op jit(solution)/shard_map/ppermute | solution.py:342
  105.0 10.0 %collective-permute-start.16 = (bf16[16,2048]{1,0:T(8,128)(2,1)S(1)}, bf16[16,2048]{1,0:T(8,128)(2,1)S(1)}, u32[]{:S(2)}, u32[]{:S(2)}) collective-permute-start(bf16[16,2048]{1,0:T(8,128)(2,1)S(1)} %slice.507), channel_id=1, source_target_pairs={{8,0},{10,2},{12,4},{14,6},{16,8},{18,10},{20,12},{22,14},{24,16},... | collective-permute-start | bytes 196616 | tf_op jit(solution)/shard_map/ppermute | solution.py:356
  108.6 6.5 %collective-permute-start.15 = (bf16[16,2048]{1,0:T(8,128)(2,1)S(1)}, bf16[16,2048]{1,0:T(8,128)(2,1)S(1)}, u32[]{:S(2)}, u32[]{:S(2)}) collective-permute-start(bf16[16,2048]{1,0:T(8,128)(2,1)S(1)} %slice.506), channel_id=1, source_target_pairs={{0,8},{2,10},{4,12},{6,14},{8,16},{10,18},{12,20},{14,22},{16,24},... | collective-permute-start | bytes 196616 | tf_op jit(solution)/shard_map/ppermute | solution.py:351
  108.6 7.0 %collective-permute-start.13 = (bf16[48,2048]{1,0:T(8,128)(2,1)S(1)}, bf16[48,2048]{1,0:T(8,128)(2,1)S(1)}, u32[]{:S(2)}, u32[]{:S(2)}) collective-permute-start(bf16[48,2048]{1,0:T(8,128)(2,1)S(1)} %slice.504), channel_id=1, source_target_pairs={{0,2},{2,0},{4,6},{6,4},{8,10},{10,8},{12,14},{14,12},{16,18},{18,... | collective-permute-start | bytes 589832 | tf_op jit(solution)/shard_map/ppermute | solution.py:342
  110.4 5.7 %collective-permute-start.14 = (bf16[48,2048]{1,0:T(8,128)(2,1)S(1)}, bf16[48,2048]{1,0:T(8,128)(2,1)S(1)}, u32[]{:S(2)}, u32[]{:S(2)}) collective-permute-start(bf16[48,2048]{1,0:T(8,128)(2,1)S(1)} %slice.505), channel_id=1, source_target_pairs={{0,4},{2,6},{4,0},{6,2},{8,12},{10,14},{12,8},{14,10},{16,20},{18,... | collective-permute-start | bytes 589832 | tf_op jit(solution)/shard_map/ppermute | solution.py:346
  115.0 3.9 %collective-permute-start.18 = (bf16[800,384]{1,0:T(8,128)(2,1)S(1)}, bf16[800,384]{1,0:T(8,128)(2,1)S(1)}, u32[]{:S(2)}, u32[]{:S(2)}) collective-permute-start(bf16[800,384]{1,0:T(8,128)(2,1)S(1)} %convolution_convert_fusion.2), channel_id=1, source_target_pairs={{0,1},{1,0},{2,3},{3,2},{4,5},{5,4},{6,7},{7,6},{8,9},{9,8},{10,11... | collective-permute-start | bytes 1843208 | tf_op jit(solution)/shard_map/ppermute | solution.py:338
  115.1 4.5 %collective-permute-start.19 = (bf16[544,384]{1,0:T(8,128)(2,1)S(1)}, bf16[544,384]{1,0:T(8,128)(2,1)S(1)}, u32[]{:S(2)}, u32[]{:S(2)}) collective-permute-start(bf16[544,384]{1,0:T(8,128)(2,1)S(1)} %convolution_convert_fusion.4), channel_id=1, source_target_pairs={{0,1},{1,0},{2,3},{3,2},{4,5},{5,4},{6,7},{7,6},{8,9},{9,8},{10,11... | collective-permute-start | bytes 1253384 | tf_op jit(solution)/shard_map/ppermute | solution.py:338
  118.2 1.4 collective-permute-start.20
  134.5 2.1 collective-permute-start.21
  139.6 11.9 %collective-permute-start.23 = (bf16[128,768]{1,0:T(8,128)(2,1)S(1)}, bf16[128,768]{1,0:T(8,128)(2,1)S(1)}, u32[]{:S(2)}, u32[]{:S(2)}) collective-permute-start(bf16[128,768]{1,0:T(8,128)(2,1)S(1)} %get-tuple-element.150), channel_id=1, source_target_pairs={{0,4},{2,6},{4,0},{6,2},{8,12},{10,14},{12,8},{14,10},{16,20},{18,... | collective-permute-start | bytes 589832 | tf_op jit(solution)/shard_map/ppermute | solution.py:346
  140.9 10.6 %collective-permute-start.22 = (bf16[128,768]{1,0:T(8,128)(2,1)S(1)}, bf16[128,768]{1,0:T(8,128)(2,1)S(1)}, u32[]{:S(2)}, u32[]{:S(2)}) collective-permute-start(bf16[128,768]{1,0:T(8,128)(2,1)S(1)} %get-tuple-element.151), channel_id=1, source_target_pairs={{0,2},{2,0},{4,6},{6,4},{8,10},{10,8},{12,14},{14,12},{16,18},{18,... | collective-permute-start | bytes 589832 | tf_op jit(solution)/shard_map/ppermute | solution.py:342
  141.5 5.8 %collective-permute-start.25 = (bf16[128,256]{1,0:T(8,128)(2,1)S(1)}, bf16[128,256]{1,0:T(8,128)(2,1)S(1)}, u32[]{:S(2)}, u32[]{:S(2)}) collective-permute-start(bf16[128,256]{1,0:T(8,128)(2,1)S(1)} %get-tuple-element.152), channel_id=1, source_target_pairs={{8,0},{10,2},{12,4},{14,6},{16,8},{18,10},{20,12},{22,14},{24,16},... | collective-permute-start | bytes 196616 | tf_op jit(solution)/shard_map/ppermute | solution.py:356
  145.3 6.1 %collective-permute-start.24 = (bf16[128,256]{1,0:T(8,128)(2,1)S(1)}, bf16[128,256]{1,0:T(8,128)(2,1)S(1)}, u32[]{:S(2)}, u32[]{:S(2)}) collective-permute-start(bf16[128,256]{1,0:T(8,128)(2,1)S(1)} %get-tuple-element.153), channel_id=1, source_target_pairs={{0,8},{2,10},{4,12},{6,14},{8,16},{10,18},{12,20},{14,22},{16,24},... | collective-permute-start | bytes 196616 | tf_op jit(solution)/shard_map/ppermute | solution.py:351
  145.3 11.3 %collective-permute-start.26 = (bf16[1280,384]{1,0:T(8,128)(2,1)S(1)}, bf16[1280,384]{1,0:T(8,128)(2,1)S(1)}, u32[]{:S(2)}, u32[]{:S(2)}) collective-permute-start(bf16[1280,384]{1,0:T(8,128)(2,1)S(1)} %get-tuple-element.71), channel_id=1, source_target_pairs={{0,1},{1,0},{2,3},{3,2},{4,5},{5,4},{6,7},{7,6},{8,9},{9,8},{10,11... | collective-permute-start | bytes 2949128 | tf_op jit(solution)/shard_map/ppermute | solution.py:338
  151.6 14.8 %collective-permute-start.30 = (bf16[128,1280]{1,0:T(8,128)(2,1)S(1)}, bf16[128,1280]{1,0:T(8,128)(2,1)S(1)}, u32[]{:S(2)}, u32[]{:S(2)}) collective-permute-start(bf16[128,1280]{1,0:T(8,128)(2,1)S(1)} %get-tuple-element.132), channel_id=1, source_target_pairs={{8,0},{10,2},{12,4},{14,6},{16,8},{18,10},{20,12},{22,14},{24,16},... | collective-permute-start | bytes 983048 | tf_op jit(solution)/shard_map/ppermute | solution.py:356
  151.7 14.7 %collective-permute-start.29 = (bf16[128,1280]{1,0:T(8,128)(2,1)S(1)}, bf16[128,1280]{1,0:T(8,128)(2,1)S(1)}, u32[]{:S(2)}, u32[]{:S(2)}) collective-permute-start(bf16[128,1280]{1,0:T(8,128)(2,1)S(1)} %get-tuple-element.133), channel_id=1, source_target_pairs={{0,8},{2,10},{4,12},{6,14},{8,16},{10,18},{12,20},{14,22},{16,24},... | collective-permute-start | bytes 983048 | tf_op jit(solution)/shard_map/ppermute | solution.py:351
  153.9 17.0 %collective-permute-start.27 = (bf16[128,3072]{1,0:T(8,128)(2,1)S(1)}, bf16[128,3072]{1,0:T(8,128)(2,1)S(1)}, u32[]{:S(2)}, u32[]{:S(2)}) collective-permute-start(bf16[128,3072]{1,0:T(8,128)(2,1)S(1)} %pad_maximum_fusion.8), channel_id=1, source_target_pairs={{0,2},{2,0},{4,6},{6,4},{8,10},{10,8},{12,14},{14,12},{16,18},{18,... | collective-permute-start | bytes 2359304 | tf_op jit(solution)/shard_map/ppermute | solution.py:342
  155.8 16.4 %collective-permute-start.28 = (bf16[128,3072]{1,0:T(8,128)(2,1)S(1)}, bf16[128,3072]{1,0:T(8,128)(2,1)S(1)}, u32[]{:S(2)}, u32[]{:S(2)}) collective-permute-start(bf16[128,3072]{1,0:T(8,128)(2,1)S(1)} %pad_maximum_fusion.9), channel_id=1, source_target_pairs={{0,4},{2,6},{4,0},{6,2},{8,12},{10,14},{12,8},{14,10},{16,20},{18,... | collective-permute-start | bytes 2359304 | tf_op jit(solution)/shard_map/ppermute | solution.py:346
  161.2 21.4 %copy-start.2 = (bf16[1280,2048]{1,0:T(8,128)(2,1)}, bf16[1280,2048]{1,0:T(8,128)(2,1)S(1)}, u32[]{:S(2)}) copy-start(bf16[1280,2048]{1,0:T(8,128)(2,1)S(1)} %convolution_convert_fusion) | copy-start | bytes 15728644
  180.9 29.2 %collective-permute-start.32 = (bf16[128,4096]{1,0:T(8,128)(2,1)}, bf16[128,4096]{1,0:T(8,128)(2,1)S(1)}, u32[]{:S(2)}, u32[]{:S(2)}) collective-permute-start(bf16[128,4096]{1,0:T(8,128)(2,1)} %get-tuple-element.106), channel_id=1, source_target_pairs={{0,4},{2,6},{4,0},{6,2},{8,12},{10,14},{12,8},{14,10},{16,20},{18,... | collective-permute-start | bytes 3145736 | tf_op jit(solution)/shard_map/ppermute | solution.py:346
  181.7 28.4 %collective-permute-start.31 = (bf16[128,4096]{1,0:T(8,128)(2,1)}, bf16[128,4096]{1,0:T(8,128)(2,1)S(1)}, u32[]{:S(2)}, u32[]{:S(2)}) collective-permute-start(bf16[128,4096]{1,0:T(8,128)(2,1)} %get-tuple-element.107), channel_id=1, source_target_pairs={{0,2},{2,0},{4,6},{6,4},{8,10},{10,8},{12,14},{14,12},{16,18},{18,... | collective-permute-start | bytes 3145736 | tf_op jit(solution)/shard_map/ppermute | solution.py:342
  183.3 18.4 %collective-permute-start.33 = (bf16[128,2304]{1,0:T(8,128)(2,1)}, bf16[128,2304]{1,0:T(8,128)(2,1)}, u32[]{:S(2)}, u32[]{:S(2)}) collective-permute-start(bf16[128,2304]{1,0:T(8,128)(2,1)} %constant_dynamic-update-slice_fusion.31), channel_id=1, source_target_pairs={{0,8},{2,10},{4,12},{6,14},{8,16},{10,18},{12,20},{14,22},{16,24},... | collective-permute-start | bytes 1769480 | tf_op jit(solution)/shard_map/ppermute | solution.py:351
  183.6 26.5 %collective-permute-start.34 = (bf16[128,2304]{1,0:T(8,128)(2,1)}, bf16[128,2304]{1,0:T(8,128)(2,1)}, u32[]{:S(2)}, u32[]{:S(2)}) collective-permute-start(bf16[128,2304]{1,0:T(8,128)(2,1)} %get-tuple-element.108), channel_id=1, source_target_pairs={{8,0},{10,2},{12,4},{14,6},{16,8},{18,10},{20,12},{22,14},{24,16},... | collective-permute-start | bytes 1769480 | tf_op jit(solution)/shard_map/ppermute | solution.py:356
  187.1 37.7 %all-to-all-start.1 = ((bf16[16,128,128]{2,1,0:T(8,128)(2,1)}), bf16[16,128,128]{2,1,0:T(8,128)(2,1)S(1)}, u32[]{:S(2)}, u32[]{:S(2)}) async-start(bf16[16,128,128]{2,1,0:T(8,128)(2,1)} %bitcast.14), calls=%async_computation.1 | async-start | bytes 1048576 | tf_op jit(solution)/shard_map/all_to_all | solution.py:509
  215.1 14.2 %collective-permute-start.37 = (bf16[128,1536]{1,0:T(8,128)(2,1)}, bf16[128,1536]{1,0:T(8,128)(2,1)}, u32[]{:S(2)}, u32[]{:S(2)}) collective-permute-start(bf16[128,1536]{1,0:T(8,128)(2,1)} %pad_maximum_fusion.19), channel_id=1, source_target_pairs={{0,8},{2,10},{4,12},{6,14},{8,16},{10,18},{12,20},{14,22},{16,24},... | collective-permute-start | bytes 1179656 | tf_op jit(solution)/shard_map/ppermute | solution.py:351
  217.4 17.4 %collective-permute-start.35 = (bf16[128,2048]{1,0:T(8,128)(2,1)S(1)}, bf16[128,2048]{1,0:T(8,128)(2,1)S(1)}, u32[]{:S(2)}, u32[]{:S(2)}) collective-permute-start(bf16[128,2048]{1,0:T(8,128)(2,1)S(1)} %pad_maximum_fusion.16), channel_id=1, source_target_pairs={{0,2},{2,0},{4,6},{6,4},{8,10},{10,8},{12,14},{14,12},{16,18},{18,... | collective-permute-start | bytes 1572872 | tf_op jit(solution)/shard_map/ppermute | solution.py:342
  218.5 16.3 %collective-permute-start.36 = (bf16[128,2048]{1,0:T(8,128)(2,1)S(1)}, bf16[128,2048]{1,0:T(8,128)(2,1)S(1)}, u32[]{:S(2)}, u32[]{:S(2)}) collective-permute-start(bf16[128,2048]{1,0:T(8,128)(2,1)S(1)} %pad_maximum_fusion.17), channel_id=1, source_target_pairs={{0,4},{2,6},{4,0},{6,2},{8,12},{10,14},{12,8},{14,10},{16,20},{18,... | collective-permute-start | bytes 1572872 | tf_op jit(solution)/shard_map/ppermute | solution.py:346
  220.5 14.3 %collective-permute-start.38 = (bf16[128,1536]{1,0:T(8,128)(2,1)}, bf16[128,1536]{1,0:T(8,128)(2,1)S(1)}, u32[]{:S(2)}, u32[]{:S(2)}) collective-permute-start(bf16[128,1536]{1,0:T(8,128)(2,1)} %pad_maximum_fusion.20), channel_id=1, source_target_pairs={{8,0},{10,2},{12,4},{14,6},{16,8},{18,10},{20,12},{22,14},{24,16},... | collective-permute-start | bytes 1179656 | tf_op jit(solution)/shard_map/ppermute | solution.py:356
  (4 other events, 14.2 us)

commit v2 on v1

--- a/solution.py
+++ b/solution.py
@@ -372,37 +372,149 @@
     return value.astype(jnp.float32)
 
 
+def halves_kernel(plan, core_ref, array, *refs):
+    outs, arrived = refs[:-1], refs[-1]
+    half = array.shape[1] // 2
+    copies = []
+    for k, (out, (count, mine)) in enumerate(zip(outs, plan)):
+        side = core_ref[0] if mine else 1 - core_ref[0]
+        part = array.at[pl.ds(0, count), pl.ds(pl.multiple_of(side * half, half), half)]
+        copies.append(pltpu.make_async_copy(part, out, arrived.at[k]))
+    for copy in copies:
+        copy.start()
+    for copy in copies:
+        copy.wait()
+
+
+def halves(array, *plan):
+    half = array.shape[1] // 2
+    core = lax.axis_index("tp").astype(jnp.int32).reshape(1)
+    moved = sum(2 * count * half for count, _ in plan)
+    return pl.pallas_call(
+        functools.partial(halves_kernel, plan),
+        out_shape=tuple(jax.ShapeDtypeStruct((count, half), jnp.bfloat16) for count, _ in plan),
+        in_specs=[pl.BlockSpec(memory_space=pltpu.SMEM), pl.BlockSpec(memory_space=pl.ANY)],
+        out_specs=(pl.BlockSpec(memory_space=pltpu.VMEM),) * len(plan),
+        scratch_shapes=[pltpu.SemaphoreType.DMA((len(plan),))],
+        compiler_params=pltpu.CompilerParams(vmem_limit_bytes=16 * 2**20),
+        cost_estimate=pl.CostEstimate(flops=0, bytes_accessed=2 * moved, transcendentals=0),
+        name="halves",
+    )(core, array)
+
+
+def assemble_kernel(inputs, plans, *refs):
+    arrays, refs = refs[:inputs], refs[inputs:]
+    outs, refs = refs[: len(plans)], refs[len(plans) :]
+    arrived, held = refs[0], refs[1:]
+    started, k, slot = [], 0, 0
+    pending = []
+    for out, plan in zip(outs, plans):
+        for row, col, height, width, sources in plan:
+            here = out.at[pl.ds(row, height), pl.ds(col, width)]
+            single = len(sources) == 1
+            mine = []
+            for index, from_row, from_col in sources:
+                part = arrays[index].at[pl.ds(from_row, height), pl.ds(from_col, width)]
+                into = here if single else held[slot]
+                copy = pltpu.make_async_copy(part, into, arrived.at[k])
+                copy.start()
+                mine.append((copy, into))
+                k += 1
+                slot += 0 if single else 1
+            if single:
+                started.append(mine[0][0])
+            else:
+                pending.append((here, mine))
+    for here, mine in pending:
+        for copy, _ in mine:
+            copy.wait()
+        here[...] = narrowed(sum(widened(into[...]) for _, into in mine))
+    for copy in started:
+        copy.wait()
+
+
+def assemble(arrays, *plans):
+    sources = [(piece, source) for plan in plans for piece in plan for source in piece[4]]
+    sums = [piece for piece, _ in sources if len(piece[4]) > 1]
+    shapes = [
+        (max(p[0] + p[2] for p in plan), max(p[1] + p[3] for p in plan)) for plan in plans
+    ]
+    moved = sum(2 * rows * cols for rows, cols in shapes)
+    return pl.pallas_call(
+        functools.partial(assemble_kernel, len(arrays), plans),
+        out_shape=tuple(jax.ShapeDtypeStruct(shape, jnp.bfloat16) for shape in shapes),
+        in_specs=[pl.BlockSpec(memory_space=pl.ANY)] * len(arrays),
+        out_specs=(pl.BlockSpec(memory_space=pltpu.VMEM),) * len(plans),
+        scratch_shapes=[pltpu.SemaphoreType.DMA((len(sources),))]
+        + [pltpu.VMEM((piece[2], piece[3]), jnp.bfloat16) for piece in sums],
+        compiler_params=pltpu.CompilerParams(vmem_limit_bytes=24 * 2**20),
+        cost_estimate=pl.CostEstimate(flops=moved, bytes_accessed=4 * moved, transcendentals=0),
+        name="assemble",
+    )(*arrays)
+
+
+def rows_of(*parts):
+    plan, start = [], 0
+    for index, first, count in parts:
+        plan.append((start, count, [(index, first, 0)]))
+        start += count
+    return plan
+
+
+def full_width(columns, plan):
+    return [(row, 0, count, columns, sources) for row, count, sources in plan]
+
+
+def columns_of(height, *parts):
+    plan, start = [], 0
+    for width, sources in parts:
+        plan.append((0, start, height, width, sources))
+        start += width
+    return plan
+
+
 def all_ways(for_x, for_y, for_above, for_below):
     return lax.optimization_barrier((over_x(for_x), over_y(for_y), up(for_above), down(for_below)))
 
 
-def gather_groups(tokens, prepared):
+def gather_groups(tokens, matrices, later):
     span = tokens.shape[0]
     n, m = span * 3 // 4, span // 4
     nh, mh = n // 2, m // 2
-    wide, narrow = tokens[:n], tokens[n:]
+    columns = tokens.shape[1] // 2
+
+    def put(arrays, *plans):
+        return assemble(arrays, *[full_width(columns, rows_of(*plan)) for plan in plans])
+
+    tokens, wide = halves(tokens, (span, True), (n, True))
     own_x, own_y, wide_3, wide_1 = all_ways(tokens, tokens, wide, wide)
-    own_x, prepared = lax.optimization_barrier((own_x, prepared))
-    members = (narrow, own_x[n:], own_y[n:])
+    own_x, matrices = lax.optimization_barrier((own_x, matrices))
     first = (tokens, own_x, own_y, wide_3, wide_1)
-    second = all_ways(
-        stack(own_y[:nh], own_y[n : n + mh], wide_3, wide_1),
-        stack(own_x[nh:n], own_x[n + mh :], wide_3, wide_1),
-        stack(wide_3[:nh], *members),
-        stack(wide_1[nh:], *members),
-    )
-    got_x, got_y, below, above = second
+    members = ((0, n, m), (1, n, m), (2, n, m))
+    sent = put(
+        first,
+        ((2, 0, nh), (2, n, mh), (3, 0, n), (4, 0, n)),
+        ((1, nh, nh), (1, n + mh, mh), (3, 0, n), (4, 0, n)),
+        ((3, 0, nh), *members),
+        ((4, nh, nh), *members),
+    )
+    second = all_ways(*sent)
+    second, later = lax.optimization_barrier((second, later))
     start = nh + mh
-    across = (got_x[nh:start], got_y[nh:start])
-    wide_2 = (below[:nh], above[:nh])
+    wide_2 = ((2, 0, nh), (3, 0, nh))
+    across = ((0, nh, mh), (1, nh, mh))
     third = all_ways(
-        stack(got_y[start : start + nh], got_y[start + n : start + n + nh], *wide_2),
-        stack(got_x[start + nh : start + n], got_x[start + n + nh :], *wide_2),
-        stack(*across, below[nh : 2 * nh]),
-        stack(*across, above[2 * nh :]),
-    )
-    got_x, got_y, below, above = third
-    fourth = all_ways(got_y[n : n + nh], got_x[n + nh :], below[:mh], above[mh:m])
+        *put(
+            second,
+            ((1, start, nh), (1, start + n, nh), *wide_2),
+            ((0, start + nh, nh), (0, start + n + nh, nh), *wide_2),
+            (*across, (2, nh, nh)),
+            (*across, (3, 2 * nh, nh)),
+        )
+    )
+    fourth = all_ways(
+        *put(third, ((1, n, nh),), ((0, n + nh, nh),), ((2, 0, mh),), ((3, mh, mh),))
+    )
     runs = [
         (0, 0, 0, 0, 3, span, 0),
         (0, 3 * span, 3, 0, 1, n, 0),
@@ -443,7 +555,7 @@
         (3, n, 2, 3, 1, mh, n),
         (3, n + mh, 2, 3, 1, mh, n + mh),
     ]
-    return [stack(*part) for part in (first, second, third, fourth)], tuple(runs), prepared
+    return [stack(*part) for part in (first, second, third, fourth)], tuple(runs), matrices, later
 
 
 ORDER = (((2, 0, 4), (1, 3, 1), (3, 3, 1)), ((1, 0, 3), (3, 0, 3), (0, 0, 4)))
@@ -453,145 +565,132 @@
     span = early.shape[0] // 6
     columns = matrix.shape[1]
     wide, narrow = columns * 3 // 8, columns // 8
-    blocks = {}
+    places = {}
+    for array, pieces in enumerate(ORDER):
+        row = 0
+        for group, base, members in pieces:
+            for member in range(base, base + members):
+                places[group, member] = (array, row)
+                row += span
 
     def product(part, other):
         both = beside(part, other)
         return narrowed(jnp.dot(both, matrix, preferred_element_type=jnp.float32))
 
-    def keep(value, pieces):
-        start = 0
-        for group, base, members in pieces:
-            for member in range(base, base + members):
-                blocks[group, member] = value[start : start + span]
-                start += span
-
-    def term(group, member, side):
-        return blocks[group, member][:, side * wide : (side + 1) * wide]
-
-    def low(group, member, side):
-        first = 2 * wide + side * narrow
-        return blocks[group, member][:, first : first + narrow]
-
-    def total(*parts):
-        return sum(widened(part) for part in parts)
-
-    def added(*parts):
-        return narrowed(total(*parts))
-
-    def cut(value, *widths):
-        parts, start = [], 0
-        for width in widths:
-            parts.append(value[:, start : start + width])
-            start += width
-        return parts
+    def term(group, member, side, *more):
+        array, row = places[group, member]
+        return (wide, [(array, row, side * wide), *more])
+
+    def low(group, member, side, *more):
+        array, row = places[group, member]
+        return (narrow, [(array, row, 2 * wide + side * narrow), *more])
+
+    def put(arrays, *plans):
+        return assemble(arrays, *[columns_of(span, *plan) for plan in plans])
 
     early = product(early, swapped(early))
-    keep(early, ORDER[0])
     other = swapped(later)
-    across_y, across_x, from_below, from_above = all_ways(
-        term(2, 3, 0), term(2, 3, 1), low(2, 3, 0), low(2, 3, 1)
-    )
-    later, across_x = lax.optimization_barrier((later, across_x))
-    got_x, got_y, below, above = all_ways(
-        beside(term(2, 1, 0), added(term(2, 1, 1), across_x), term(1, 3, 0), term(3, 3, 0)),
-        beside(added(term(2, 2, 0), across_y), term(2, 2, 1), term(1, 3, 1), term(3, 3, 1)),
-        beside(
-            added(low(1, 3, 0), from_below), low(1, 3, 1), *[low(2, k, 0) for k in range(3)]
-        ),
-        beside(
-            low(3, 3, 0), added(low(3, 3, 1), from_above), *[low(2, k, 1) for k in range(3)]
-        ),
+    first = all_ways(
+        *put([early], [term(2, 3, 0)], [term(2, 3, 1)], [low(2, 3, 0)], [low(2, 3, 1)])
+    )
+    later, first = lax.optimization_barrier((later, first))
+    x, y, below, above = range(1, 5)
+    second = all_ways(
+        *put(
+            [early, *first],
+            [term(2, 1, 0), term(2, 1, 1, (y, 0, 0)), term(1, 3, 0), term(3, 3, 0)],
+            [term(2, 2, 0, (x, 0, 0)), term(2, 2, 1), term(1, 3, 1), term(3, 3, 1)],
+            [low(1, 3, 0, (below, 0, 0)), low(1, 3, 1), *[low(2, k, 0) for k in range(3)]],
+            [low(3, 3, 0), low(3, 3, 1, (above, 0, 0)), *[low(2, k, 1) for k in range(3)]],
+        )
     )
     later = product(later, other)
-    later, hyena, got_x = lax.optimization_barrier((later, hyena, got_x))
-    keep(later, ORDER[1])
+    later, hyena, second = lax.optimization_barrier((later, hyena, second))
     hyena_out = lax.all_to_all(hyena, "ctx", split_axis=0, concat_axis=1, tiled=True).T
-    *own_x, across_1y, across_3y = cut(got_x, *[wide] * 4)
-    *own_y, across_1x, across_3x = cut(got_y, *[wide] * 4)
-    below_0, below_1, *from_below = cut(below, *[narrow] * 5)
-    above_0, above_1, *from_above = cut(above, *[narrow] * 5)
-    sum_2 = [added(term(2, 0, side), own_x[side], own_y[side]) for side in (0, 1)]
-    low_3 = [added(low(0, 3, 0), below_0, above_0), added(low(0, 3, 1), below_1, above_1)]
+    x, y, below, above = range(2, 6)
+
+    def low_3(side):
+        return low(0, 3, side, (below, 0, side * narrow), (above, 0, side * narrow))
+
+    def sum_2(side):
+        return term(2, 0, side, (x, 0, side * wide), (y, 0, side * wide))
+
     for_above, for_below = [], []
     for k in range(3):
-        for_above += [added(low(1, k, 0), from_below[k]), low(1, k, 1)]
-        for_below += [low(3, k, 0), added(low(3, k, 1), from_above[k])]
-    got_x, got_y, below, above = all_ways(
-        beside(
-            term(1, 1, 0),
-            added(term(1, 1, 1), across_1x),
-            term(3, 1, 0),
-            added(term(3, 1, 1), across_3x),
-            term(0, 3, 0),
-            low_3[0],
-        ),
-        beside(
-            added(term(1, 2, 0), across_1y),
-            term(1, 2, 1),
-            added(term(3, 2, 0), across_3y),
-            term(3, 2, 1),
-            term(0, 3, 1),
-            low_3[1],
-        ),
-        beside(sum_2[0], *for_above),
-        beside(sum_2[1], *for_below),
-    )
-    *own_x, across_y, low_across_y = cut(got_x, *[wide] * 5, narrow)
-    *own_y, across_x, low_across_x = cut(got_y, *[wide] * 5, narrow)
-    from_below, *low_below = cut(below, wide, *[narrow] * 6)
-    from_above, *low_above = cut(above, wide, *[narrow] * 6)
-    low_own = [
-        [total(low(0, k, side), low_below[2 * k + side], low_above[2 * k + side]) for side in (0, 1)]
-        for k in range(3)
-    ]
-    got_x, got_y, below, above = all_ways(
-        beside(
-            term(0, 1, 0),
-            added(term(0, 1, 1), across_x),
-            narrowed(low_own[1][0]),
-            added(low_own[1][1], low_across_x),
-        ),
-        beside(
-            added(term(0, 2, 0), across_y),
-            term(0, 2, 1),
-            added(low_own[2][0], low_across_y),
-            narrowed(low_own[2][1]),
-        ),
-        beside(
-            added(term(1, 0, 0), own_x[0], own_y[0], from_below),
-            added(term(1, 0, 1), own_x[1], own_y[1]),
-        ),
-        beside(
-            added(term(3, 0, 0), own_x[2], own_y[2]),
-            added(term(3, 0, 1), own_x[3], own_y[3], from_above),
-        ),
-    )
-    return (
-        beside(
-            added(
-                blocks[0, 0][:, : 2 * wide], got_x[:, : 2 * wide], got_y[:, : 2 * wide], below, above
-            ),
-            added(
-                beside(*low_own[0]), got_x[:, 2 * wide :], got_y[:, 2 * wide :]
-            ),
-        ),
-        hyena_out,
-    )
+        start = (2 + k) * narrow
+        for_above += [low(1, k, 0, (below, 0, start)), low(1, k, 1)]
+        for_below += [low(3, k, 0), low(3, k, 1, (above, 0, start))]
+    third = all_ways(
+        *put(
+            [early, later, *second],
+            [
+                term(1, 1, 0),
+                term(1, 1, 1, (y, 0, 2 * wide)),
+                term(3, 1, 0),
+                term(3, 1, 1, (y, 0, 3 * wide)),
+                term(0, 3, 0),
+                low_3(0),
+            ],
+            [
+                term(1, 2, 0, (x, 0, 2 * wide)),
+                term(1, 2, 1),
+                term(3, 2, 0, (x, 0, 3 * wide)),
+                term(3, 2, 1),
+                term(0, 3, 1),
+                low_3(1),
+            ],
+            [sum_2(0), *for_above],
+            [sum_2(1), *for_below],
+        )
+    )
+
+    def low_own(k, side, *more):
+        start = wide + (2 * k + side) * narrow
+        return low(0, k, side, (below, 0, start), (above, 0, start), *more)
+
+    def own(group, side, *more):
+        start = (group - 1 + side) * wide
+        return term(group, 0, side, (x, 0, start), (y, 0, start), *more)
+
+    fourth = all_ways(
+        *put(
+            [early, later, *third],
+            [
+                term(0, 1, 0),
+                term(0, 1, 1, (y, 0, 4 * wide)),
+                low_own(1, 0),
+                low_own(1, 1, (y, 0, 5 * wide)),
+            ],
+            [
+                term(0, 2, 0, (x, 0, 4 * wide)),
+                term(0, 2, 1),
+                low_own(2, 0, (x, 0, 5 * wide)),
+                low_own(2, 1),
+            ],
+            [own(1, 0, (below, 0, 0)), own(1, 1)],
+            [own(3, 0), own(3, 1, (above, 0, 0))],
+        )
+    )
+    last = range(6, 10)
+    (grad_input,) = put(
+        [early, later, *third, *fourth],
+        [term(0, 0, side, *[(way, 0, side * wide) for way in last]) for side in (0, 1)]
+        + [
+            low_own(0, side, *[(way, 0, 2 * wide + side * narrow) for way in (6, 7)])
+            for side in (0, 1)
+        ],
+    )
+    return grad_input, hyena_out
 
 
 def gather_tokens(tokens, weights, residues, decay_rates, cotangent):
-    core = lax.axis_index("tp")
     me = lax.axis_index("ctx").astype(jnp.int32).reshape(1)
-    half = tokens.shape[1] // 2
     channels = weights.shape[1]
-    rows = weights[0].swapaxes(0, 1).reshape(3 * channels, 2 * half)
-    kept = lax.dynamic_slice_in_dim(rows, core * half, half, 1)
-    taken = swapped(lax.dynamic_slice_in_dim(rows, (1 - core) * half, half, 1))
+    rows = weights[0].swapaxes(0, 1).reshape(3 * channels, weights.shape[3])
+    kept, given = halves(rows, (3 * channels, True), (3 * channels, False))
+    taken = swapped(given)
+    parts, runs, (kept, taken), cotangent = gather_groups(tokens, (kept, taken), cotangent)
     cot_cols = lax.all_to_all(cotangent.T, "ctx", split_axis=1, concat_axis=0, tiled=True)
-    parts, runs, (kept, taken, cot_cols) = gather_groups(
-        lax.dynamic_slice_in_dim(tokens, core * half, half, 1), (kept, taken, cot_cols)
-    )
 
     def project(part, matrix):
         return jnp.einsum("td,rd->tr", part, matrix, preferred_element_type=jnp.float32)

time: 238 us -> 237 us (level)
  Pallas kernels: 14.9 us -> 34.4 us
  other arithmetic: 14.8 us -> 0 us
  waiting for transfers between devices: 103 us -> 89.7 us
  starting transfers between devices: 56.8 us -> 61.6 us
  matrix products: 23.5 us -> 27.4 us
    pallas_call x0 -> x10, Pallas kernels: none -> 19.5 us  [the longest x8 17.2 us: assemble(): pl.pallas_call(functools.partial(assemble_kernel, len(arrays), plans), ou...]
    slice x22 -> x0, local copies, waits for them, and re-layouts: 8.35 us -> none  [the longest x3 1.75 us: gather_groups(): wide, narrow = (tokens[:n], tokens[n:])]
    unnamed x39 -> x44, local copies, waits for them, and re-layouts: 6.55 us -> 14.9 us
    ppermute x8, waiting for transfers between devices: 49.1 us -> 41 us  [up(): lax.ppermute(value, 'ctx', [(i, (i + PLANE) % count) for i in range(count)])]
    ppermute x8, starting transfers between devices: 17 us -> 25 us  [down(): lax.ppermute(value, 'ctx', [((i + PLANE) % count, i) for i in range(count)])]
    convert_element_type x6 -> x0, other arithmetic: 5.72 us -> none  [narrowed(): return value.astype(jnp.bfloat16)]
    ppermute x8, waiting for transfers between devices: 4.79 us -> 9.92 us  [over_x(): lax.ppermute(value, 'ctx', [(i, i ^ 1) for i in range(lax.axis_size('ctx'...]
    unnamed x8 -> x0, other arithmetic: 5.02 us -> none
  transfers between devices with their start and end apart: 41 -> 41, of which waited for: 20 -> 17; matrix products, arithmetic and copies ran while one was open for 16% -> 16% of each run, Pallas kernels for 0% -> 4%
where the time goes in v2:
time: 237 us; the launch traced here: 236 us
  waiting for transfers between devices  89.7 us (38%)
  starting transfers between devices  61.6 us (26%)
  Pallas kernels  34.4 us (15%)
  matrix products  27.4 us (12%)
  local copies, waits for them, and re-layouts  21.5 us (9%)
    ppermute x8, waiting for transfers between devices, up(): lax.ppermute(value, 'ctx', [(i, (i + PLANE) % count) for i in range(count)])  41 us
    ppermute x8, waiting for transfers between devices, down(): lax.ppermute(value, 'ctx', [((i + PLANE) % count, i) for i in range(count)])  37.8 us
    ppermute x8, starting transfers between devices, down(): lax.ppermute(value, 'ctx', [((i + PLANE) % count, i) for i in range(count)])  25 us
    dot_general x8, matrix products, project(): jnp.einsum('td,rd->tr', part, matrix, preferred_element_type=jnp.float32)  20 us
    pallas_call x8, Pallas kernels, assemble(): pl.pallas_call(functools.partial(assemble_kernel, len(arrays), plans), ou...  17.2 us
    pallas_call x1, Pallas kernels, scan_all(): pl.pallas_call(functools.partial(scan_kernel, PLANE, runs, order), out_sh...  15 us
    unnamed x44, local copies, waits for them, and re-layouts  14.9 us
    ppermute x8, starting transfers between devices, over_y(): lax.ppermute(value, 'ctx', [(i, i ^ 2) for i in range(lax.axis_size('ctx'...  10.4 us
  transfers between devices with their start and end apart: 41, of which 17 were waited for; matrix products, arithmetic and copies ran while one was open for 16% of the time, Pallas kernels for 4%

profile of v2, /device:TPU:0, one launch (start us, length us, event | category | flops | bytes accessed | tf_op | source)
XLA Modules:
  0.0 236.0 jit_solution(3475655825451772211)
XLA Ops:
  0.6 1.9 copy-done.3
  5.3 2.6 %collective-permute-start.1 = (bf16[128,2048]{1,0:T(8,128)(2,1)S(1)}, bf16[128,2048]{1,0:T(8,128)(2,1)S(1)}, u32[]{:S(2)}, u32[]{:S(2)}) collective-permute-start(bf16[128,2048]{1,0:T(8,128)(2,1)S(1)} %get-tuple-element.90.refs_0_), channel_id=1, source_target_pairs={{0,4},{2,6},{4,0},{6,2},{8,12},{10,14},{12,8},{14,10},{16,20},{18,... | collective-permute-start | bytes 1572872 | tf_op jit(solution)/shard_map/ppermute | solution.py:346
  9.4 3.6 %collective-permute-start.3 = (bf16[96,2048]{1,0:T(8,128)(2,1)}, bf16[96,2048]{1,0:T(8,128)(2,1)S(1)}, u32[]{:S(2)}, u32[]{:S(2)}) collective-permute-start(bf16[96,2048]{1,0:T(8,128)(2,1)} %get-tuple-element.91), channel_id=1, source_target_pairs={{8,0},{10,2},{12,4},{14,6},{16,8},{18,10},{20,12},{22,14},{24,16},... | collective-permute-start | bytes 1179656 | tf_op jit(solution)/shard_map/ppermute | solution.py:356
  13.1 9.8 %collective-permute-done.3.refs_4_ = bf16[96,2048]{1,0:T(8,128)(2,1)S(1)} collective-permute-done((bf16[96,2048]{1,0:T(8,128)(2,1)}, bf16[96,2048]{1,0:T(8,128)(2,1)S(1)}, u32[]{:S(2)}, u32[]{:S(2)}) %collective-permute-start.3) | collective-permute-done | bytes 393248 | tf_op jit(solution)/shard_map/ppermute | solution.py:356
  22.9 8.3 %collective-permute-done.2.refs_3_ = bf16[96,2048]{1,0:T(8,128)(2,1)} collective-permute-done((bf16[96,2048]{1,0:T(8,128)(2,1)}, bf16[96,2048]{1,0:T(8,128)(2,1)}, u32[]{:S(2)}, u32[]{:S(2)}) %collective-permute-start.2) | collective-permute-done | bytes 393248 | tf_op jit(solution)/shard_map/ppermute | solution.py:351
  31.3 2.5 %assemble.8 = (bf16[256,2048]{1,0:T(8,128)(2,1)S(1)}, bf16[256,2048]{1,0:T(8,128)(2,1)S(1)}, bf16[144,2048]{1,0:T(8,128)(2,1)S(1)}, bf16[144,2048]{1,0:T(8,128)(2,1)S(1)}) custom-call(bf16[128,2048]{1,0:T(8,128)(2,1)S(1)} %get-tuple-element.90.refs_0_, bf16[128,2048]{1,0:T(8,128)(2,1)S(1)} %collective-permute-done.refs_1_, ...), custom_call_target="tpu_custom_call" | custom-call | flops 3276800 | bytes 13107200 | tf_op jit(solution)/shard_map/assemble/pallas_call | solution.py:443
  37.6 2.2 collective-permute-start.8
  40.8 3.6 %convolution_convert_fusion.3 = bf16[576,384]{1,0:T(8,128)(2,1)} fusion(bf16[576,2048]{1,0:T(8,128)(2,1)S(1)} %constant_dynamic-update-slice_fusion, bf16[384,2048]{1,0:T(8,128)(2,1)} %collective-permute-done.4), kind=kOutput, calls=%fused_computation.6 | convolution fusion | flops 906190848 | bytes 4374528 | tf_op jit(solution)/shard_map/td,rd->tr/dot_general | solution.py:696
  44.4 2.3 fusion.8.refs_1_
  46.7 7.3 %collective-permute-done.7.refs_2_ = bf16[144,2048]{1,0:T(8,128)(2,1)S(1)} collective-permute-done((bf16[144,2048]{1,0:T(8,128)(2,1)S(1)}, bf16[144,2048]{1,0:T(8,128)(2,1)S(1)}, u32[]{:S(2)}, u32[]{:S(2)}) %collective-permute-start.7) | collective-permute-done | bytes 589856 | tf_op jit(solution)/shard_map/ppermute | solution.py:351
  54.0 9.7 %collective-permute-done.8.refs_3_ = bf16[144,2048]{1,0:T(8,128)(2,1)S(1)} collective-permute-done((bf16[144,2048]{1,0:T(8,128)(2,1)S(1)}, bf16[144,2048]{1,0:T(8,128)(2,1)S(1)}, u32[]{:S(2)}, u32[]{:S(2)}) %collective-permute-start.8) | collective-permute-done | bytes 589856 | tf_op jit(solution)/shard_map/ppermute | solution.py:356
  64.5 2.0 copy.8
  66.6 5.4 %all-to-all-start = ((bf16[128,16,128]{2,0,1:T(8,128)(2,1)}), bf16[128,16,128]{2,0,1:T(8,128)(2,1)}, u32[]{:S(2)}, u32[]{:S(2)}) async-start(bf16[128,16,128]{2,0,1:T(8,128)(2,1)} %copy.8), calls=%async_computation | async-start | bytes 1048576 | tf_op jit(solution)/shard_map/all_to_all | solution.py:693
  73.4 2.9 %assemble.9 = (bf16[192,2048]{1,0:T(8,128)(2,1)S(1)}, bf16[192,2048]{1,0:T(8,128)(2,1)S(1)}, bf16[80,2048]{1,0:T(8,128)(2,1)S(1)}, bf16[80,2048]{1,0:T(8,128)(2,1)S(1)}) custom-call(bf16[256,2048]{1,0:T(8,128)(2,1)} %collective-permute-done.5.refs_0_, bf16[256,2048]{1,0:T(8,128)(2,1)S(1)} %collective-permute-done.6.refs_1_, ...), custom_call_target="tpu_custom_call" | custom-call | flops 2228224 | bytes 8912896 | tf_op jit(solution)/shard_map/assemble/pallas_call | solution.py:443
  76.3 1.9 collective-permute-start.11
  78.2 2.0 collective-permute-start.12
  80.2 1.9 collective-permute-start.9
  83.7 3.3 %convolution_convert_fusion.2 = bf16[800,384]{1,0:T(8,128)(2,1)S(1)} fusion(bf16[800,2048]{1,0:T(8,128)(2,1)S(1)} %constant_dynamic-update-slice_fusion.5, bf16[384,2048]{1,0:T(8,128)(2,1)} %collective-permute-done.4), kind=kOutput, calls=%fused_computation.5 | convolution fusion | flops 1258598400 | bytes 5464064 | tf_op jit(solution)/shard_map/td,rd->tr/dot_general | solution.py:696
  87.0 1.9 fusion.9.refs_2_
  88.8 4.2 %collective-permute-done.11.refs_2_ = bf16[80,2048]{1,0:T(8,128)(2,1)S(1)} collective-permute-done((bf16[80,2048]{1,0:T(8,128)(2,1)S(1)}, bf16[80,2048]{1,0:T(8,128)(2,1)S(1)}, u32[]{:S(2)}, u32[]{:S(2)}) %collective-permute-start.11) | collective-permute-done | bytes 327712 | tf_op jit(solution)/shard_map/ppermute | solution.py:351
  93.0 2.3 collective-permute-done.12.refs_3_
  95.3 3.9 %collective-permute-done.9.refs_0_ = bf16[192,2048]{1,0:T(8,128)(2,1)S(1)} collective-permute-done((bf16[192,2048]{1,0:T(8,128)(2,1)S(1)}, bf16[192,2048]{1,0:T(8,128)(2,1)S(1)}, u32[]{:S(2)}, u32[]{:S(2)}) %collective-permute-start.9) | collective-permute-done | bytes 786464 | tf_op jit(solution)/shard_map/ppermute | solution.py:342
  101.2 3.1 %collective-permute-start.16 = (bf16[16,2048]{1,0:T(8,128)(2,1)S(1)}, bf16[16,2048]{1,0:T(8,128)(2,1)S(1)}, u32[]{:S(2)}, u32[]{:S(2)}) collective-permute-start(bf16[16,2048]{1,0:T(8,128)(2,1)S(1)} %get-tuple-element.124), channel_id=1, source_target_pairs={{8,0},{10,2},{12,4},{14,6},{16,8},{18,10},{20,12},{22,14},{24,16},... | collective-permute-start | bytes 196616 | tf_op jit(solution)/shard_map/ppermute | solution.py:356
  106.5 3.5 %convolution_convert_fusion.4 = bf16[544,384]{1,0:T(8,128)(2,1)} fusion(bf16[544,2048]{1,0:T(8,128)(2,1)S(1)} %constant_dynamic-update-slice_fusion.9, bf16[384,2048]{1,0:T(8,128)(2,1)} %collective-permute-done.4), kind=kOutput, calls=%fused_computation.7 | convolution fusion | flops 855846912 | bytes 4218880 | tf_op jit(solution)/shard_map/td,rd->tr/dot_general | solution.py:696
  110.1 2.3 fusion.10.refs_3_
  112.9 2.6 %convolution_convert_fusion.5 = bf16[128,384]{1,0:T(8,128)(2,1)} fusion(bf16[128,2048]{1,0:T(8,128)(2,1)S(1)} %constant_dynamic-update-slice_fusion.13, bf16[384,2048]{1,0:T(8,128)(2,1)} %collective-permute-done.4), kind=kOutput, calls=%fused_computation.11 | convolution fusion | flops 201375744 | bytes 2195456 | tf_op jit(solution)/shard_map/td,rd->tr/dot_general | solution.py:696
  120.5 15.0 %modal_scan.1 = (bf16[2048,128]{1,0:T(8,128)(2,1)S(1)}, f32[16,128]{1,0:T(8,128)}, bf16[768,384]{1,0:T(8,128)(2,1)S(1)}, bf16[1280,384]{1,0:T(8,128)(2,1)S(1)}) custom-call(s32[1]{0:T(128)} %bitcast.me_ref, f32[16,128]{1,0:T(8,128)S(1)} %bitcast.47, f32[16,128]{1,0:T(8,128)S(1)} %bitcast.48, bf16[2048,128]{1,0:T(8,128)(2,1)} %bitcast.12.refs_0_, ...), custom_call_target="tpu_custom_call" | custom-call | tf_op jit(solution)/shard_map/modal_scan/pallas_call | solution.py:315
  137.8 2.9 %convolution_convert_fusion.1.refs_0_ = bf16[768,2048]{1,0:T(8,128)(2,1)S(1)} fusion(bf16[768,2048]{1,0:T(8,128)(2,1)S(1)} %constant_dynamic-update-slice_fusion.17, bf16[768,384]{1,0:T(8,128)(2,1)S(1)} %collective-permute-done.21, bf16[768,384]{1,0:T(8,128)(2,1)S(1)} %get-tuple-element.131), kind=kOutput, calls=%fused_computation.1 | convolution fusion | flops 2419851264 | bytes 7471104 | tf_op jit(solution)/shard_map/dot_general | solution.py:578
  142.9 3.8 %collective-permute-start.25 = (bf16[128,256]{1,0:T(8,128)(2,1)S(1)}, bf16[128,256]{1,0:T(8,128)(2,1)S(1)}, u32[]{:S(2)}, u32[]{:S(2)}) collective-permute-start(bf16[128,256]{1,0:T(8,128)(2,1)S(1)} %get-tuple-element.135), channel_id=1, source_target_pairs={{8,0},{10,2},{12,4},{14,6},{16,8},{18,10},{20,12},{22,14},{24,16},... | collective-permute-start | bytes 196616 | tf_op jit(solution)/shard_map/ppermute | solution.py:356
  146.7 2.6 %collective-permute-done.24.refs_3_ = bf16[128,256]{1,0:T(8,128)(2,1)S(1)} collective-permute-done((bf16[128,256]{1,0:T(8,128)(2,1)S(1)}, bf16[128,256]{1,0:T(8,128)(2,1)S(1)}, u32[]{:S(2)}, u32[]{:S(2)}) %collective-permute-start.24) | collective-permute-done | bytes 65568 | tf_op jit(solution)/shard_map/ppermute | solution.py:351
  150.7 3.8 %collective-permute-start.30 = (bf16[128,1280]{1,0:T(8,128)(2,1)S(1)}, bf16[128,1280]{1,0:T(8,128)(2,1)S(1)}, u32[]{:S(2)}, u32[]{:S(2)}) collective-permute-start(bf16[128,1280]{1,0:T(8,128)(2,1)S(1)} %get-tuple-element.149), channel_id=1, source_target_pairs={{8,0},{10,2},{12,4},{14,6},{16,8},{18,10},{20,12},{22,14},{24,16},... | collective-permute-start | bytes 983048 | tf_op jit(solution)/shard_map/ppermute | solution.py:356
  156.6 4.5 %convolution_convert_fusion.refs_1_ = bf16[1280,2048]{1,0:T(8,128)(2,1)S(1)} fusion(bf16[768,2048]{1,0:T(8,128)(2,1)S(1)} %constant_dynamic-update-slice_fusion.17, bf16[1280,384]{1,0:T(8,128)(2,1)S(1)} %collective-permute-done.26, bf16[1280,384]{1,0:T(8,128)(2,1)S(1)} %get-tuple-element.140), kind=kOutput, calls=%fused_computation | convolution fusion | flops 4033085440 | bytes 10354688 | tf_op jit(solution)/shard_map/dot_general | solution.py:578
  161.1 2.0 collective-permute-done.29.refs_4_
  163.1 3.4 %collective-permute-done.30.refs_5_ = bf16[128,1280]{1,0:T(8,128)(2,1)S(1)} collective-permute-done((bf16[128,1280]{1,0:T(8,128)(2,1)S(1)}, bf16[128,1280]{1,0:T(8,128)(2,1)S(1)}, u32[]{:S(2)}, u32[]{:S(2)}) %collective-permute-start.30) | collective-permute-done | bytes 327712 | tf_op jit(solution)/shard_map/ppermute | solution.py:356
  166.5 6.0 %collective-permute-done.27.refs_2_ = bf16[128,3072]{1,0:T(8,128)(2,1)S(1)} collective-permute-done((bf16[128,3072]{1,0:T(8,128)(2,1)S(1)}, bf16[128,3072]{1,0:T(8,128)(2,1)S(1)}, u32[]{:S(2)}, u32[]{:S(2)}) %collective-permute-start.27) | collective-permute-done | bytes 786464 | tf_op jit(solution)/shard_map/ppermute | solution.py:342
  173.1 3.4 %assemble.13 = (bf16[128,4096]{1,0:T(8,128)(2,1)}, bf16[128,4096]{1,0:T(8,128)(2,1)}, bf16[128,2304]{1,0:T(8,128)(2,1)}, bf16[128,2304]{1,0:T(8,128)(2,1)}) custom-call(bf16[768,2048]{1,0:T(8,128)(2,1)S(1)} %convolution_convert_fusion.1.refs_0_, bf16[1280,2048]{1,0:T(8,128)(2,1)S(1)} %convolution_convert_fusion.refs_1_, ...), custom_call_target="tpu_custom_call" | custom-call | flops 3276800 | bytes 13107200 | tf_op jit(solution)/shard_map/assemble/pallas_call | solution.py:443
  178.5 3.8 %collective-permute-start.34 = (bf16[128,2304]{1,0:T(8,128)(2,1)}, bf16[128,2304]{1,0:T(8,128)(2,1)}, u32[]{:S(2)}, u32[]{:S(2)}) collective-permute-start(bf16[128,2304]{1,0:T(8,128)(2,1)} %get-tuple-element.163), channel_id=1, source_target_pairs={{8,0},{10,2},{12,4},{14,6},{16,8},{18,10},{20,12},{22,14},{24,16},... | collective-permute-start | bytes 1769480 | tf_op jit(solution)/shard_map/ppermute | solution.py:356
  182.4 4.2 %all-to-all-start.1 = ((bf16[16,128,128]{2,1,0:T(8,128)(2,1)}), bf16[16,128,128]{2,1,0:T(8,128)(2,1)}, u32[]{:S(2)}, u32[]{:S(2)}) async-start(bf16[16,128,128]{2,1,0:T(8,128)(2,1)} %bitcast.46), calls=%async_computation.1 | async-start | bytes 1048576 | tf_op jit(solution)/shard_map/all_to_all | solution.py:609
  186.6 10.3 %collective-permute-done.33.refs_4_ = bf16[128,2304]{1,0:T(8,128)(2,1)} collective-permute-done((bf16[128,2304]{1,0:T(8,128)(2,1)}, bf16[128,2304]{1,0:T(8,128)(2,1)}, u32[]{:S(2)}, u32[]{:S(2)}) %collective-permute-start.33) | collective-permute-done | bytes 589856 | tf_op jit(solution)/shard_map/ppermute | solution.py:351
  196.9 9.7 %collective-permute-done.34.refs_5_ = bf16[128,2304]{1,0:T(8,128)(2,1)} collective-permute-done((bf16[128,2304]{1,0:T(8,128)(2,1)}, bf16[128,2304]{1,0:T(8,128)(2,1)}, u32[]{:S(2)}, u32[]{:S(2)}) %collective-permute-start.34) | collective-permute-done | bytes 589856 | tf_op jit(solution)/shard_map/ppermute | solution.py:356
  206.7 2.5 %copy-done.1 = bf16[1280,2048]{1,0:T(8,128)(2,1)S(1)} copy-done((bf16[1280,2048]{1,0:T(8,128)(2,1)S(1)}, bf16[1280,2048]{1,0:T(8,128)(2,1)}, u32[]{:S(2)}) %copy-start.1) | copy-done | bytes 5242904
  209.2 3.6 %assemble.14 = (bf16[128,2048]{1,0:T(8,128)(2,1)}, bf16[128,2048]{1,0:T(8,128)(2,1)}, bf16[128,1536]{1,0:T(8,128)(2,1)}, bf16[128,1536]{1,0:T(8,128)(2,1)}) custom-call(bf16[768,2048]{1,0:T(8,128)(2,1)S(1)} %convolution_convert_fusion.1.refs_0_, bf16[1280,2048]{1,0:T(8,128)(2,1)S(1)} %copy-done.1, bf16[128,4096]{1,0:T(8,128)(2,1)} %collective-permute-done.31.refs_2_, ...), custom_call_target="tpu_custom_call" | custom-call | flops 1835008 | bytes 7340032 | tf_op jit(solution)/shard_map/assemble/pallas_call | solution.py:443
  216.8 2.7 %collective-permute-start.38 = (bf16[128,1536]{1,0:T(8,128)(2,1)}, bf16[128,1536]{1,0:T(8,128)(2,1)}, u32[]{:S(2)}, u32[]{:S(2)}) collective-permute-start(bf16[128,1536]{1,0:T(8,128)(2,1)} %get-tuple-element.171), channel_id=1, source_target_pairs={{8,0},{10,2},{12,4},{14,6},{16,8},{18,10},{20,12},{22,14},{24,16},... | collective-permute-start | bytes 1179656 | tf_op jit(solution)/shard_map/ppermute | solution.py:356
  219.5 2.0 copy.9
  221.5 6.3 %collective-permute-done.37.refs_8_ = bf16[128,1536]{1,0:T(8,128)(2,1)S(1)} collective-permute-done((bf16[128,1536]{1,0:T(8,128)(2,1)}, bf16[128,1536]{1,0:T(8,128)(2,1)S(1)}, u32[]{:S(2)}, u32[]{:S(2)}) %collective-permute-start.37) | collective-permute-done | bytes 393248 | tf_op jit(solution)/shard_map/ppermute | solution.py:351
  227.8 2.9 %collective-permute-done.38.refs_9_ = bf16[128,1536]{1,0:T(8,128)(2,1)} collective-permute-done((bf16[128,1536]{1,0:T(8,128)(2,1)}, bf16[128,1536]{1,0:T(8,128)(2,1)}, u32[]{:S(2)}, u32[]{:S(2)}) %collective-permute-start.38) | collective-permute-done | bytes 393248 | tf_op jit(solution)/shard_map/ppermute | solution.py:356
  230.8 2.5 %copy-done.2 = bf16[1280,2048]{1,0:T(8,128)(2,1)S(1)} copy-done((bf16[1280,2048]{1,0:T(8,128)(2,1)S(1)}, bf16[1280,2048]{1,0:T(8,128)(2,1)}, u32[]{:S(2)}) %copy-start.2) | copy-done | bytes 5242904
  233.3 2.6 %assemble.15 = bf16[128,2048]{1,0:T(8,128)(2,1)} custom-call(bf16[768,2048]{1,0:T(8,128)(2,1)S(1)} %convolution_convert_fusion.1.refs_0_, bf16[1280,2048]{1,0:T(8,128)(2,1)S(1)} %copy-done.2, bf16[128,4096]{1,0:T(8,128)(2,1)} %collective-permute-done.31.refs_2_, bf16[128,4096]{1,0:T(8,128)(2,1)} %collective-permute-done.32.refs_3_, ...), custom_call_target="tpu_custom_call" | custom-call | flops 524288 | bytes 2097152 | tf_op jit(solution)/shard_map/assemble/pallas_call | solution.py:443
  (106 shorter events, 37.3 us)
Async XLA Ops:
  4.0 27.2 %collective-permute-start.4 = (bf16[384,2048]{1,0:T(8,128)(2,1)}, bf16[384,2048]{1,0:T(8,128)(2,1)}, u32[]{:S(2)}, u32[]{:S(2)}) collective-permute-start(bf16[384,2048]{1,0:T(8,128)(2,1)} %get-tuple-element.94), channel_id=1, source_target_pairs={{0,1},{1,0},{2,3},{3,2},{4,5},{5,4},{6,7},{7,6},{8,9},{9,8},{10,11... | collective-permute-start | bytes 4718600 | tf_op jit(solution)/shard_map/ppermute | solution.py:338
  5.3 25.8 %collective-permute-start.1 = (bf16[128,2048]{1,0:T(8,128)(2,1)S(1)}, bf16[128,2048]{1,0:T(8,128)(2,1)S(1)}, u32[]{:S(2)}, u32[]{:S(2)}) collective-permute-start(bf16[128,2048]{1,0:T(8,128)(2,1)S(1)} %get-tuple-element.90.refs_0_), channel_id=1, source_target_pairs={{0,4},{2,6},{4,0},{6,2},{8,12},{10,14},{12,8},{14,10},{16,20},{18,... | collective-permute-start | bytes 1572872 | tf_op jit(solution)/shard_map/ppermute | solution.py:346
  7.9 23.2 %collective-permute-start = (bf16[128,2048]{1,0:T(8,128)(2,1)S(1)}, bf16[128,2048]{1,0:T(8,128)(2,1)S(1)}, u32[]{:S(2)}, u32[]{:S(2)}) collective-permute-start(bf16[128,2048]{1,0:T(8,128)(2,1)S(1)} %get-tuple-element.90.refs_0_), channel_id=1, source_target_pairs={{0,2},{2,0},{4,6},{6,4},{8,10},{10,8},{12,14},{14,12},{16,18},{18,... | collective-permute-start | bytes 1572872 | tf_op jit(solution)/shard_map/ppermute | solution.py:342
  9.4 13.4 %collective-permute-start.3 = (bf16[96,2048]{1,0:T(8,128)(2,1)}, bf16[96,2048]{1,0:T(8,128)(2,1)S(1)}, u32[]{:S(2)}, u32[]{:S(2)}) collective-permute-start(bf16[96,2048]{1,0:T(8,128)(2,1)} %get-tuple-element.91), channel_id=1, source_target_pairs={{8,0},{10,2},{12,4},{14,6},{16,8},{18,10},{20,12},{22,14},{24,16},... | collective-permute-start | bytes 1179656 | tf_op jit(solution)/shard_map/ppermute | solution.py:356
  13.0 18.1 %collective-permute-start.2 = (bf16[96,2048]{1,0:T(8,128)(2,1)}, bf16[96,2048]{1,0:T(8,128)(2,1)}, u32[]{:S(2)}, u32[]{:S(2)}) collective-permute-start(bf16[96,2048]{1,0:T(8,128)(2,1)} %get-tuple-element.91), channel_id=1, source_target_pairs={{0,8},{2,10},{4,12},{6,14},{8,16},{10,18},{12,20},{14,22},{16,24},... | collective-permute-start | bytes 1179656 | tf_op jit(solution)/shard_map/ppermute | solution.py:351
  22.9 13.0 %copy-start.6 = (bf16[96,2048]{1,0:T(8,128)(2,1)}, bf16[96,2048]{1,0:T(8,128)(2,1)S(1)}, u32[]{:S(2)}) copy-start(bf16[96,2048]{1,0:T(8,128)(2,1)S(1)} %collective-permute-done.3.refs_4_) | copy-start | bytes 1179652
  33.7 30.8 %collective-permute-start.5 = (bf16[256,2048]{1,0:T(8,128)(2,1)S(1)}, bf16[256,2048]{1,0:T(8,128)(2,1)}, u32[]{:S(2)}, u32[]{:S(2)}) collective-permute-start(bf16[256,2048]{1,0:T(8,128)(2,1)S(1)} %get-tuple-element.99), channel_id=1, source_target_pairs={{0,2},{2,0},{4,6},{6,4},{8,10},{10,8},{12,14},{14,12},{16,18},{18,... | collective-permute-start | bytes 3145736 | tf_op jit(solution)/shard_map/ppermute | solution.py:342
  34.3 30.2 %collective-permute-start.6 = (bf16[256,2048]{1,0:T(8,128)(2,1)S(1)}, bf16[256,2048]{1,0:T(8,128)(2,1)S(1)}, u32[]{:S(2)}, u32[]{:S(2)}) collective-permute-start(bf16[256,2048]{1,0:T(8,128)(2,1)S(1)} %get-tuple-element.100), channel_id=1, source_target_pairs={{0,4},{2,6},{4,0},{6,2},{8,12},{10,14},{12,8},{14,10},{16,20},{18,... | collective-permute-start | bytes 3145736 | tf_op jit(solution)/shard_map/ppermute | solution.py:346
  35.9 18.1 %collective-permute-start.7 = (bf16[144,2048]{1,0:T(8,128)(2,1)S(1)}, bf16[144,2048]{1,0:T(8,128)(2,1)S(1)}, u32[]{:S(2)}, u32[]{:S(2)}) collective-permute-start(bf16[144,2048]{1,0:T(8,128)(2,1)S(1)} %get-tuple-element.101), channel_id=1, source_target_pairs={{0,8},{2,10},{4,12},{6,14},{8,16},{10,18},{12,20},{14,22},{16,24},... | collective-permute-start | bytes 1769480 | tf_op jit(solution)/shard_map/ppermute | solution.py:351
  37.6 26.1 %collective-permute-start.8 = (bf16[144,2048]{1,0:T(8,128)(2,1)S(1)}, bf16[144,2048]{1,0:T(8,128)(2,1)S(1)}, u32[]{:S(2)}, u32[]{:S(2)}) collective-permute-start(bf16[144,2048]{1,0:T(8,128)(2,1)S(1)} %get-tuple-element.102), channel_id=1, source_target_pairs={{8,0},{10,2},{12,4},{14,6},{16,8},{18,10},{20,12},{22,14},{24,16},... | collective-permute-start | bytes 1769480 | tf_op jit(solution)/shard_map/ppermute | solution.py:356
  44.4 71.9 %collective-permute-start.17 = (bf16[576,384]{1,0:T(8,128)(2,1)}, bf16[576,384]{1,0:T(8,128)(2,1)}, u32[]{:S(2)}, u32[]{:S(2)}) collective-permute-start(bf16[576,384]{1,0:T(8,128)(2,1)} %convolution_convert_fusion.3), channel_id=1, source_target_pairs={{0,1},{1,0},{2,3},{3,2},{4,5},{5,4},{6,7},{7,6},{8,9},{9,8},{10,11... | collective-permute-start | bytes 1327112 | tf_op jit(solution)/shard_map/ppermute | solution.py:338
  66.6 50.5 %all-to-all-start = ((bf16[128,16,128]{2,0,1:T(8,128)(2,1)}), bf16[128,16,128]{2,0,1:T(8,128)(2,1)}, u32[]{:S(2)}, u32[]{:S(2)}) async-start(bf16[128,16,128]{2,0,1:T(8,128)(2,1)} %copy.8), calls=%async_computation | async-start | bytes 1048576 | tf_op jit(solution)/shard_map/all_to_all | solution.py:693
  76.3 16.7 %collective-permute-start.11 = (bf16[80,2048]{1,0:T(8,128)(2,1)S(1)}, bf16[80,2048]{1,0:T(8,128)(2,1)S(1)}, u32[]{:S(2)}, u32[]{:S(2)}) collective-permute-start(bf16[80,2048]{1,0:T(8,128)(2,1)S(1)} %get-tuple-element.115), channel_id=1, source_target_pairs={{0,8},{2,10},{4,12},{6,14},{8,16},{10,18},{12,20},{14,22},{16,24},... | collective-permute-start | bytes 983048 | tf_op jit(solution)/shard_map/ppermute | solution.py:351
  78.2 17.1 %collective-permute-start.12 = (bf16[80,2048]{1,0:T(8,128)(2,1)S(1)}, bf16[80,2048]{1,0:T(8,128)(2,1)S(1)}, u32[]{:S(2)}, u32[]{:S(2)}) collective-permute-start(bf16[80,2048]{1,0:T(8,128)(2,1)S(1)} %get-tuple-element.116), channel_id=1, source_target_pairs={{8,0},{10,2},{12,4},{14,6},{16,8},{18,10},{20,12},{22,14},{24,16},... | collective-permute-start | bytes 983048 | tf_op jit(solution)/shard_map/ppermute | solution.py:356
  80.2 19.1 %collective-permute-start.9 = (bf16[192,2048]{1,0:T(8,128)(2,1)S(1)}, bf16[192,2048]{1,0:T(8,128)(2,1)S(1)}, u32[]{:S(2)}, u32[]{:S(2)}) collective-permute-start(bf16[192,2048]{1,0:T(8,128)(2,1)S(1)} %get-tuple-element.113), channel_id=1, source_target_pairs={{0,2},{2,0},{4,6},{6,4},{8,10},{10,8},{12,14},{14,12},{16,18},{18,... | collective-permute-start | bytes 2359304 | tf_op jit(solution)/shard_map/ppermute | solution.py:342
  82.0 17.6 %collective-permute-start.10 = (bf16[192,2048]{1,0:T(8,128)(2,1)S(1)}, bf16[192,2048]{1,0:T(8,128)(2,1)S(1)}, u32[]{:S(2)}, u32[]{:S(2)}) collective-permute-start(bf16[192,2048]{1,0:T(8,128)(2,1)S(1)} %get-tuple-element.114), channel_id=1, source_target_pairs={{0,4},{2,6},{4,0},{6,2},{8,12},{10,14},{12,8},{14,10},{16,20},{18,... | collective-permute-start | bytes 2359304 | tf_op jit(solution)/shard_map/ppermute | solution.py:346
  100.4 11.9 %collective-permute-start.15 = (bf16[16,2048]{1,0:T(8,128)(2,1)S(1)}, bf16[16,2048]{1,0:T(8,128)(2,1)S(1)}, u32[]{:S(2)}, u32[]{:S(2)}) collective-permute-start(bf16[16,2048]{1,0:T(8,128)(2,1)S(1)} %get-tuple-element.123), channel_id=1, source_target_pairs={{0,8},{2,10},{4,12},{6,14},{8,16},{10,18},{12,20},{14,22},{16,24},... | collective-permute-start | bytes 196616 | tf_op jit(solution)/shard_map/ppermute | solution.py:351
  101.2 11.1 %collective-permute-start.16 = (bf16[16,2048]{1,0:T(8,128)(2,1)S(1)}, bf16[16,2048]{1,0:T(8,128)(2,1)S(1)}, u32[]{:S(2)}, u32[]{:S(2)}) collective-permute-start(bf16[16,2048]{1,0:T(8,128)(2,1)S(1)} %get-tuple-element.124), channel_id=1, source_target_pairs={{8,0},{10,2},{12,4},{14,6},{16,8},{18,10},{20,12},{22,14},{24,16},... | collective-permute-start | bytes 196616 | tf_op jit(solution)/shard_map/ppermute | solution.py:356
  104.3 8.5 %collective-permute-start.13 = (bf16[48,2048]{1,0:T(8,128)(2,1)S(1)}, bf16[48,2048]{1,0:T(8,128)(2,1)S(1)}, u32[]{:S(2)}, u32[]{:S(2)}) collective-permute-start(bf16[48,2048]{1,0:T(8,128)(2,1)S(1)} %get-tuple-element.121), channel_id=1, source_target_pairs={{0,2},{2,0},{4,6},{6,4},{8,10},{10,8},{12,14},{14,12},{16,18},{18,... | collective-permute-start | bytes 589832 | tf_op jit(solution)/shard_map/ppermute | solution.py:342
  105.2 7.6 %collective-permute-start.14 = (bf16[48,2048]{1,0:T(8,128)(2,1)S(1)}, bf16[48,2048]{1,0:T(8,128)(2,1)S(1)}, u32[]{:S(2)}, u32[]{:S(2)}) collective-permute-start(bf16[48,2048]{1,0:T(8,128)(2,1)S(1)} %get-tuple-element.122), channel_id=1, source_target_pairs={{0,4},{2,6},{4,0},{6,2},{8,12},{10,14},{12,8},{14,10},{16,20},{18,... | collective-permute-start | bytes 589832 | tf_op jit(solution)/shard_map/ppermute | solution.py:346
  112.3 3.9 %collective-permute-start.18 = (bf16[800,384]{1,0:T(8,128)(2,1)S(1)}, bf16[800,384]{1,0:T(8,128)(2,1)S(1)}, u32[]{:S(2)}, u32[]{:S(2)}) collective-permute-start(bf16[800,384]{1,0:T(8,128)(2,1)S(1)} %convolution_convert_fusion.2), channel_id=1, source_target_pairs={{0,1},{1,0},{2,3},{3,2},{4,5},{5,4},{6,7},{7,6},{8,9},{9,8},{10,11... | collective-permute-start | bytes 1843208 | tf_op jit(solution)/shard_map/ppermute | solution.py:338
  112.3 4.8 %collective-permute-start.19 = (bf16[544,384]{1,0:T(8,128)(2,1)}, bf16[544,384]{1,0:T(8,128)(2,1)S(1)}, u32[]{:S(2)}, u32[]{:S(2)}) collective-permute-start(bf16[544,384]{1,0:T(8,128)(2,1)} %convolution_convert_fusion.4), channel_id=1, source_target_pairs={{0,1},{1,0},{2,3},{3,2},{4,5},{5,4},{6,7},{7,6},{8,9},{9,8},{10,11... | collective-permute-start | bytes 1253384 | tf_op jit(solution)/shard_map/ppermute | solution.py:338
  112.9 4.3 %copy-start.13 = (f32[1,128,16]{1,2,0:T(8,128)S(1)}, f32[1,128,16]{1,2,0:T(8,128)}, u32[]{:S(2)}) copy-start(f32[1,128,16]{1,2,0:T(8,128)} %param.7) | copy-start | bytes 24580
  112.9 4.2 %copy-start.14 = (f32[1,128,16]{1,2,0:T(8,128)S(1)}, f32[1,128,16]{1,2,0:T(8,128)}, u32[]{:S(2)}) copy-start(f32[1,128,16]{1,2,0:T(8,128)} %param.8) | copy-start | bytes 24580
  115.6 1.5 collective-permute-start.20
  135.5 5.2 %copy-start.12 = (bf16[2048,128]{1,0:T(8,128)(2,1)}, bf16[2048,128]{1,0:T(8,128)(2,1)S(1)}, u32[]{:S(2)}) copy-start(bf16[2048,128]{1,0:T(8,128)(2,1)S(1)} %get-tuple-element.154) | copy-start | bytes 1572868
  135.5 2.3 collective-permute-start.21
  136.2 20.5 %collective-permute-start.26 = (bf16[1280,384]{1,0:T(8,128)(2,1)S(1)}, bf16[1280,384]{1,0:T(8,128)(2,1)S(1)}, u32[]{:S(2)}, u32[]{:S(2)}) collective-permute-start(bf16[1280,384]{1,0:T(8,128)(2,1)S(1)} %get-tuple-element.140), channel_id=1, source_target_pairs={{0,1},{1,0},{2,3},{3,2},{4,5},{5,4},{6,7},{7,6},{8,9},{9,8},{10,11... | collective-permute-start | bytes 2949128 | tf_op jit(solution)/shard_map/ppermute | solution.py:338
  140.9 8.4 %collective-permute-start.22 = (bf16[128,768]{1,0:T(8,128)(2,1)S(1)}, bf16[128,768]{1,0:T(8,128)(2,1)S(1)}, u32[]{:S(2)}, u32[]{:S(2)}) collective-permute-start(bf16[128,768]{1,0:T(8,128)(2,1)S(1)} %get-tuple-element.132), channel_id=1, source_target_pairs={{0,2},{2,0},{4,6},{6,4},{8,10},{10,8},{12,14},{14,12},{16,18},{18,... | collective-permute-start | bytes 589832 | tf_op jit(solution)/shard_map/ppermute | solution.py:342
  142.1 7.2 %collective-permute-start.23 = (bf16[128,768]{1,0:T(8,128)(2,1)S(1)}, bf16[128,768]{1,0:T(8,128)(2,1)S(1)}, u32[]{:S(2)}, u32[]{:S(2)}) collective-permute-start(bf16[128,768]{1,0:T(8,128)(2,1)S(1)} %get-tuple-element.133), channel_id=1, source_target_pairs={{0,4},{2,6},{4,0},{6,2},{8,12},{10,14},{12,8},{14,10},{16,20},{18,... | collective-permute-start | bytes 589832 | tf_op jit(solution)/shard_map/ppermute | solution.py:346
  142.9 6.4 %collective-permute-start.24 = (bf16[128,256]{1,0:T(8,128)(2,1)S(1)}, bf16[128,256]{1,0:T(8,128)(2,1)S(1)}, u32[]{:S(2)}, u32[]{:S(2)}) collective-permute-start(bf16[128,256]{1,0:T(8,128)(2,1)S(1)} %get-tuple-element.134), channel_id=1, source_target_pairs={{0,8},{2,10},{4,12},{6,14},{8,16},{10,18},{12,20},{14,22},{16,24},... | collective-permute-start | bytes 196616 | tf_op jit(solution)/shard_map/ppermute | solution.py:351
  142.9 6.4 %collective-permute-start.25 = (bf16[128,256]{1,0:T(8,128)(2,1)S(1)}, bf16[128,256]{1,0:T(8,128)(2,1)S(1)}, u32[]{:S(2)}, u32[]{:S(2)}) collective-permute-start(bf16[128,256]{1,0:T(8,128)(2,1)S(1)} %get-tuple-element.135), channel_id=1, source_target_pairs={{8,0},{10,2},{12,4},{14,6},{16,8},{18,10},{20,12},{22,14},{24,16},... | collective-permute-start | bytes 196616 | tf_op jit(solution)/shard_map/ppermute | solution.py:356
  150.6 12.5 %collective-permute-start.29 = (bf16[128,1280]{1,0:T(8,128)(2,1)S(1)}, bf16[128,1280]{1,0:T(8,128)(2,1)S(1)}, u32[]{:S(2)}, u32[]{:S(2)}) collective-permute-start(bf16[128,1280]{1,0:T(8,128)(2,1)S(1)} %get-tuple-element.148), channel_id=1, source_target_pairs={{0,8},{2,10},{4,12},{6,14},{8,16},{10,18},{12,20},{14,22},{16,24},... | collective-permute-start | bytes 983048 | tf_op jit(solution)/shard_map/ppermute | solution.py:351
  150.7 15.8 %collective-permute-start.30 = (bf16[128,1280]{1,0:T(8,128)(2,1)S(1)}, bf16[128,1280]{1,0:T(8,128)(2,1)S(1)}, u32[]{:S(2)}, u32[]{:S(2)}) collective-permute-start(bf16[128,1280]{1,0:T(8,128)(2,1)S(1)} %get-tuple-element.149), channel_id=1, source_target_pairs={{8,0},{10,2},{12,4},{14,6},{16,8},{18,10},{20,12},{22,14},{24,16},... | collective-permute-start | bytes 983048 | tf_op jit(solution)/shard_map/ppermute | solution.py:356
  154.5 18.0 %collective-permute-start.27 = (bf16[128,3072]{1,0:T(8,128)(2,1)S(1)}, bf16[128,3072]{1,0:T(8,128)(2,1)S(1)}, u32[]{:S(2)}, u32[]{:S(2)}) collective-permute-start(bf16[128,3072]{1,0:T(8,128)(2,1)S(1)} %get-tuple-element.146), channel_id=1, source_target_pairs={{0,2},{2,0},{4,6},{6,4},{8,10},{10,8},{12,14},{14,12},{16,18},{18,... | collective-permute-start | bytes 2359304 | tf_op jit(solution)/shard_map/ppermute | solution.py:342
  155.4 17.7 %collective-permute-start.28 = (bf16[128,3072]{1,0:T(8,128)(2,1)S(1)}, bf16[128,3072]{1,0:T(8,128)(2,1)S(1)}, u32[]{:S(2)}, u32[]{:S(2)}) collective-permute-start(bf16[128,3072]{1,0:T(8,128)(2,1)S(1)} %get-tuple-element.147), channel_id=1, source_target_pairs={{0,4},{2,6},{4,0},{6,2},{8,12},{10,14},{12,8},{14,10},{16,20},{18,... | collective-permute-start | bytes 2359304 | tf_op jit(solution)/shard_map/ppermute | solution.py:346
  161.1 15.4 %copy-start = (bf16[1280,2048]{1,0:T(8,128)(2,1)}, bf16[1280,2048]{1,0:T(8,128)(2,1)S(1)}, u32[]{:S(2)}) copy-start(bf16[1280,2048]{1,0:T(8,128)(2,1)S(1)} %convolution_convert_fusion.refs_1_) | copy-start | bytes 15728644
  176.5 30.1 %collective-permute-start.31 = (bf16[128,4096]{1,0:T(8,128)(2,1)}, bf16[128,4096]{1,0:T(8,128)(2,1)}, u32[]{:S(2)}, u32[]{:S(2)}) collective-permute-start(bf16[128,4096]{1,0:T(8,128)(2,1)} %get-tuple-element.160), channel_id=1, source_target_pairs={{0,2},{2,0},{4,6},{6,4},{8,10},{10,8},{12,14},{14,12},{16,18},{18,... | collective-permute-start | bytes 3145736 | tf_op jit(solution)/shard_map/ppermute | solution.py:342
  177.7 28.9 %collective-permute-start.32 = (bf16[128,4096]{1,0:T(8,128)(2,1)}, bf16[128,4096]{1,0:T(8,128)(2,1)}, u32[]{:S(2)}, u32[]{:S(2)}) collective-permute-start(bf16[128,4096]{1,0:T(8,128)(2,1)} %get-tuple-element.161), channel_id=1, source_target_pairs={{0,4},{2,6},{4,0},{6,2},{8,12},{10,14},{12,8},{14,10},{16,20},{18,... | collective-permute-start | bytes 3145736 | tf_op jit(solution)/shard_map/ppermute | solution.py:346
  178.5 18.4 %collective-permute-start.33 = (bf16[128,2304]{1,0:T(8,128)(2,1)}, bf16[128,2304]{1,0:T(8,128)(2,1)}, u32[]{:S(2)}, u32[]{:S(2)}) collective-permute-start(bf16[128,2304]{1,0:T(8,128)(2,1)} %get-tuple-element.162), channel_id=1, source_target_pairs={{0,8},{2,10},{4,12},{6,14},{8,16},{10,18},{12,20},{14,22},{16,24},... | collective-permute-start | bytes 1769480 | tf_op jit(solution)/shard_map/ppermute | solution.py:351
  178.5 28.1 %collective-permute-start.34 = (bf16[128,2304]{1,0:T(8,128)(2,1)}, bf16[128,2304]{1,0:T(8,128)(2,1)}, u32[]{:S(2)}, u32[]{:S(2)}) collective-permute-start(bf16[128,2304]{1,0:T(8,128)(2,1)} %get-tuple-element.163), channel_id=1, source_target_pairs={{8,0},{10,2},{12,4},{14,6},{16,8},{18,10},{20,12},{22,14},{24,16},... | collective-permute-start | bytes 1769480 | tf_op jit(solution)/shard_map/ppermute | solution.py:356
  182.4 37.1 %all-to-all-start.1 = ((bf16[16,128,128]{2,1,0:T(8,128)(2,1)}), bf16[16,128,128]{2,1,0:T(8,128)(2,1)}, u32[]{:S(2)}, u32[]{:S(2)}) async-start(bf16[16,128,128]{2,1,0:T(8,128)(2,1)} %bitcast.46), calls=%async_computation.1 | async-start | bytes 1048576 | tf_op jit(solution)/shard_map/all_to_all | solution.py:609
  206.7 2.5 %copy-start.1 = (bf16[1280,2048]{1,0:T(8,128)(2,1)S(1)}, bf16[1280,2048]{1,0:T(8,128)(2,1)}, u32[]{:S(2)}) copy-start(bf16[1280,2048]{1,0:T(8,128)(2,1)} %copy-done) | copy-start | bytes 15728644
  212.8 18.0 %collective-permute-start.35 = (bf16[128,2048]{1,0:T(8,128)(2,1)}, bf16[128,2048]{1,0:T(8,128)(2,1)}, u32[]{:S(2)}, u32[]{:S(2)}) collective-permute-start(bf16[128,2048]{1,0:T(8,128)(2,1)} %get-tuple-element.168), channel_id=1, source_target_pairs={{0,2},{2,0},{4,6},{6,4},{8,10},{10,8},{12,14},{14,12},{16,18},{18,... | collective-permute-start | bytes 1572872 | tf_op jit(solution)/shard_map/ppermute | solution.py:342
  213.8 16.9 %collective-permute-start.36 = (bf16[128,2048]{1,0:T(8,128)(2,1)}, bf16[128,2048]{1,0:T(8,128)(2,1)}, u32[]{:S(2)}, u32[]{:S(2)}) collective-permute-start(bf16[128,2048]{1,0:T(8,128)(2,1)} %get-tuple-element.169), channel_id=1, source_target_pairs={{0,4},{2,6},{4,0},{6,2},{8,12},{10,14},{12,8},{14,10},{16,20},{18,... | collective-permute-start | bytes 1572872 | tf_op jit(solution)/shard_map/ppermute | solution.py:346
  215.7 12.2 %collective-permute-start.37 = (bf16[128,1536]{1,0:T(8,128)(2,1)}, bf16[128,1536]{1,0:T(8,128)(2,1)S(1)}, u32[]{:S(2)}, u32[]{:S(2)}) collective-permute-start(bf16[128,1536]{1,0:T(8,128)(2,1)} %get-tuple-element.170), channel_id=1, source_target_pairs={{0,8},{2,10},{4,12},{6,14},{8,16},{10,18},{12,20},{14,22},{16,24},... | collective-permute-start | bytes 1179656 | tf_op jit(solution)/shard_map/ppermute | solution.py:351
  216.8 14.0 %collective-permute-start.38 = (bf16[128,1536]{1,0:T(8,128)(2,1)}, bf16[128,1536]{1,0:T(8,128)(2,1)}, u32[]{:S(2)}, u32[]{:S(2)}) collective-permute-start(bf16[128,1536]{1,0:T(8,128)(2,1)} %get-tuple-element.171), channel_id=1, source_target_pairs={{8,0},{10,2},{12,4},{14,6},{16,8},{18,10},{20,12},{22,14},{24,16},... | collective-permute-start | bytes 1179656 | tf_op jit(solution)/shard_map/ppermute | solution.py:356
  230.8 2.5 %copy-start.2 = (bf16[1280,2048]{1,0:T(8,128)(2,1)S(1)}, bf16[1280,2048]{1,0:T(8,128)(2,1)}, u32[]{:S(2)}) copy-start(bf16[1280,2048]{1,0:T(8,128)(2,1)} %copy-done) | copy-start | bytes 15728644
  (8 other events, 10.3 us)
